TPU v7x, 128 devices: a whole 4x4x4 slice. The times are simulated.
128 devices in a mesh: adapter: 8 (over x, core), row: 16 (over z, y).
Axes of the slice: x: 4, y: 4, z: 4, core: 2. Of those that a mesh axis runs over, the one named last changes fastest.
Arguments:
- up_factors_wide: bfloat16 [4096, 24576], P('row', 'adapter'), may hold values from -0.75 to 0.75
- transposed_down_factors: bfloat16 [4096, 24576], P('row', 'adapter'), may hold values from -0.75 to 0.75
- ranks: int32 [1536], P('adapter'), may hold values from 1 to 16
- initial_left_basis: float32 [4096, 256], P('row'), may hold values from -0.09375 to 0.09375
- initial_right_basis: float32 [4096, 256], P('row'), may hold values from -0.09375 to 0.09375
Outputs:
- fitted_u: float32 [4096, 256], P('row')
- fitted_v: float32 [4096, 256], P('row')
- cores: float32 [1536, 256, 256], P('adapter', 'row')
All inputs are finite; a program needn't handle non-finite values.
Results may differ from a plain program's by a relative error of at most 0.012.
Values sent between devices are 32-bit elements; how exact they have to be, the bound alone decides.
No kernel may reach another device: no remote copies, remote signals or barrier semaphores. Data moves between devices by JAX's collectives and lax.ppermute only.
A program may use at most 128 MiB of HBM per device.

v0:
```python
import jax
import jax.numpy as jnp
from jax import lax
from jax.sharding import PartitionSpec as P

PADDED_RANK = 16
ITERS = 2


def column_scale(ranks):
    positions = jnp.arange(PADDED_RANK, dtype=jnp.int32)
    live = positions[None, :] < ranks[:, None]
    factor = 4.0 / jnp.sqrt(ranks.astype(jnp.float32))
    return jnp.where(live, factor[:, None], jnp.float32(0.0)).reshape(-1)


def project_locally(basis, factors, column_scaling):
    return (
        jnp.dot(basis.T, factors.astype(jnp.float32), precision=lax.Precision.HIGHEST)
        * column_scaling[None, :]
    )


def coupling_of(own_proj, other_proj, column_scaling):
    count = own_proj.shape[1] // PADDED_RANK
    own_rows = own_proj.reshape(own_proj.shape[0], count, PADDED_RANK)
    other_rows = other_proj.reshape(other_proj.shape[0], count, PADDED_RANK)
    gram_small = jnp.einsum("kar,kas->ars", other_rows, other_rows, precision=lax.Precision.HIGHEST)
    coupling = jnp.einsum("ars,kas->ark", gram_small, own_rows, precision=lax.Precision.HIGHEST)
    return coupling.reshape(count * PADDED_RANK, own_proj.shape[0]) * column_scaling[:, None]


def project_sum(basis, factors, column_scaling):
    return lax.psum(project_locally(basis, factors, column_scaling), "row")


def basis_refitting(factors, column_scaling, own_proj, other_proj):
    coupling = coupling_of(own_proj, other_proj, column_scaling)
    partial_update = jnp.dot(factors.astype(jnp.float32), coupling, precision=lax.Precision.HIGHEST)
    update = lax.psum(partial_update, "adapter")
    gram_part = jnp.dot(update.T, update, precision=lax.Precision.HIGHEST)
    gram_total = lax.psum(gram_part, "row")
    lower = jnp.linalg.cholesky(gram_total)
    basis = lax.linalg.triangular_solve(
        lower, update, left_side=False, lower=True, transpose_a=True
    )
    new_proj = project_sum(basis, factors, column_scaling)
    return (basis, new_proj)


def shards(
    up_factors_wide, transposed_down_factors, ranks, initial_left_basis, initial_right_basis
):
    column_scaling = column_scale(ranks)
    partial_left_coupling = project_locally(initial_left_basis, up_factors_wide, column_scaling)
    partial_right_coupling = project_locally(
        initial_right_basis, transposed_down_factors, column_scaling
    )
    left_projected, right_projected = lax.psum(
        (partial_left_coupling, partial_right_coupling), "row"
    )
    for sweep_index in range(ITERS):
        initial_left_basis, left_projected = basis_refitting(
            up_factors_wide, column_scaling, left_projected, right_projected
        )
        initial_right_basis, right_projected = basis_refitting(
            transposed_down_factors, column_scaling, right_projected, left_projected
        )
    width_k = left_projected.shape[0]
    block_rows = width_k // lax.axis_size("row")
    offset = lax.axis_index("row") * block_rows
    p_block = lax.dynamic_slice_in_dim(left_projected, offset, block_rows, 0)
    count = left_projected.shape[1] // PADDED_RANK
    p_rows = p_block.reshape(block_rows, count, PADDED_RANK)
    q_rows = right_projected.reshape(width_k, count, PADDED_RANK)
    cores = jnp.einsum("kar,jar->akj", p_rows, q_rows, precision=lax.Precision.HIGHEST)
    return (initial_left_basis, initial_right_basis, cores)


def solution(mesh):
    return jax.shard_map(
        shards,
        mesh=mesh,
        in_specs=(
            P("row", "adapter"),
            P("row", "adapter"),
            P("adapter"),
            P("row", None),
            P("row", None),
        ),
        out_specs=(P("row", None), P("row", None), P("adapter", "row", None)),
        check_vma=False,
    )
```

profile of v0, /device:TPU:0, one launch (start us, length us, event | category | flops | bytes accessed | tf_op | source)
XLA Modules:
  0.0 1520.3 jit_solution(16661837987380532375)
XLA Ops:
  24.1 125.0 %all-reduce.40.cloned.1.call-done = (f32[256,192,16]{0,2,1:T(8,128)}, f32[256,192,16]{0,2,1:T(8,128)}) async-done(((f32[256,192,16]{0,2,1:T(8,128)}, f32[256,192,16]{0,2,1:T(8,128)}), (f32[256,192,16]{0,2,1:T(8,128)}, f32[256,192,16]{0,2,1:T(8,128)})) %all-reduce.40.cloned.1.call-update) | async-done | bytes 6291472 | tf_op jit(solution)/shard_map/psum | solution.py:59
  162.1 59.4 %all-reduce.16.cloned.1.call-done = f32[256,256]{0,1:T(8,128)} async-done(((f32[256,256]{0,1:T(8,128)}), f32[256,256]{0,1:T(8,128)}) %all-reduce.16.cloned.1.call-update) | async-done | bytes 262160 | tf_op jit(solution)/shard_map/psum | solution.py:40
  224.1 84.7 %all-reduce.18.cloned.1.call-done = f32[256,256]{0,1:T(8,128)} async-done(((f32[256,256]{0,1:T(8,128)}), f32[256,256]{0,1:T(8,128)}) %all-reduce.18.cloned.1.call-update) | async-done | bytes 262160 | tf_op jit(solution)/shard_map/psum | solution.py:42
  310.9 11.7 cholesky.214
  322.7 9.8 custom-call.17
  333.0 11.7 cholesky.231
  346.8 14.2 while.8
  361.1 19.7 %custom-call.18 = f32[2,128,128]{1,2,0:T(8,128)S(1)} custom-call(f32[2,128,128]{2,1,0:T(8,128)S(1)} %get-tuple-element.31), custom_call_target="InvertDiagBlocksLowerTriangular" | custom-call | tf_op jit(solution)/shard_map/triangular_solve/custom-call.0 | solution.py:44
  388.4 95.3 %all-reduce.20.cloned.1.call-done = f32[256,192,16]{0,2,1:T(8,128)} async-done(((f32[256,192,16]{0,2,1:T(8,128)}), f32[256,192,16]{0,2,1:T(8,128)}) %all-reduce.20.cloned.1.call-update) | async-done | bytes 3145744 | tf_op jit(solution)/shard_map/psum | solution.py:34
  497.4 58.7 %all-reduce.22.cloned.1.call-done = f32[256,256]{0,1:T(8,128)} async-done(((f32[256,256]{0,1:T(8,128)}), f32[256,256]{0,1:T(8,128)}) %all-reduce.22.cloned.1.call-update) | async-done | bytes 262160 | tf_op jit(solution)/shard_map/psum | solution.py:40
  558.8 84.5 %all-reduce.24.cloned.1.call-done = f32[256,256]{0,1:T(8,128)} async-done(((f32[256,256]{0,1:T(8,128)}), f32[256,256]{0,1:T(8,128)}) %all-reduce.24.cloned.1.call-update) | async-done | bytes 262160 | tf_op jit(solution)/shard_map/psum | solution.py:42
  646.8 11.7 cholesky.248
  659.3 9.8 custom-call.19
  671.9 11.7 cholesky.265
  696.2 20.5 %custom-call.20 = f32[2,128,128]{1,2,0:T(8,128)S(1)} custom-call(f32[2,128,128]{2,1,0:T(8,128)} %copy-done.19), custom_call_target="InvertDiagBlocksLowerTriangular" | custom-call | tf_op jit(solution)/shard_map/triangular_solve/custom-call.0 | solution.py:44
  725.2 95.4 %all-reduce.26.cloned.1.call-done = f32[256,192,16]{0,2,1:T(8,128)} async-done(((f32[256,192,16]{0,2,1:T(8,128)}), f32[256,192,16]{0,2,1:T(8,128)}) %all-reduce.26.cloned.1.call-update) | async-done | bytes 3145744 | tf_op jit(solution)/shard_map/psum | solution.py:34
  833.4 58.7 %all-reduce.28.cloned.1.call-done = f32[256,256]{0,1:T(8,128)} async-done(((f32[256,256]{0,1:T(8,128)}), f32[256,256]{0,1:T(8,128)}) %all-reduce.28.cloned.1.call-update) | async-done | bytes 262160 | tf_op jit(solution)/shard_map/psum | solution.py:40
  894.7 84.7 %all-reduce.30.cloned.1.call-done = f32[256,256]{0,1:T(8,128)} async-done(((f32[256,256]{0,1:T(8,128)}), f32[256,256]{0,1:T(8,128)}) %all-reduce.30.cloned.1.call-update) | async-done | bytes 262160 | tf_op jit(solution)/shard_map/psum | solution.py:42
  983.0 11.7 cholesky.282
  995.4 9.8 custom-call.21
  1008.0 11.7 cholesky.299
  1024.7 7.2 while.10
  1031.9 20.3 %custom-call.22 = f32[2,128,128]{1,2,0:T(8,128)} custom-call(f32[2,128,128]{2,1,0:T(8,128)S(1)} %get-tuple-element.33), custom_call_target="InvertDiagBlocksLowerTriangular" | custom-call | tf_op jit(solution)/shard_map/triangular_solve/custom-call.0 | solution.py:44
  1058.8 95.4 %all-reduce.32.cloned.1.call-done = f32[256,3072]{1,0:T(8,128)} async-done(((f32[256,3072]{1,0:T(8,128)}), f32[256,3072]{1,0:T(8,128)}) %all-reduce.32.cloned.1.call-update) | async-done | bytes 3145744 | tf_op jit(solution)/shard_map/psum | solution.py:34
  1170.5 58.7 %all-reduce.34.cloned.1.call-done = f32[256,256]{0,1:T(8,128)} async-done(((f32[256,256]{0,1:T(8,128)}), f32[256,256]{0,1:T(8,128)}) %all-reduce.34.cloned.1.call-update) | async-done | bytes 262160 | tf_op jit(solution)/shard_map/psum | solution.py:40
  1231.7 84.7 %all-reduce.36.cloned.1.call-done = f32[256,256]{0,1:T(8,128)} async-done(((f32[256,256]{0,1:T(8,128)}), f32[256,256]{0,1:T(8,128)}) %all-reduce.36.cloned.1.call-update) | async-done | bytes 262160 | tf_op jit(solution)/shard_map/psum | solution.py:42
  1320.6 13.2 cholesky.316
  1336.8 11.3 custom-call.23
  1351.5 13.2 cholesky.333
  1371.1 8.4 while.11
  1379.5 21.1 %custom-call.24 = f32[2,128,128]{1,2,0:T(8,128)} custom-call(f32[2,128,128]{2,1,0:T(8,128)} %get-tuple-element.34), custom_call_target="InvertDiagBlocksLowerTriangular" | custom-call | tf_op jit(solution)/shard_map/triangular_solve/custom-call.0 | solution.py:44
  1415.8 90.4 %all-reduce.38.cloned.1.call-done = f32[256,192,16]{0,2,1:T(8,128)} async-done(((f32[256,192,16]{0,2,1:T(8,128)}), f32[256,192,16]{0,2,1:T(8,128)}) %all-reduce.38.cloned.1.call-update) | async-done | bytes 3145744 | tf_op jit(solution)/shard_map/psum | solution.py:34
  (196 shorter events, 202.3 us)
Async XLA Ops:
  7.2 10.0 copy-start
  7.2 141.9 %all-reduce.40.cloned.1.call-start = ((), (), s32[]{:S(2)}) async-start(), calls=%async_computation.12 | async-start | bytes 12582912 | tf_op jit(solution)/shard_map/psum | solution.py:59
  13.5 3.6 copy-start.18
  23.8 197.7 %all-reduce.16.cloned.1.call-start = ((), (), s32[]{:S(2)}) async-start(), calls=%async_computation | async-start | bytes 524288 | tf_op jit(solution)/shard_map/psum | solution.py:40
  149.0 6.0 copy-start.5
  162.0 146.8 %all-reduce.18.cloned.1.call-start = ((), (), s32[]{:S(2)}) async-start(), calls=%async_computation.1 | async-start | bytes 524288 | tf_op jit(solution)/shard_map/psum | solution.py:42
  221.5 159.3 %copy-start.6 = (f32[256,256]{0,1:T(8,128)S(1)}, f32[256,256]{0,1:T(8,128)}, u32[]{:S(2)}) copy-start(f32[256,256]{0,1:T(8,128)} %all-reduce.16.cloned.1.call-done) | copy-start | bytes 786436
  223.7 260.0 %all-reduce.20.cloned.1.call-start = ((), (), s32[]{:S(2)}) async-start(), calls=%async_computation.2 | async-start | bytes 6291456 | tf_op jit(solution)/shard_map/psum | solution.py:34
  361.0 19.7 %copy-start.20 = (s32[2,2]{1,0:T(2,128)}, s32[2,2]{1,0:T(2,128)S(1)}, u32[]{:S(2)}) copy-start(s32[2,2]{1,0:T(2,128)S(1)} %get-tuple-element.347) | copy-start | bytes 52
  388.4 167.7 %all-reduce.22.cloned.1.call-start = ((), (), s32[]{:S(2)}) async-start(), calls=%async_computation.3 | async-start | bytes 524288 | tf_op jit(solution)/shard_map/psum | solution.py:40
  483.7 6.0 copy-start.2
  492.5 1.4 copy-start.1
  497.4 145.9 %all-reduce.24.cloned.1.call-start = ((), (), s32[]{:S(2)}) async-start(), calls=%async_computation.4 | async-start | bytes 524288 | tf_op jit(solution)/shard_map/psum | solution.py:42
  556.1 160.6 %copy-start.8 = (f32[256,256]{0,1:T(8,128)S(1)}, f32[256,256]{0,1:T(8,128)}, u32[]{:S(2)}) copy-start(f32[256,256]{0,1:T(8,128)} %all-reduce.22.cloned.1.call-done) | copy-start | bytes 786436
  558.3 262.2 %all-reduce.26.cloned.1.call-start = ((), (), s32[]{:S(2)}) async-start(), calls=%async_computation.5 | async-start | bytes 6291456 | tf_op jit(solution)/shard_map/psum | solution.py:34
  646.1 0.7 copy-start.15
  725.2 166.9 %all-reduce.28.cloned.1.call-start = ((), (), s32[]{:S(2)}) async-start(), calls=%async_computation.6 | async-start | bytes 524288 | tf_op jit(solution)/shard_map/psum | solution.py:40
  820.6 6.0 copy-start.3
  833.3 146.0 %all-reduce.30.cloned.1.call-start = ((), (), s32[]{:S(2)}) async-start(), calls=%async_computation.7 | async-start | bytes 524288 | tf_op jit(solution)/shard_map/psum | solution.py:42
  892.0 160.2 %copy-start.9 = (f32[256,256]{0,1:T(8,128)S(1)}, f32[256,256]{0,1:T(8,128)}, u32[]{:S(2)}) copy-start(f32[256,256]{0,1:T(8,128)} %all-reduce.28.cloned.1.call-done) | copy-start | bytes 786436
  894.3 259.9 %all-reduce.32.cloned.1.call-start = ((), (), s32[]{:S(2)}) async-start(), calls=%async_computation.8 | async-start | bytes 6291456 | tf_op jit(solution)/shard_map/psum | solution.py:34
  982.2 0.7 copy-start.16
  1055.7 3.1 copy-start.12
  1058.8 170.4 %all-reduce.34.cloned.1.call-start = ((), (), s32[]{:S(2)}) async-start(), calls=%async_computation.9 | async-start | bytes 524288 | tf_op jit(solution)/shard_map/psum | solution.py:40
  1157.7 6.0 copy-start.4
  1170.5 145.9 %all-reduce.36.cloned.1.call-start = ((), (), s32[]{:S(2)}) async-start(), calls=%async_computation.10 | async-start | bytes 524288 | tf_op jit(solution)/shard_map/psum | solution.py:42
  1229.2 171.4 %copy-start.7 = (f32[256,256]{0,1:T(8,128)S(1)}, f32[256,256]{0,1:T(8,128)}, u32[]{:S(2)}) copy-start(f32[256,256]{0,1:T(8,128)} %all-reduce.34.cloned.1.call-done) | copy-start | bytes 786436
  1231.4 274.8 %all-reduce.38.cloned.1.call-start = ((), (), s32[]{:S(2)}) async-start(), calls=%async_computation.11 | async-start | bytes 6291456 | tf_op jit(solution)/shard_map/psum | solution.py:34
  1401.8 2.4 copy-start.10
  1404.1 3.1 copy-start.14
  1410.8 0.9 copy-start.13
  1410.8 3.2 copy-start.11
  (2 other events, 1.4 us)
Sparse Core Ops, SparseCore 0:
  23.9 125.0 all-reduce.39
  162.1 59.2 all-reduce.15
  225.2 83.5 all-reduce.17
  388.5 95.1 all-reduce.19
  497.5 58.5 all-reduce.21
  559.7 83.5 all-reduce.23
  725.3 95.2 all-reduce.25
  833.5 58.5 all-reduce.27
  895.8 83.5 all-reduce.29
  1058.9 95.2 all-reduce.31
  1170.6 58.5 all-reduce.33
  1232.8 83.5 all-reduce.35
  1410.9 95.2 all-reduce.37
where the time goes:
time: 1530 us; the launch traced here: 1520 us
  waiting for transfers between devices  1080 us (71%)
  other arithmetic  241 us (16%)
  matrix products  104 us (7%)
  local copies, waits for them, and re-layouts  66.2 us (4%)
  between operations  20 us (1%)
    psum x4, waiting for transfers between devices, project_sum(): return lax.psum(project_locally(basis, factors, column_scaling), 'row')  376 us
    psum x4, waiting for transfers between devices, basis_refitting(): gram_total = lax.psum(gram_part, 'row')  339 us
    psum x4, waiting for transfers between devices, basis_refitting(): update = lax.psum(partial_update, 'adapter')  235 us
    another operation x27, other arithmetic, basis_refitting(): lower = jnp.linalg.cholesky(gram_total)  146 us
    psum x1, waiting for transfers between devices, shards(): lax.psum((partial_left_coupling, partial_right_coupling), 'row')  125 us
    another operation x11, other arithmetic, basis_refitting(): lax.linalg.triangular_solve(lower, update, left_side=False, lower=True, t...  87.6 us
  transfers between devices with their start and end apart: 13, of which 13 were waited for; matrix products, arithmetic and copies ran while one was open for 0% of the time, Pallas kernels for 0%

commit v1 on v0

v1 whole, which is shorter than its diff:
```python
import functools

import jax
import jax.numpy as jnp
from jax import lax
from jax.experimental import pallas as pl
from jax.experimental.pallas import tpu as pltpu
from jax.sharding import PartitionSpec as P

PADDED_RANK = 16
ITERS = 2
RING = 4
K = 256
PANEL = 32
HIGH = lax.Precision.HIGHEST
F32 = jnp.float32
BF16 = jnp.bfloat16
VMEM = pl.BlockSpec(memory_space=pltpu.VMEM)
SMEM = pl.BlockSpec(memory_space=pltpu.SMEM)
PARAMS = pltpu.CompilerParams(vmem_limit_bytes=32 * 1024 * 1024)


def call(kernel, outs, n_in, flops, nbytes, scratch=(), smem=0):
    return pl.pallas_call(
        kernel,
        out_shape=outs,
        in_specs=[SMEM] * smem + [VMEM] * (n_in - smem),
        out_specs=jax.tree.map(lambda _: VMEM, outs),
        scratch_shapes=list(scratch),
        compiler_params=PARAMS,
        cost_estimate=pl.CostEstimate(flops=flops, bytes_accessed=nbytes, transcendentals=0),
    )


def f32s(*shape):
    return jax.ShapeDtypeStruct(shape, F32)


def shift(axis, d):
    if axis == "x":
        return "adapter", [(i, ((i // 2 + d) % RING) * 2 + i % 2) for i in range(8)]
    if axis == "core":
        return "adapter", [(i, i ^ 1) for i in range(8)]
    if axis == "y":
        return "row", [(i, (i // 4) * 4 + (i % 4 + d) % RING) for i in range(16)]
    return "row", [(i, ((i // 4 + d) % RING) * 4 + i % 4) for i in range(16)]


def send(value, axis, d=1):
    name, perm = shift(axis, d)
    return lax.ppermute(value, name, perm)


def exchange(value, axis):
    return [value] + [send(value, axis, d) for d in (1, 2, 3)]


def split3(value):
    high = value.astype(BF16)
    rest = value - high.astype(F32)
    mid = rest.astype(BF16)
    return high, mid, (rest - mid.astype(F32)).astype(BF16)


def arrange_kernel(pos_ref, a_ref, o_ref):
    c, z, y = pos_ref[1], pos_ref[2], pos_ref[3]
    for h in range(2):
        for first in range(RING):
            for second in range(RING):
                dy, dz = (first, second) if h == 0 else (second, first)
                source = lax.rem(z + RING - dz, RING) * RING + lax.rem(y + RING - dy, RING)
                block = a_ref[source, h]
                swapped = jnp.concatenate([block[:, 128:], block[:, :128]], axis=1)
                at = (h * 16 + first * 4 + second) * 96
                o_ref[at : at + 96, :] = jnp.where(c == 0, block, swapped)


def arrange(pos, factors):
    turned = factors.T.reshape(16, 2, 96, 256)
    return call(
        arrange_kernel, jax.ShapeDtypeStruct((3072, 256), BF16), 2, 0, 3 << 20, smem=1
    )(pos, turned)


def project_kernel(a_ref, top_ref, low_ref, *o_refs):
    parts = split3(jnp.concatenate([top_ref[...], low_ref[...]], axis=0))
    for i, o_ref in enumerate(o_refs):
        block = a_ref[i * 384 : (i + 1) * 384, :]
        o_ref[...] = sum(
            jnp.dot(block, part, preferred_element_type=F32) for part in reversed(parts)
        )


def project(turned, top, low):
    return call(project_kernel, [f32s(384, 256)] * 8, 3, 6 * 3072 << 16, 5 << 20)(
        turned, top, low
    )


def gram_kernel(pos_ref, top_ref, low_ref, o_ref, g_ref):
    g = sum(
        lax.dot_general(r[...], r[...], (((0,), (0,)), ((), ())), precision=HIGH,
                        preferred_element_type=F32)
        for r in (top_ref, low_ref)
    )
    g_ref[...] = g
    at = pl.multiple_of((pos_ref[0] * 2 + pos_ref[1]) * 32, 32)
    o_ref[...] = g_ref[pl.ds(at, 32), :]


def gram(pos, top, low):
    return call(gram_kernel, f32s(32, 256), 3, 12 << 24, 1 << 19,
                [pltpu.VMEM((256, 256), F32)], smem=1)(pos, top, low)


def inverse_kernel(pos_ref, g0, g1, g2, g3, o_ref, w_ref):
    x = pos_ref[0]
    for dx, g in enumerate((g0, g1, g2, g3)):
        at = pl.multiple_of(lax.rem(x + RING - dx, RING) * 64, 64)
        w_ref[pl.ds(at, 64), :] = g[...]
    lane = lax.broadcasted_iota(jnp.int32, (PANEL, K), 1)
    row = lax.broadcasted_iota(jnp.int32, (PANEL, K), 0)
    row_one = lax.broadcasted_iota(jnp.int32, (PANEL, 1), 0)
    lane_one = lax.broadcasted_iota(jnp.int32, (1, K), 1)
    all_lane = lax.broadcasted_iota(jnp.int32, (K, K), 1)
    all_row = lax.broadcasted_iota(jnp.int32, (K, K), 0)
    for lo in range(0, K, PANEL):
        hi = lo + PANEL
        r = w_ref[lo:hi, :]
        pivots = jnp.ones((PANEL, 1), F32)
        for j in range(PANEL):
            at = lo + j
            pivot = r[j : j + 1, at : at + 1]
            column = jnp.where(row_one > j, r[:, at : at + 1], 0.0)
            line = jnp.where(lane_one == at, 1.0, r[j : j + 1, :]) * (1.0 / pivot)
            pivots = jnp.where(row_one == j, pivot, pivots)
            kept = jnp.where((lane == at) & (row >= j), jnp.where(row == j, 1.0, 0.0), r)
            r = kept - column * line
        clean = jnp.where((lane < hi) & (lane > row + lo), 0.0, r)
        o_ref[lo:hi, :] = jnp.where(lane <= row + lo, clean, 0.0) * lax.rsqrt(pivots)
        if hi < K:
            times = jnp.where(lane >= hi, r, 0.0) / pivots
            change = jnp.dot(times.T, clean, precision=HIGH, preferred_element_type=F32)
            gone = (all_lane >= lo) & (all_lane < hi) & (all_row >= hi)
            w_ref[...] = jnp.where(gone, 0.0, w_ref[...]) - change


def inverse_factor(pos, pieces):
    return call(inverse_kernel, f32s(K, K), 5, 1 << 31, 1 << 19,
                [pltpu.VMEM((K, K), F32)], smem=1)(pos, *pieces)


def block_mask(n):
    rows = lax.broadcasted_iota(jnp.int32, (n, n), 0) // PADDED_RANK
    return rows == lax.broadcasted_iota(jnp.int32, (n, n), 1) // PADDED_RANK


def couple(own, other, scale):
    small = lax.dot_general(other, other, (((1,), (1,)), ((), ())), precision=HIGH,
                            preferred_element_type=F32)
    small = jnp.where(block_mask(192), small, 0.0)
    return jnp.dot(small, own, precision=HIGH, preferred_element_type=F32) * scale


def first_kernel(*refs):
    left, right = refs[0:8], refs[8:16]
    scale_ref, c0, c1, p_ref, q_ref = refs[16:]
    scale = scale_ref[...]
    p, q = (
        jnp.concatenate([sum(r[...] for r in s[0:4]), sum(r[...] for r in s[4:8])], axis=0) * scale
        for s in (left, right)
    )
    coupling = couple(p, q, scale)
    c0[...] = coupling[:96]
    c1[...] = coupling[96:]
    p_ref[...] = p
    q_ref[...] = q


def next_kernel(*refs):
    pieces = refs[0:8]
    linv_ref, scale_ref, other_ref, c0, c1, p_ref = refs[8:]
    scale = scale_ref[...]
    total = jnp.concatenate(
        [sum(r[...] for r in pieces[0:4]), sum(r[...] for r in pieces[4:8])], axis=0
    )
    p = lax.dot_general(total, linv_ref[...], (((1,), (1,)), ((), ())), precision=HIGH,
                        preferred_element_type=F32) * scale
    coupling = couple(other_ref[...], p, scale)
    c0[...] = coupling[:96]
    c1[...] = coupling[96:]
    p_ref[...] = p


def last_kernel(*refs):
    pieces = refs[0:8]
    linv_ref, scale_ref, q0, q1 = refs[8:]
    total = jnp.concatenate(
        [sum(r[...] for r in pieces[0:4]), sum(r[...] for r in pieces[4:8])], axis=0
    )
    q = lax.dot_general(total, linv_ref[...], (((1,), (1,)), ((), ())), precision=HIGH,
                        preferred_element_type=F32) * scale_ref[...]
    q0[...] = q[:96]
    q1[...] = q[96:]


def update_kernel(a_ref, *refs):
    blocks, (keep_ref, send_ref) = refs[:8], refs[8:]
    total = jnp.zeros((256, 256), F32)
    for i, block in enumerate(blocks):
        a = a_ref[:, i * 384 : (i + 1) * 384]
        total += sum(
            jnp.dot(a, part, preferred_element_type=F32) for part in reversed(split3(block[...]))
        )
    keep_ref[...] = total[:128]
    send_ref[...] = total[128:]


def update(factors, blocks):
    return call(update_kernel, [f32s(128, 256)] * 2, 9, 6 * 3072 << 16, 5 << 20)(
        factors, *blocks
    )


def basis_kernel(pos_ref, top_ref, low_ref, linv_ref, o_ref):
    c = pos_ref[1]
    linv = linv_ref[...]
    for at, r in ((c, top_ref), (1 - c, low_ref)):
        o_ref[pl.ds(pl.multiple_of(at * 128, 128), 128), :] = lax.dot_general(
            r[...], linv, (((1,), (1,)), ((), ())), precision=HIGH, preferred_element_type=F32
        )


def basis_of(pos, top, low, linv):
    return call(basis_kernel, f32s(256, 256), 4, 12 << 24, 1 << 20, smem=1)(
        pos, top, low, linv
    )


def cores_kernel(pos_ref, p_ref, *refs):
    blocks, o_ref = refs[:8], refs[8]
    z, y = pos_ref[2], pos_ref[3]
    mask = block_mask(96)
    for h in range(2):
        for first in range(RING):
            for second in range(RING):
                dy, dz = (first, second) if h == 0 else (second, first)
                source = lax.rem(z + RING - dz, RING) * RING + lax.rem(y + RING - dy, RING)
                p = p_ref[source, h]
                wide = jnp.where(mask, jnp.concatenate([p] * 6, axis=0), 0.0)
                q = blocks[h * 4 + first][second * 96 : second * 96 + 96, :]
                core = jnp.dot(wide, q, precision=HIGH, preferred_element_type=F32)
                o_ref[pl.ds(source * 12 + h * 6, 6)] = core.reshape(6, 16, 256)


def scatter(blocks):
    pieces = []
    for mine, (axis, other) in ((blocks[:4], ("y", "z")), (blocks[4:], ("z", "y"))):
        arrived = [mine[0]] + [send(mine[d], axis, -d) for d in (1, 2, 3)]
        parts = [sum(a[i * 96 : i * 96 + 96] for a in arrived) for i in range(RING)]
        pieces += [parts[0]] + [send(parts[d], other, -d) for d in (1, 2, 3)]
    return pieces


def gather(halves):
    blocks = []
    for half, (axis, other) in zip(halves, (("z", "y"), ("y", "z"))):
        blocks += exchange(jnp.concatenate(exchange(half, axis), axis=0), other)
    return blocks


def refit(pos, factors, turned, coupling):
    keep, other = update(factors, gather(coupling))
    half = sum(exchange(keep + send(other, "core"), "x"))
    rest = send(half, "core")
    piece = gram(pos, half, rest)
    piece = sum(exchange(piece, "z"))
    piece = sum(exchange(piece, "y"))
    mate = send(piece, "core")
    pair = jnp.where(
        pos[1] == 0,
        jnp.concatenate([piece, mate], axis=0),
        jnp.concatenate([mate, piece], axis=0),
    )
    linv = inverse_factor(pos, exchange(pair, "x"))
    pieces = scatter(project(turned, half, rest))
    return half, rest, linv, pieces


def column_scale(ranks):
    positions = jnp.arange(PADDED_RANK, dtype=jnp.int32)
    live = positions[None, :] < ranks[:, None]
    factor = 4.0 / jnp.sqrt(ranks.astype(F32))
    return jnp.where(live, factor[:, None], F32(0.0)).reshape(-1, 1)


def shards(up, down, ranks, left, right):
    adapter, row = lax.axis_index("adapter"), lax.axis_index("row")
    c = adapter % 2
    pos = jnp.stack([adapter // 2, c, row // 4, row % 4]).astype(jnp.int32)
    scale = column_scale(lax.dynamic_slice_in_dim(ranks, row * 12, 12, 0))

    def halves(basis):
        return (
            lax.dynamic_slice_in_dim(basis, c * 128, 128, 0),
            lax.dynamic_slice_in_dim(basis, (1 - c) * 128, 128, 0),
        )

    up_turned = arrange(pos, up)
    left_pieces = scatter(project(up_turned, *halves(left)))
    down_turned = arrange(pos, down)
    right_pieces = scatter(project(down_turned, *halves(right)))
    up, down = up_turned.T, down_turned.T
    c0, c1, p, q = call(
        first_kernel, [f32s(96, 256)] * 2 + [f32s(192, 256)] * 2, 17, 1 << 28, 3 << 20
    )(*left_pieces, *right_pieces, scale)

    step = call(next_kernel, [f32s(96, 256)] * 2 + [f32s(192, 256)], 11, 1 << 29, 3 << 20)
    for sweep in range(ITERS):
        top, low, linv, pieces = refit(pos, up, up_turned, (c0, c1))
        if sweep == ITERS - 1:
            left = basis_of(pos, top, low, linv)
        c0, c1, p = step(*pieces, linv, scale, q)
        if sweep == ITERS - 1:
            sent = p.reshape(2, 96, 16, 16).transpose(2, 0, 3, 1)
            p_rows = lax.all_to_all(sent, "row", 0, 0)
        top, low, linv, pieces = refit(pos, down, down_turned, (c0, c1))
        if sweep == ITERS - 1:
            right = basis_of(pos, top, low, linv)
            q_halves = call(last_kernel, [f32s(96, 256)] * 2, 10, 1 << 28, 2 << 20)(
                *pieces, linv, scale
            )
        else:
            c0, c1, q = step(*pieces, linv, scale, p)
    cores = call(cores_kernel, f32s(192, 16, 256), 10, 1 << 30, 6 << 20, smem=1)(
        pos, p_rows, *gather(q_halves)
    )
    return left, right, cores


def solution(mesh):
    return jax.shard_map(
        shards,
        mesh=mesh,
        in_specs=(
            P("row", "adapter"),
            P("row", "adapter"),
            P("adapter"),
            P("row", None),
            P("row", None),
        ),
        out_specs=(P("row", None), P("row", None), P("adapter", "row", None)),
        check_vma=False,
    )
```

time: 1530 us -> 675 us (0.44)
  waiting for transfers between devices: 1080 us -> 189 us
  starting transfers between devices: 2.09 us -> 285 us
  other arithmetic: 241 us -> 8.5 us
  Pallas kernels: 0 us -> 147 us
  matrix products: 104 us -> 0 us
  local copies, waits for them, and re-layouts: 66.2 us -> 32 us
  between operations: 20 us -> 2.42 us
    psum x13 -> x0, waiting for transfers between devices: 1080 us -> none  [the longest x4 376 us: project_sum(): return lax.psum(project_locally(basis, factors, column_scaling), 'row')]
    ppermute x0 -> x192, starting transfers between devices: none -> 282 us  [send(): return lax.ppermute(value, name, perm)]
    another operation x38 -> x1, other arithmetic: 234 us -> 0.08 us  [shards(): pos = jnp.stack([adapter // 2, c, row // 4, row % 4]).astype(jnp.int32)]
    ppermute x0 -> x192, waiting for transfers between devices: none -> 186 us  [send(): return lax.ppermute(value, name, perm)]
    pallas_call x0 -> x28, Pallas kernels: none -> 147 us  [the longest x4 105 us: inverse_factor(): call(inverse_kernel, f32s(K, K), 5, 1 << 31, 1 << 19, [pltpu.VMEM((K, K),...]
    dot_general x23 -> x0, matrix products: 85.1 us -> none  [the longest x4 24 us: coupling_of(): jnp.einsum('kar,kas->ars', other_rows, other_rows, precision=lax.Precisio...]
    another operation x37 -> x0, local copies, waits for them, and re-layouts: 30.4 us -> none  [the longest x29 26.8 us: basis_refitting(): lax.linalg.triangular_solve(lower, update, left_side=False, lower=True, t...]
    another operation x20 -> x0, matrix products: 19 us -> none  [the longest x12 9.5 us: basis_refitting(): lax.linalg.triangular_solve(lower, update, left_side=False, lower=True, t...]
  transfers between devices with their start and end apart: 13 -> 193, of which waited for: 13 -> 70; matrix products, arithmetic and copies ran while one was open for 0% -> 4% of each run, Pallas kernels for 0% -> 18%
where the time goes in v1:
time: 675 us; the launch traced here: 664 us
  starting transfers between devices  285 us (42%)
  waiting for transfers between devices  189 us (28%)
  Pallas kernels  147 us (22%)
  local copies, waits for them, and re-layouts  32 us (5%)
  other arithmetic  8.5 us (1%)
    ppermute x192, starting transfers between devices, send(): return lax.ppermute(value, name, perm)  282 us
    ppermute x192, waiting for transfers between devices, send(): return lax.ppermute(value, name, perm)  186 us
    pallas_call x4, Pallas kernels, inverse_factor(): call(inverse_kernel, f32s(K, K), 5, 1 << 31, 1 << 19, [pltpu.VMEM((K, K),...  105 us
    unnamed x100, local copies, waits for them, and re-layouts  20.8 us
  transfers between devices with their start and end apart: 193, of which 70 were waited for; matrix products, arithmetic and copies ran while one was open for 4% of the time, Pallas kernels for 18%

profile of v1, /device:TPU:0, one launch (start us, length us, event | category | flops | bytes accessed | tf_op | source)
XLA Modules:
  0.0 664.2 jit_solution(12252796095328392828)
XLA Ops:
  7.6 4.1 collective-permute-start.18
  24.0 4.9 collective-permute-done.18
  42.2 7.9 %collective-permute-done.6 = f32[384,256]{1,0:T(8,128)} collective-permute-done((f32[384,256]{1,0:T(8,128)}, f32[384,256]{1,0:T(8,128)}, u32[]{:S(2)}, u32[]{:S(2)}) %collective-permute-start.6) | collective-permute-done | bytes 393248 | tf_op jit(solution)/shard_map/ppermute | solution.py:51
  61.5 4.6 collective-permute-start.17
  112.5 4.2 collective-permute-done.28.refs_2_
  157.9 6.2 collective-permute-done.48
  165.4 4.5 collective-permute-done.49
  183.8 9.6 %collective-permute-start.46 = (f32[96,256]{1,0:T(8,128)S(1)}, f32[96,256]{1,0:T(8,128)S(1)}, u32[]{:S(2)}, u32[]{:S(2)}) collective-permute-start(f32[96,256]{1,0:T(8,128)S(1)} %get-tuple-element.173), channel_id=1, source_target_pairs={{0,4},{1,5},{2,6},{3,7},{4,8},{5,9},{6,10},{7,11},{8,12},{9,13},{1... | collective-permute-start | bytes 294920 | tf_op jit(solution)/shard_map/ppermute | solution.py:51
  193.3 26.3 %shard_map.84.refs_8_ = f32[256,256]{1,0:T(8,128)S(1)} custom-call(s32[4]{0:T(128)S(1)} %pad_add_fusion.pos_ref, f32[64,256]{1,0:T(8,128)S(1)} %maximum_select_fusion.g0, f32[64,256]{1,0:T(8,128)S(1)} %collective-permute-done.60.g1, f32[64,256]{1,0:T(8,128)S(1)} %collective-permute-done.61.g2, f32[64,256]{1,0:T(8,128)S(1)} %collective-permute-done.62.g3), custom_call_target="tpu_custom_call" | custom-call | flops 2147483648 | bytes 524288 | tf_op jit(solution)/shard_map/pallas_call | solution.py:149
  241.1 6.4 collective-permute-done.64
  255.7 6.5 collective-permute-done.66.refs_1_
  273.6 5.1 collective-permute-done.76
  282.6 4.5 collective-permute-start.93
  302.9 6.3 collective-permute-done.87
  309.8 4.1 collective-permute-done.88
  316.5 5.5 collective-permute-start.89
  326.8 26.3 %shard_map.89.refs_8_ = f32[256,256]{1,0:T(8,128)S(1)} custom-call(s32[4]{0:T(128)S(1)} %pad_add_fusion.pos_ref, f32[64,256]{1,0:T(8,128)S(1)} %maximum_select_fusion.1.g0, f32[64,256]{1,0:T(8,128)S(1)} %collective-permute-done.99.g1, f32[64,256]{1,0:T(8,128)S(1)} %collective-permute-done.100.g2, f32[64,256]{1,0:T(8,128)S(1)} %collective-permute-done.101.g3), custom_call_target="tpu_custom_call" | custom-call | flops 2147483648 | bytes 524288 | tf_op jit(solution)/shard_map/pallas_call | solution.py:149
  373.4 7.1 %collective-permute-done.103 = f32[96,256]{1,0:T(8,128)S(1)} collective-permute-done((f32[96,256]{1,0:T(8,128)S(1)}, f32[96,256]{1,0:T(8,128)S(1)}, u32[]{:S(2)}, u32[]{:S(2)}) %collective-permute-start.103) | collective-permute-done | bytes 98336 | tf_op jit(solution)/shard_map/ppermute | solution.py:51
  389.1 7.2 %collective-permute-done.105.refs_1_ = f32[384,256]{1,0:T(8,128)S(1)} collective-permute-done((f32[384,256]{1,0:T(8,128)S(1)}, f32[384,256]{1,0:T(8,128)S(1)}, u32[]{:S(2)}, u32[]{:S(2)}) %collective-permute-start.105) | collective-permute-done | bytes 393248 | tf_op jit(solution)/shard_map/ppermute | solution.py:51
  431.1 6.1 collective-permute-done.136
  437.5 5.5 collective-permute-done.137
  458.7 26.3 %shard_map.93.linv_ref.refs_8_ = f32[256,256]{1,0:T(8,128)S(1)} custom-call(s32[4]{0:T(128)S(1)} %pad_add_fusion.pos_ref, f32[64,256]{1,0:T(8,128)S(1)} %maximum_select_fusion.2.g0, f32[64,256]{1,0:T(8,128)S(1)} %collective-permute-done.126.g1, f32[64,256]{1,0:T(8,128)S(1)} %collective-permute-done.127.g2, f32[64,256]{1,0:T(8,128)S(1)} %collective-permute-done.128.g3), custom_call_target="tpu_custom_call" | custom-call | flops 2147483648 | bytes 524288 | tf_op jit(solution)/shard_map/pallas_call | solution.py:149
  486.5 4.6 collective-permute-start.148
  504.1 7.2 %collective-permute-done.142 = f32[96,256]{1,0:T(8,128)S(1)} collective-permute-done((f32[96,256]{1,0:T(8,128)S(1)}, f32[96,256]{1,0:T(8,128)S(1)}, u32[]{:S(2)}, u32[]{:S(2)}) %collective-permute-start.142) | collective-permute-done | bytes 98336 | tf_op jit(solution)/shard_map/ppermute | solution.py:51
  517.5 7.1 %collective-permute-done.144.refs_1_ = f32[384,256]{1,0:T(8,128)S(1)} collective-permute-done((f32[384,256]{1,0:T(8,128)S(1)}, f32[384,256]{1,0:T(8,128)S(1)}, u32[]{:S(2)}, u32[]{:S(2)}) %collective-permute-start.144) | collective-permute-done | bytes 393248 | tf_op jit(solution)/shard_map/ppermute | solution.py:51
  559.7 6.3 collective-permute-done.175
  566.2 5.3 collective-permute-done.176
  574.7 4.3 collective-permute-start.177
  587.0 26.3 %shard_map.99.linv_ref.refs_8_ = f32[256,256]{1,0:T(8,128)S(1)} custom-call(s32[4]{0:T(128)S(1)} %pad_add_fusion.pos_ref, f32[64,256]{1,0:T(8,128)S(1)} %maximum_select_fusion.3.g0, f32[64,256]{1,0:T(8,128)S(1)} %collective-permute-done.165.g1, f32[64,256]{1,0:T(8,128)S(1)} %collective-permute-done.166.g2, f32[64,256]{1,0:T(8,128)S(1)} %collective-permute-done.167.g3), custom_call_target="tpu_custom_call" | custom-call | flops 2147483648 | bytes 524288 | tf_op jit(solution)/shard_map/pallas_call | solution.py:149
  613.9 4.6 collective-permute-start.187
  631.6 7.2 %collective-permute-done.181 = f32[96,256]{1,0:T(8,128)S(1)} collective-permute-done((f32[96,256]{1,0:T(8,128)S(1)}, f32[96,256]{1,0:T(8,128)S(1)}, u32[]{:S(2)}, u32[]{:S(2)}) %collective-permute-start.181) | collective-permute-done | bytes 98336 | tf_op jit(solution)/shard_map/ppermute | solution.py:51
  658.3 5.4 shard_map.103
  (536 shorter events, 394.1 us)
Async XLA Ops:
  7.6 21.2 %collective-permute-start.18 = (f32[384,256]{1,0:T(8,128)}, f32[384,256]{1,0:T(8,128)}, u32[]{:S(2)}, u32[]{:S(2)}) collective-permute-start(f32[384,256]{1,0:T(8,128)} %get-tuple-element.86), channel_id=1, source_target_pairs={{0,12},{1,13},{2,14},{3,15},{4,0},{5,1},{6,2},{7,3},{8,4},{9,5},{1... | collective-permute-start | bytes 1179656 | tf_op jit(solution)/shard_map/ppermute | solution.py:51
  11.7 22.5 %collective-permute-start.20 = (f32[384,256]{1,0:T(8,128)}, f32[384,256]{1,0:T(8,128)}, u32[]{:S(2)}, u32[]{:S(2)}) collective-permute-start(f32[384,256]{1,0:T(8,128)} %get-tuple-element.88), channel_id=1, source_target_pairs={{0,4},{1,5},{2,6},{3,7},{4,8},{5,9},{6,10},{7,11},{8,12},{9,13},{1... | collective-permute-start | bytes 1179656 | tf_op jit(solution)/shard_map/ppermute | solution.py:51
  13.0 21.3 %collective-permute-start.12 = (f32[384,256]{1,0:T(8,128)}, f32[384,256]{1,0:T(8,128)}, u32[]{:S(2)}, u32[]{:S(2)}) collective-permute-start(f32[384,256]{1,0:T(8,128)} %get-tuple-element.82), channel_id=1, source_target_pairs={{0,3},{1,0},{2,1},{3,2},{4,7},{5,4},{6,5},{7,6},{8,11},{9,8},{10,9... | collective-permute-start | bytes 1179656 | tf_op jit(solution)/shard_map/ppermute | solution.py:51
  16.0 20.6 %collective-permute-start.13 = (f32[384,256]{1,0:T(8,128)}, f32[384,256]{1,0:T(8,128)}, u32[]{:S(2)}, u32[]{:S(2)}) collective-permute-start(f32[384,256]{1,0:T(8,128)} %get-tuple-element.83), channel_id=1, source_target_pairs={{0,2},{1,3},{2,0},{3,1},{4,6},{5,7},{6,4},{7,5},{8,10},{9,11},{10,... | collective-permute-start | bytes 1179656 | tf_op jit(solution)/shard_map/ppermute | solution.py:51
  34.2 20.6 %collective-permute-start.8 = (f32[384,256]{1,0:T(8,128)}, f32[384,256]{1,0:T(8,128)S(1)}, u32[]{:S(2)}, u32[]{:S(2)}) collective-permute-start(f32[384,256]{1,0:T(8,128)} %copy-done.27), channel_id=1, source_target_pairs={{0,4},{1,5},{2,6},{3,7},{4,8},{5,9},{6,10},{7,11},{8,12},{9,13},{1... | collective-permute-start | bytes 1179656 | tf_op jit(solution)/shard_map/ppermute | solution.py:51
  36.6 21.2 %collective-permute-start = (f32[384,256]{1,0:T(8,128)S(1)}, f32[384,256]{1,0:T(8,128)S(1)}, u32[]{:S(2)}, u32[]{:S(2)}) collective-permute-start(f32[384,256]{1,0:T(8,128)S(1)} %copy-done.26), channel_id=1, source_target_pairs={{0,3},{1,0},{2,1},{3,2},{4,7},{5,4},{6,5},{7,6},{8,11},{9,8},{10,9... | collective-permute-start | bytes 1179656 | tf_op jit(solution)/shard_map/ppermute | solution.py:51
  153.7 20.3 %collective-permute-start.41 = (f32[384,256]{1,0:T(8,128)}, f32[384,256]{1,0:T(8,128)S(1)}, u32[]{:S(2)}, u32[]{:S(2)}) collective-permute-start(f32[384,256]{1,0:T(8,128)} %get-tuple-element.94), channel_id=1, source_target_pairs={{0,3},{1,0},{2,1},{3,2},{4,7},{5,4},{6,5},{7,6},{8,11},{9,8},{10,9... | collective-permute-start | bytes 1179656 | tf_op jit(solution)/shard_map/ppermute | solution.py:51
  157.1 21.9 %collective-permute-start.43 = (f32[384,256]{1,0:T(8,128)}, f32[384,256]{1,0:T(8,128)}, u32[]{:S(2)}, u32[]{:S(2)}) collective-permute-start(f32[384,256]{1,0:T(8,128)} %get-tuple-element.96), channel_id=1, source_target_pairs={{0,1},{1,2},{2,3},{3,0},{4,5},{5,6},{6,7},{7,4},{8,9},{9,10},{10,1... | collective-permute-start | bytes 1179656 | tf_op jit(solution)/shard_map/ppermute | solution.py:51
  179.0 40.6 %collective-permute-start.51 = (f32[96,256]{1,0:T(8,128)S(1)}, f32[96,256]{1,0:T(8,128)S(1)}, u32[]{:S(2)}, u32[]{:S(2)}) collective-permute-start(f32[96,256]{1,0:T(8,128)S(1)} %get-tuple-element.170), channel_id=1, source_target_pairs={{0,2},{1,3},{2,0},{3,1},{4,6},{5,7},{6,4},{7,5},{8,10},{9,11},{10,... | collective-permute-start | bytes 294920 | tf_op jit(solution)/shard_map/ppermute | solution.py:51
  180.3 39.3 %collective-permute-start.52 = (f32[96,256]{1,0:T(8,128)S(1)}, f32[96,256]{1,0:T(8,128)S(1)}, u32[]{:S(2)}, u32[]{:S(2)}) collective-permute-start(f32[96,256]{1,0:T(8,128)S(1)} %get-tuple-element.169), channel_id=1, source_target_pairs={{0,1},{1,2},{2,3},{3,0},{4,5},{5,6},{6,7},{7,4},{8,9},{9,10},{10,1... | collective-permute-start | bytes 294920 | tf_op jit(solution)/shard_map/ppermute | solution.py:51
  181.2 38.5 %collective-permute-start.44 = (f32[96,256]{1,0:T(8,128)S(1)}, f32[96,256]{1,0:T(8,128)S(1)}, u32[]{:S(2)}, u32[]{:S(2)}) collective-permute-start(f32[96,256]{1,0:T(8,128)S(1)} %get-tuple-element.175), channel_id=1, source_target_pairs={{0,12},{1,13},{2,14},{3,15},{4,0},{5,1},{6,2},{7,3},{8,4},{9,5},{1... | collective-permute-start | bytes 294920 | tf_op jit(solution)/shard_map/ppermute | solution.py:51
  183.7 36.0 %collective-permute-start.45 = (f32[96,256]{1,0:T(8,128)S(1)}, f32[96,256]{1,0:T(8,128)S(1)}, u32[]{:S(2)}, u32[]{:S(2)}) collective-permute-start(f32[96,256]{1,0:T(8,128)S(1)} %get-tuple-element.174), channel_id=1, source_target_pairs={{0,8},{1,9},{2,10},{3,11},{4,12},{5,13},{6,14},{7,15},{8,0},{9,1},... | collective-permute-start | bytes 294920 | tf_op jit(solution)/shard_map/ppermute | solution.py:51
  183.8 36.0 %collective-permute-start.46 = (f32[96,256]{1,0:T(8,128)S(1)}, f32[96,256]{1,0:T(8,128)S(1)}, u32[]{:S(2)}, u32[]{:S(2)}) collective-permute-start(f32[96,256]{1,0:T(8,128)S(1)} %get-tuple-element.173), channel_id=1, source_target_pairs={{0,4},{1,5},{2,6},{3,7},{4,8},{5,9},{6,10},{7,11},{8,12},{9,13},{1... | collective-permute-start | bytes 294920 | tf_op jit(solution)/shard_map/ppermute | solution.py:51
  231.5 20.3 %collective-permute-start.72 = (f32[384,256]{1,0:T(8,128)}, f32[384,256]{1,0:T(8,128)S(1)}, u32[]{:S(2)}, u32[]{:S(2)}) collective-permute-start(f32[384,256]{1,0:T(8,128)} %constant_dynamic-update-slice_fusion.12.refs_4_), channel_id=1, source_target_pairs={{0,4},{1,5},{2,6},{3,7},{4,8},{5,9},{6,10},{7,11},{8,12},{9,13},{1... | collective-permute-start | bytes 1179656 | tf_op jit(solution)/shard_map/ppermute | solution.py:51
  322.1 31.0 %collective-permute-start.90 = (f32[96,256]{1,0:T(8,128)S(1)}, f32[96,256]{1,0:T(8,128)S(1)}, u32[]{:S(2)}, u32[]{:S(2)}) collective-permute-start(f32[96,256]{1,0:T(8,128)S(1)} %get-tuple-element.162), channel_id=1, source_target_pairs={{0,2},{1,3},{2,0},{3,1},{4,6},{5,7},{6,4},{7,5},{8,10},{9,11},{10,... | collective-permute-start | bytes 294920 | tf_op jit(solution)/shard_map/ppermute | solution.py:51
  323.4 29.7 %collective-permute-start.91 = (f32[96,256]{1,0:T(8,128)S(1)}, f32[96,256]{1,0:T(8,128)S(1)}, u32[]{:S(2)}, u32[]{:S(2)}) collective-permute-start(f32[96,256]{1,0:T(8,128)S(1)} %get-tuple-element.161), channel_id=1, source_target_pairs={{0,1},{1,2},{2,3},{3,0},{4,5},{5,6},{6,7},{7,4},{8,9},{9,10},{10,1... | collective-permute-start | bytes 294920 | tf_op jit(solution)/shard_map/ppermute | solution.py:51
  323.7 29.4 %collective-permute-start.83 = (f32[96,256]{1,0:T(8,128)S(1)}, f32[96,256]{1,0:T(8,128)S(1)}, u32[]{:S(2)}, u32[]{:S(2)}) collective-permute-start(f32[96,256]{1,0:T(8,128)S(1)} %get-tuple-element.167), channel_id=1, source_target_pairs={{0,12},{1,13},{2,14},{3,15},{4,0},{5,1},{6,2},{7,3},{8,4},{9,5},{1... | collective-permute-start | bytes 294920 | tf_op jit(solution)/shard_map/ppermute | solution.py:51
  325.2 27.9 %collective-permute-start.84 = (f32[96,256]{1,0:T(8,128)S(1)}, f32[96,256]{1,0:T(8,128)S(1)}, u32[]{:S(2)}, u32[]{:S(2)}) collective-permute-start(f32[96,256]{1,0:T(8,128)S(1)} %get-tuple-element.166), channel_id=1, source_target_pairs={{0,8},{1,9},{2,10},{3,11},{4,12},{5,13},{6,14},{7,15},{8,0},{9,1},... | collective-permute-start | bytes 294920 | tf_op jit(solution)/shard_map/ppermute | solution.py:51
  326.2 26.9 %collective-permute-start.85 = (f32[96,256]{1,0:T(8,128)S(1)}, f32[96,256]{1,0:T(8,128)S(1)}, u32[]{:S(2)}, u32[]{:S(2)}) collective-permute-start(f32[96,256]{1,0:T(8,128)S(1)} %get-tuple-element.165), channel_id=1, source_target_pairs={{0,4},{1,5},{2,6},{3,7},{4,8},{5,9},{6,10},{7,11},{8,12},{9,13},{1... | collective-permute-start | bytes 294920 | tf_op jit(solution)/shard_map/ppermute | solution.py:51
  450.3 34.7 %collective-permute-start.139 = (f32[96,256]{1,0:T(8,128)S(1)}, f32[96,256]{1,0:T(8,128)S(1)}, u32[]{:S(2)}, u32[]{:S(2)}) collective-permute-start(f32[96,256]{1,0:T(8,128)S(1)} %get-tuple-element.154), channel_id=1, source_target_pairs={{0,2},{1,3},{2,0},{3,1},{4,6},{5,7},{6,4},{7,5},{8,10},{9,11},{10,... | collective-permute-start | bytes 294920 | tf_op jit(solution)/shard_map/ppermute | solution.py:51
  454.2 30.8 %collective-permute-start.140 = (f32[96,256]{1,0:T(8,128)S(1)}, f32[96,256]{1,0:T(8,128)S(1)}, u32[]{:S(2)}, u32[]{:S(2)}) collective-permute-start(f32[96,256]{1,0:T(8,128)S(1)} %get-tuple-element.153), channel_id=1, source_target_pairs={{0,1},{1,2},{2,3},{3,0},{4,5},{5,6},{6,7},{7,4},{8,9},{9,10},{10,1... | collective-permute-start | bytes 294920 | tf_op jit(solution)/shard_map/ppermute | solution.py:51
  454.3 30.7 %collective-permute-start.132 = (f32[96,256]{1,0:T(8,128)S(1)}, f32[96,256]{1,0:T(8,128)S(1)}, u32[]{:S(2)}, u32[]{:S(2)}) collective-permute-start(f32[96,256]{1,0:T(8,128)S(1)} %get-tuple-element.159), channel_id=1, source_target_pairs={{0,12},{1,13},{2,14},{3,15},{4,0},{5,1},{6,2},{7,3},{8,4},{9,5},{1... | collective-permute-start | bytes 294920 | tf_op jit(solution)/shard_map/ppermute | solution.py:51
  454.5 30.5 %collective-permute-start.133 = (f32[96,256]{1,0:T(8,128)S(1)}, f32[96,256]{1,0:T(8,128)S(1)}, u32[]{:S(2)}, u32[]{:S(2)}) collective-permute-start(f32[96,256]{1,0:T(8,128)S(1)} %get-tuple-element.158), channel_id=1, source_target_pairs={{0,8},{1,9},{2,10},{3,11},{4,12},{5,13},{6,14},{7,15},{8,0},{9,1},... | collective-permute-start | bytes 294920 | tf_op jit(solution)/shard_map/ppermute | solution.py:51
  457.3 27.7 %collective-permute-start.134 = (f32[96,256]{1,0:T(8,128)S(1)}, f32[96,256]{1,0:T(8,128)S(1)}, u32[]{:S(2)}, u32[]{:S(2)}) collective-permute-start(f32[96,256]{1,0:T(8,128)S(1)} %get-tuple-element.157), channel_id=1, source_target_pairs={{0,4},{1,5},{2,6},{3,7},{4,8},{5,9},{6,10},{7,11},{8,12},{9,13},{1... | collective-permute-start | bytes 294920 | tf_op jit(solution)/shard_map/ppermute | solution.py:51
  579.0 34.3 %collective-permute-start.178 = (f32[96,256]{1,0:T(8,128)S(1)}, f32[96,256]{1,0:T(8,128)S(1)}, u32[]{:S(2)}, u32[]{:S(2)}) collective-permute-start(f32[96,256]{1,0:T(8,128)S(1)} %get-tuple-element.146), channel_id=1, source_target_pairs={{0,2},{1,3},{2,0},{3,1},{4,6},{5,7},{6,4},{7,5},{8,10},{9,11},{10,... | collective-permute-start | bytes 294920 | tf_op jit(solution)/shard_map/ppermute | solution.py:51
  582.5 30.8 %collective-permute-start.179 = (f32[96,256]{1,0:T(8,128)S(1)}, f32[96,256]{1,0:T(8,128)S(1)}, u32[]{:S(2)}, u32[]{:S(2)}) collective-permute-start(f32[96,256]{1,0:T(8,128)S(1)} %get-tuple-element.145), channel_id=1, source_target_pairs={{0,1},{1,2},{2,3},{3,0},{4,5},{5,6},{6,7},{7,4},{8,9},{9,10},{10,1... | collective-permute-start | bytes 294920 | tf_op jit(solution)/shard_map/ppermute | solution.py:51
  582.6 30.7 %collective-permute-start.171 = (f32[96,256]{1,0:T(8,128)S(1)}, f32[96,256]{1,0:T(8,128)S(1)}, u32[]{:S(2)}, u32[]{:S(2)}) collective-permute-start(f32[96,256]{1,0:T(8,128)S(1)} %get-tuple-element.151), channel_id=1, source_target_pairs={{0,12},{1,13},{2,14},{3,15},{4,0},{5,1},{6,2},{7,3},{8,4},{9,5},{1... | collective-permute-start | bytes 294920 | tf_op jit(solution)/shard_map/ppermute | solution.py:51
  583.0 30.4 %collective-permute-start.172 = (f32[96,256]{1,0:T(8,128)S(1)}, f32[96,256]{1,0:T(8,128)S(1)}, u32[]{:S(2)}, u32[]{:S(2)}) collective-permute-start(f32[96,256]{1,0:T(8,128)S(1)} %get-tuple-element.150), channel_id=1, source_target_pairs={{0,8},{1,9},{2,10},{3,11},{4,12},{5,13},{6,14},{7,15},{8,0},{9,1},... | collective-permute-start | bytes 294920 | tf_op jit(solution)/shard_map/ppermute | solution.py:51
  585.7 27.7 %collective-permute-start.173 = (f32[96,256]{1,0:T(8,128)S(1)}, f32[96,256]{1,0:T(8,128)S(1)}, u32[]{:S(2)}, u32[]{:S(2)}) collective-permute-start(f32[96,256]{1,0:T(8,128)S(1)} %get-tuple-element.149), channel_id=1, source_target_pairs={{0,4},{1,5},{2,6},{3,7},{4,8},{5,9},{6,10},{7,11},{8,12},{9,13},{1... | collective-permute-start | bytes 294920 | tf_op jit(solution)/shard_map/ppermute | solution.py:51
  623.1 20.2 %collective-permute-start.189 = (f32[384,256]{1,0:T(8,128)S(1)}, f32[384,256]{1,0:T(8,128)S(1)}, u32[]{:S(2)}, u32[]{:S(2)}) collective-permute-start(f32[384,256]{1,0:T(8,128)S(1)} %constant_dynamic-update-slice_fusion.36.refs_4_), channel_id=1, source_target_pairs={{0,4},{1,5},{2,6},{3,7},{4,8},{5,9},{6,10},{7,11},{8,12},{9,13},{1... | collective-permute-start | bytes 1179656 | tf_op jit(solution)/shard_map/ppermute | solution.py:51
  627.8 30.5 %collective-permute-start.190 = (f32[384,256]{1,0:T(8,128)S(1)}, f32[384,256]{1,0:T(8,128)S(1)}, u32[]{:S(2)}, u32[]{:S(2)}) collective-permute-start(f32[384,256]{1,0:T(8,128)S(1)} %constant_dynamic-update-slice_fusion.36.refs_4_), channel_id=1, source_target_pairs={{0,8},{1,9},{2,10},{3,11},{4,12},{5,13},{6,14},{7,15},{8,0},{9,1},... | collective-permute-start | bytes 1179656 | tf_op jit(solution)/shard_map/ppermute | solution.py:51
  629.7 28.6 %collective-permute-start.191 = (f32[384,256]{1,0:T(8,128)S(1)}, f32[384,256]{1,0:T(8,128)S(1)}, u32[]{:S(2)}, u32[]{:S(2)}) collective-permute-start(f32[384,256]{1,0:T(8,128)S(1)} %constant_dynamic-update-slice_fusion.36.refs_4_), channel_id=1, source_target_pairs={{0,12},{1,13},{2,14},{3,15},{4,0},{5,1},{6,2},{7,3},{8,4},{9,5},{1... | collective-permute-start | bytes 1179656 | tf_op jit(solution)/shard_map/ppermute | solution.py:51
  (196 other events, 2035.8 us)

commit v2 on v1

v2 whole, which is shorter than its diff:
```python
import jax
import jax.numpy as jnp
from jax import lax
from jax.experimental import pallas as pl
from jax.experimental.pallas import tpu as pltpu
from jax.sharding import PartitionSpec as P

PADDED_RANK = 16
ITERS = 2
RING = 4
K = 256
PANEL = 32
ORDER = (0, 1, 3, 2)
HIGH = lax.Precision.HIGHEST
F32 = jnp.float32
BF16 = jnp.bfloat16
VMEM = pl.BlockSpec(memory_space=pltpu.VMEM)
SMEM = pl.BlockSpec(memory_space=pltpu.SMEM)
PARAMS = pltpu.CompilerParams(vmem_limit_bytes=32 * 1024 * 1024)


def call(kernel, outs, n_in, flops, nbytes, scratch=(), smem=0):
    return pl.pallas_call(
        kernel,
        out_shape=outs,
        in_specs=[SMEM] * smem + [VMEM] * (n_in - smem),
        out_specs=jax.tree.map(lambda _: VMEM, outs),
        scratch_shapes=list(scratch),
        compiler_params=PARAMS,
        cost_estimate=pl.CostEstimate(flops=flops, bytes_accessed=nbytes, transcendentals=0),
    )


def f32s(*shape):
    return jax.ShapeDtypeStruct(shape, F32)


def moved(axis, d, x, c, z, y):
    if axis == "core":
        return x, 1 - c, z, y
    if axis == "x":
        return (x + d) % RING, c, z, y
    if (axis == "first") == (c == 0):
        return x, c, z, (y + d) % RING
    return x, c, (z + d) % RING, y


def send(value, axis, d=1):
    perm = []
    for i in range(128):
        x, c, z, y = moved(axis, d, i // 32, i // 16 % 2, i // 4 % 4, i % 4)
        perm.append((i, x * 32 + c * 16 + z * 4 + y))
    return lax.ppermute(value, ("adapter", "row"), perm)


def exchange(value, axis):
    return [value] + [send(value, axis, d) for d in (1, 3, 2)]


def chunk_at(pos_ref, first, second):
    c, z, y = pos_ref[1], pos_ref[2], pos_ref[3]
    dy = jnp.where(c == 0, first, second)
    dz = jnp.where(c == 0, second, first)
    return lax.rem(z + RING - dz, RING) * RING + lax.rem(y + RING - dy, RING)


def split3(value):
    high = value.astype(BF16)
    rest = value - high.astype(F32)
    mid = rest.astype(BF16)
    return high, mid, (rest - mid.astype(F32)).astype(BF16)


def arrange_kernel(pos_ref, a_ref, o_ref):
    for i, first in enumerate(ORDER):
        for j, second in enumerate(ORDER):
            block = a_ref[chunk_at(pos_ref, first, second)]
            swapped = jnp.concatenate([block[:, 128:], block[:, :128]], axis=1)
            at = (i * 4 + j) * 192
            o_ref[at : at + 192, :] = jnp.where(pos_ref[1] == 0, block, swapped)


def arrange(pos, factors):
    return call(
        arrange_kernel, jax.ShapeDtypeStruct((3072, 256), BF16), 2, 0, 3 << 20, smem=1
    )(pos, factors.T.reshape(16, 192, 256))


def project_kernel(a_ref, top_ref, low_ref, *o_refs):
    parts = split3(jnp.concatenate([top_ref[...], low_ref[...]], axis=0))
    for i, o_ref in enumerate(o_refs):
        block = a_ref[i * 768 : (i + 1) * 768, :]
        o_ref[...] = sum(
            jnp.dot(block, part, preferred_element_type=F32) for part in reversed(parts)
        )


def project(turned, top, low):
    return call(project_kernel, [f32s(768, 256)] * 4, 3, 6 * 3072 << 16, 5 << 20)(
        turned, top, low
    )


def gram_kernel(pos_ref, top_ref, low_ref, o_ref, g_ref):
    g_ref[...] = sum(
        lax.dot_general(r[...], r[...], (((0,), (0,)), ((), ())), precision=HIGH,
                        preferred_element_type=F32)
        for r in (top_ref, low_ref)
    )
    o_ref[...] = g_ref[pl.ds(pl.multiple_of(pos_ref[1] * 128, 128), 128), :]


def gram(pos, top, low):
    return call(gram_kernel, f32s(128, 256), 3, 12 << 24, 1 << 19,
                [pltpu.VMEM((256, 256), F32)], smem=1)(pos, top, low)


def eliminate(tall, at):
    n = tall.shape[0]
    sub = lax.broadcasted_iota(jnp.int32, (n, 128), 0)
    lane = lax.broadcasted_iota(jnp.int32, (n, 128), 1)
    half, base = at // 128, at % 128
    columns = [
        jnp.broadcast_to(tall[:, at + k : at + k + 1], (n, 128)) for k in range(8)
    ]
    sides = [tall[:, :128], tall[:, 128:]]
    pivots = jnp.ones((8, 128), F32)
    for j in range(8):
        pivot = columns[j][j : j + 1, :]
        times = jnp.where(sub > j, columns[j], 0.0) * (1.0 / pivot)
        pivots = jnp.where(sub[:8] == j, pivot, pivots)
        for k in range(j + 1, 8):
            columns[k] = columns[k] - times * columns[k][j : j + 1, :]
        here = lane == base + j
        kept = jnp.where(here & (sub >= j), jnp.where(sub == j, 1.0, 0.0), sides[half])
        other = sides[1 - half]
        sides[half] = kept - times * kept[j : j + 1, :]
        sides[1 - half] = other - times * other[j : j + 1, :]
    return jnp.concatenate(sides, axis=1), pivots


def inverse_kernel(pos_ref, mine_ref, mate_ref, o_ref, w_ref):
    for c, ref in ((pos_ref[1], mine_ref), (1 - pos_ref[1], mate_ref)):
        w_ref[pl.ds(pl.multiple_of(c * 128, 128), 128), :] = ref[...]
    lane = lax.broadcasted_iota(jnp.int32, (PANEL, K), 1)
    row = lax.broadcasted_iota(jnp.int32, (PANEL, K), 0)
    all_lane = lax.broadcasted_iota(jnp.int32, (K, K), 1)
    all_row = lax.broadcasted_iota(jnp.int32, (K, K), 0)
    for lo in range(0, K, PANEL):
        hi = lo + PANEL
        rest = w_ref[lo:hi, :]
        done, pivots = [], []
        for at in range(lo, hi, 8):
            rest, found = eliminate(rest, at)
            done.append(rest[:8])
            pivots.append(found)
            rest = rest[8:]
        r = jnp.concatenate(done, axis=0)
        pivots = jnp.concatenate(pivots, axis=0)
        pivots = jnp.concatenate([pivots, pivots], axis=1)
        clean = jnp.where((lane < hi) & (lane > row + lo), 0.0, r)
        o_ref[lo:hi, :] = jnp.where(lane <= row + lo, clean, 0.0) * lax.rsqrt(pivots)
        if hi < K:
            times = jnp.where(lane >= hi, r, 0.0) / pivots
            change = jnp.dot(times.T, clean, precision=HIGH, preferred_element_type=F32)
            gone = (all_lane >= lo) & (all_lane < hi) & (all_row >= hi)
            w_ref[...] = jnp.where(gone, 0.0, w_ref[...]) - change


def inverse_factor(pos, mine, mate):
    return call(inverse_kernel, f32s(K, K), 3, 1 << 33, 1 << 19,
                [pltpu.VMEM((K, K), F32)], smem=1)(pos, mine, mate)


def block_mask(n):
    rows = lax.broadcasted_iota(jnp.int32, (n, n), 0) // PADDED_RANK
    return rows == lax.broadcasted_iota(jnp.int32, (n, n), 1) // PADDED_RANK


def couple(own, other, scale):
    small = lax.dot_general(other, other, (((1,), (1,)), ((), ())), precision=HIGH,
                            preferred_element_type=F32)
    small = jnp.where(block_mask(192), small, 0.0)
    return jnp.dot(small, own, precision=HIGH, preferred_element_type=F32) * scale


def first_kernel(*refs):
    left, right = refs[0:4], refs[4:8]
    scale_ref, c_ref, p_ref, q_ref = refs[8:]
    scale = scale_ref[...]
    p, q = (sum(r[...] for r in side) * scale for side in (left, right))
    c_ref[...] = couple(p, q, scale)
    p_ref[...] = p
    q_ref[...] = q


def normalised(pieces, linv_ref, scale):
    return lax.dot_general(sum(r[...] for r in pieces), linv_ref[...], (((1,), (1,)), ((), ())),
                           precision=HIGH, preferred_element_type=F32) * scale


def next_kernel(*refs):
    linv_ref, scale_ref, other_ref, c_ref, p_ref = refs[4:]
    scale = scale_ref[...]
    p = normalised(refs[:4], linv_ref, scale)
    c_ref[...] = couple(other_ref[...], p, scale)
    p_ref[...] = p


def last_kernel(*refs):
    linv_ref, scale_ref, q_ref = refs[4:]
    q_ref[...] = normalised(refs[:4], linv_ref, scale_ref[...])


def product(a_ref, places, blocks):
    total = 0.0
    for i, block in zip(places, blocks):
        a = a_ref[:, i * 768 : (i + 1) * 768]
        total += sum(
            jnp.dot(a, part, preferred_element_type=F32) for part in reversed(split3(block[...]))
        )
    return total


def early_kernel(a_ref, b0, b1, b2, o_ref):
    o_ref[...] = product(a_ref, (0, 1, 2), (b0, b1, b2))


def late_kernel(a_ref, b3, part_ref, keep_ref, send_ref):
    total = part_ref[...] + product(a_ref, (3,), (b3,))
    keep_ref[...] = total[:128]
    send_ref[...] = total[128:]


def update(factors, blocks):
    part = call(early_kernel, f32s(256, 256), 4, 4 * 3072 << 16, 4 << 20)(factors, *blocks[:3])
    return call(late_kernel, [f32s(128, 256)] * 2, 3, 3 * 3072 << 16, 2 << 20)(
        factors, blocks[3], part
    )


def basis_kernel(pos_ref, top_ref, low_ref, linv_ref, o_ref):
    c = pos_ref[1]
    linv = linv_ref[...]
    for at, r in ((c, top_ref), (1 - c, low_ref)):
        o_ref[pl.ds(pl.multiple_of(at * 128, 128), 128), :] = lax.dot_general(
            r[...], linv, (((1,), (1,)), ((), ())), precision=HIGH, preferred_element_type=F32
        )


def basis_of(pos, top, low, linv):
    return call(basis_kernel, f32s(256, 256), 4, 12 << 24, 1 << 20, smem=1)(
        pos, top, low, linv
    )


def cores_kernel(pos_ref, p_ref, *refs):
    blocks, o_ref = refs[:4], refs[4]
    mask = block_mask(192)
    for i, first in enumerate(ORDER):
        for j, second in enumerate(ORDER):
            source = chunk_at(pos_ref, first, second)
            wide = jnp.where(mask, jnp.concatenate([p_ref[source]] * 12, axis=0), 0.0)
            q = blocks[i][j * 192 : j * 192 + 192, :]
            core = jnp.dot(wide, q, precision=HIGH, preferred_element_type=F32)
            o_ref[pl.ds(source * 12, 12)] = core.reshape(12, 16, 256)


def join_kernel(b0, b1, b2, b3, o_ref):
    for i, b in enumerate((b0, b1, b2, b3)):
        o_ref[i * 192 : (i + 1) * 192, :] = b[...]


def scatter_start(blocks):
    return [blocks[0]] + [send(b, "first", -d) for d, b in zip(ORDER[1:], blocks[1:])]


def scatter_end(arrived):
    parts = [sum(a[i * 192 : i * 192 + 192] for a in arrived) for i in range(RING)]
    return [parts[0]] + [send(p, "second", -d) for d, p in zip(ORDER[1:], parts[1:])]


def gather(value):
    joined = call(join_kernel, f32s(768, 256), 4, 0, 2 << 20)(*exchange(value, "second"))
    return exchange(joined, "first")


def refit(pos, factors, turned, coupling):
    keep, other = update(factors, gather(coupling))
    half = sum(exchange(keep + send(other, "core"), "x"))
    rest = send(half, "core")
    piece = gram(pos, half, rest)
    piece = sum(exchange(piece, "first"))
    arrived = scatter_start(project(turned, half, rest))
    piece = sum(exchange(piece, "second"))
    linv = inverse_factor(pos, piece, send(piece, "core"))
    linv, *arrived = lax.optimization_barrier((linv, *arrived))
    return half, rest, linv, scatter_end(arrived)


def column_scale(ranks):
    positions = jnp.arange(PADDED_RANK, dtype=jnp.int32)
    live = positions[None, :] < ranks[:, None]
    factor = 4.0 / jnp.sqrt(ranks.astype(F32))
    return jnp.where(live, factor[:, None], F32(0.0)).reshape(-1, 1)


def shards(up, down, ranks, left, right):
    adapter, row = lax.axis_index("adapter"), lax.axis_index("row")
    c = adapter % 2
    pos = jnp.stack([adapter // 2, c, row // 4, row % 4]).astype(jnp.int32)
    scale = column_scale(lax.dynamic_slice_in_dim(ranks, row * 12, 12, 0))

    def halves(basis):
        return (
            lax.dynamic_slice_in_dim(basis, c * 128, 128, 0),
            lax.dynamic_slice_in_dim(basis, (1 - c) * 128, 128, 0),
        )

    up_turned = arrange(pos, up)
    left_pieces = scatter_start(project(up_turned, *halves(left)))
    down_turned = arrange(pos, down)
    right_pieces = scatter_start(project(down_turned, *halves(right)))
    left_pieces, right_pieces = scatter_end(left_pieces), scatter_end(right_pieces)
    up, down = up_turned.T, down_turned.T
    side = f32s(192, 256)
    coupling, p, q = call(first_kernel, [side] * 3, 9, 1 << 28, 3 << 20)(
        *left_pieces, *right_pieces, scale
    )

    step = call(next_kernel, [side] * 2, 7, 1 << 29, 3 << 20)
    for sweep in range(ITERS):
        top, low, linv, pieces = refit(pos, up, up_turned, coupling)
        if sweep == ITERS - 1:
            left = basis_of(pos, top, low, linv)
        coupling, p = step(*pieces, linv, scale, q)
        if sweep == ITERS - 1:
            p_rows = lax.all_to_all(p.T.reshape(16, 16, 192), "row", 0, 0)
        top, low, linv, pieces = refit(pos, down, down_turned, coupling)
        if sweep == ITERS - 1:
            right = basis_of(pos, top, low, linv)
            q = call(last_kernel, side, 6, 1 << 28, 2 << 20)(*pieces, linv, scale)
        else:
            coupling, q = step(*pieces, linv, scale, p)
    cores = call(cores_kernel, f32s(192, 16, 256), 6, 1 << 30, 6 << 20, smem=1)(
        pos, p_rows, *gather(q)
    )
    return left, right, cores


def solution(mesh):
    return jax.shard_map(
        shards,
        mesh=mesh,
        in_specs=(
            P("row", "adapter"),
            P("row", "adapter"),
            P("adapter"),
            P("row", None),
            P("row", None),
        ),
        out_specs=(P("row", None), P("row", None), P("adapter", "row", None)),
        check_vma=False,
    )
```

time: 675 us -> 552 us (0.82)
  starting transfers between devices: 285 us -> 138 us
  waiting for transfers between devices: 189 us -> 298 us
  Pallas kernels: 147 us -> 87.8 us
  local copies, waits for them, and re-layouts: 32 us -> 11.1 us
    ppermute x192 -> x114, starting transfers between devices: 282 us -> 133 us  [send(): return lax.ppermute(value, ('adapter', 'row'), perm)]
    ppermute x192 -> x114, waiting for transfers between devices: 186 us -> 289 us  [send(): return lax.ppermute(value, ('adapter', 'row'), perm)]
    pallas_call x24 -> x33, Pallas kernels: 142 us -> 82.4 us  [the longest x4 41.4 us: inverse_factor(): call(inverse_kernel, f32s(K, K), 3, 1 << 33, 1 << 19, [pltpu.VMEM((K, K),...]
    unnamed x100 -> x32, local copies, waits for them, and re-layouts: 20.8 us -> 3.53 us
    all_to_all x1, waiting for transfers between devices: 2.13 us -> 9.54 us  [shards(): p_rows = lax.all_to_all(p.T.reshape(16, 16, 192), 'row', 0, 0)]
  transfers between devices with their start and end apart: 193 -> 115, of which waited for: 70 -> 81; matrix products, arithmetic and copies ran while one was open for 4% -> 2% of each run, Pallas kernels for 18% -> 11%
where the time goes in v2:
time: 552 us; the launch traced here: 544 us
  waiting for transfers between devices  298 us (54%)
  starting transfers between devices  138 us (25%)
  Pallas kernels  87.8 us (16%)
  local copies, waits for them, and re-layouts  11.1 us (2%)
  other arithmetic  6.82 us (1%)
    ppermute x114, waiting for transfers between devices, send(): return lax.ppermute(value, ('adapter', 'row'), perm)  289 us
    ppermute x114, starting transfers between devices, send(): return lax.ppermute(value, ('adapter', 'row'), perm)  133 us
    pallas_call x4, Pallas kernels, inverse_factor(): call(inverse_kernel, f32s(K, K), 3, 1 << 33, 1 << 19, [pltpu.VMEM((K, K),...  41.4 us
  transfers between devices with their start and end apart: 115, of which 81 were waited for; matrix products, arithmetic and copies ran while one was open for 2% of the time, Pallas kernels for 11%

profile of v2, /device:TPU:0, one launch (start us, length us, event | category | flops | bytes accessed | tf_op | source)
XLA Modules:
  0.0 543.7 jit_solution(15221655288283928589)
XLA Ops:
  20.3 9.8 %collective-permute-done.6 = f32[768,256]{1,0:T(8,128)} collective-permute-done((f32[768,256]{1,0:T(8,128)}, f32[768,256]{1,0:T(8,128)}, u32[]{:S(2)}, u32[]{:S(2)}) %collective-permute-start.6) | collective-permute-done | bytes 786464 | tf_op jit(solution)/shard_map/ppermute | solution.py:53
  41.9 7.1 %collective-permute-done = f32[768,256]{1,0:T(8,128)} collective-permute-done((f32[768,256]{1,0:T(8,128)}, f32[768,256]{1,0:T(8,128)}, u32[]{:S(2)}, u32[]{:S(2)}) %collective-permute-start) | collective-permute-done | bytes 786464 | tf_op jit(solution)/shard_map/ppermute | solution.py:53
  49.0 4.0 collective-permute-start.9
  57.3 4.1 collective-permute-start.3
  65.0 5.7 %collective-permute-done.4.refs_2_ = f32[192,256]{1,0:T(8,128)S(1)} collective-permute-done((f32[192,256]{1,0:T(8,128)}, f32[192,256]{1,0:T(8,128)S(1)}, u32[]{:S(2)}, u32[]{:S(2)}) %collective-permute-start.4) | collective-permute-done | bytes 196640 | tf_op jit(solution)/shard_map/ppermute | solution.py:53
  74.9 3.6 collective-permute-done.12.b1
  87.8 17.7 %collective-permute-done.16.b1 = f32[768,256]{1,0:T(8,128)} collective-permute-done((f32[768,256]{1,0:T(8,128)}, f32[768,256]{1,0:T(8,128)}, u32[]{:S(2)}, u32[]{:S(2)}) %collective-permute-start.16) | collective-permute-done | bytes 786464 | tf_op jit(solution)/shard_map/ppermute | solution.py:53
  149.8 10.3 %shard_map.85.refs_4_ = f32[256,256]{1,0:T(8,128)S(1)} custom-call(s32[4]{0:T(128)S(1)} %pad_add_fusion.pos_ref, f32[128,256]{1,0:T(8,128)S(1)} %add_add_fusion.9.mine_ref, f32[128,256]{1,0:T(8,128)S(1)} %collective-permute-done.29.mate_ref), custom_call_target="tpu_custom_call" | custom-call | flops 8589934592 | bytes 524288 | tf_op jit(solution)/shard_map/pallas_call | solution.py:171
  160.2 5.7 %collective-permute-done.30 = f32[768,256]{1,0:T(8,128)S(1)} collective-permute-done((f32[768,256]{1,0:T(8,128)S(1)}, f32[768,256]{1,0:T(8,128)S(1)}, u32[]{:S(2)}, u32[]{:S(2)}) %collective-permute-start.30) | collective-permute-done | bytes 786464 | tf_op jit(solution)/shard_map/ppermute | solution.py:53
  165.8 3.7 collective-permute-done.31
  175.5 4.4 collective-permute-done.34.refs_2_
  185.1 3.6 collective-permute-done.36.b1
  198.4 17.0 %collective-permute-done.40.b1 = f32[768,256]{1,0:T(8,128)} collective-permute-done((f32[768,256]{1,0:T(8,128)}, f32[768,256]{1,0:T(8,128)}, u32[]{:S(2)}, u32[]{:S(2)}) %collective-permute-start.40) | collective-permute-done | bytes 786464 | tf_op jit(solution)/shard_map/ppermute | solution.py:53
  258.8 10.4 %shard_map.92.refs_4_ = f32[256,256]{1,0:T(8,128)S(1)} custom-call(s32[4]{0:T(128)S(1)} %pad_add_fusion.pos_ref, f32[128,256]{1,0:T(8,128)S(1)} %add_add_fusion.6.mine_ref, f32[128,256]{1,0:T(8,128)S(1)} %collective-permute-done.53.mate_ref), custom_call_target="tpu_custom_call" | custom-call | flops 8589934592 | bytes 524288 | tf_op jit(solution)/shard_map/pallas_call | solution.py:171
  269.1 6.0 %collective-permute-done.54 = f32[768,256]{1,0:T(8,128)S(1)} collective-permute-done((f32[768,256]{1,0:T(8,128)S(1)}, f32[768,256]{1,0:T(8,128)S(1)}, u32[]{:S(2)}, u32[]{:S(2)}) %collective-permute-start.54) | collective-permute-done | bytes 786464 | tf_op jit(solution)/shard_map/ppermute | solution.py:53
  275.2 3.7 collective-permute-done.55
  284.8 4.4 collective-permute-done.58.refs_2_
  293.9 3.6 collective-permute-done.60.b1
  305.7 18.4 %collective-permute-done.64.b1 = f32[768,256]{1,0:T(8,128)S(1)} collective-permute-done((f32[768,256]{1,0:T(8,128)S(1)}, f32[768,256]{1,0:T(8,128)S(1)}, u32[]{:S(2)}, u32[]{:S(2)}) %collective-permute-start.64) | collective-permute-done | bytes 786464 | tf_op jit(solution)/shard_map/ppermute | solution.py:53
  365.7 10.3 %shard_map.99.linv_ref.refs_4_ = f32[256,256]{1,0:T(8,128)S(1)} custom-call(s32[4]{0:T(128)S(1)} %pad_add_fusion.pos_ref, f32[128,256]{1,0:T(8,128)S(1)} %add_add_fusion.3.mine_ref, f32[128,256]{1,0:T(8,128)S(1)} %collective-permute-done.77.mate_ref), custom_call_target="tpu_custom_call" | custom-call | flops 8589934592 | bytes 524288 | tf_op jit(solution)/shard_map/pallas_call | solution.py:171
  376.1 6.1 %collective-permute-done.78 = f32[768,256]{1,0:T(8,128)S(1)} collective-permute-done((f32[768,256]{1,0:T(8,128)S(1)}, f32[768,256]{1,0:T(8,128)S(1)}, u32[]{:S(2)}, u32[]{:S(2)}) %collective-permute-start.78) | collective-permute-done | bytes 786464 | tf_op jit(solution)/shard_map/ppermute | solution.py:53
  382.2 3.7 collective-permute-done.79
  391.9 4.4 collective-permute-done.82.refs_2_
  401.0 3.6 collective-permute-done.84.b1
  412.9 18.4 %collective-permute-done.88.b1 = f32[768,256]{1,0:T(8,128)S(1)} collective-permute-done((f32[768,256]{1,0:T(8,128)S(1)}, f32[768,256]{1,0:T(8,128)S(1)}, u32[]{:S(2)}, u32[]{:S(2)}) %collective-permute-start.88) | collective-permute-done | bytes 786464 | tf_op jit(solution)/shard_map/ppermute | solution.py:53
  469.9 10.4 %shard_map.107.linv_ref.refs_4_ = f32[256,256]{1,0:T(8,128)S(1)} custom-call(s32[4]{0:T(128)S(1)} %pad_add_fusion.pos_ref, f32[128,256]{1,0:T(8,128)S(1)} %add_add_fusion.mine_ref, f32[128,256]{1,0:T(8,128)S(1)} %collective-permute-done.101.mate_ref), custom_call_target="tpu_custom_call" | custom-call | flops 8589934592 | bytes 524288 | tf_op jit(solution)/shard_map/pallas_call | solution.py:171
  480.2 5.9 %collective-permute-done.102 = f32[768,256]{1,0:T(8,128)S(1)} collective-permute-done((f32[768,256]{1,0:T(8,128)S(1)}, f32[768,256]{1,0:T(8,128)S(1)}, u32[]{:S(2)}, u32[]{:S(2)}) %collective-permute-start.102) | collective-permute-done | bytes 786464 | tf_op jit(solution)/shard_map/ppermute | solution.py:53
  486.1 3.7 collective-permute-done.103
  495.7 5.1 collective-permute-done.106.refs_2_
  517.3 5.2 all-to-all-start
  528.2 9.5 %all-to-all-done.p_ref = f32[16,16,192]{2,1,0:T(8,128)S(1)} async-done(((f32[16,16,192]{2,1,0:T(8,128)}), f32[16,16,192]{2,1,0:T(8,128)S(1)}, u32[]{:S(2)}, u32[]{:S(2)}) %all-to-all-start) | async-done | bytes 196640 | tf_op jit(solution)/shard_map/all_to_all | solution.py:338
  537.7 5.7 %shard_map.112 = f32[192,16,256]{2,1,0:T(8,128)} custom-call(s32[4]{0:T(128)S(1)} %pad_add_fusion.pos_ref, f32[16,16,192]{2,1,0:T(8,128)S(1)} %all-to-all-done.p_ref, f32[768,256]{1,0:T(8,128)S(1)} %shard_map.111.refs_0_, f32[768,256]{1,0:T(8,128)S(1)} %collective-permute-done.111.refs_1_, f32[768,256]{1,0:T(8,128)S(1)} %collective-permute-done.112.refs_2_, ...), custom_call_target="tpu_custom_call" | custom-call | flops 1073741824 | bytes 6291456 | tf_op jit(solution)/shard_map/pallas_call | solution.py:345
  (299 shorter events, 306.7 us)
Async XLA Ops:
  8.7 21.3 %collective-permute-start.6 = (f32[768,256]{1,0:T(8,128)}, f32[768,256]{1,0:T(8,128)}, u32[]{:S(2)}, u32[]{:S(2)}) collective-permute-start(f32[768,256]{1,0:T(8,128)} %get-tuple-element.68), channel_id=1, source_target_pairs={{0,3},{1,0},{2,1},{3,2},{4,7},{5,4},{6,5},{7,6},{8,11},{9,8},{10,9... | collective-permute-start | bytes 2359304 | tf_op jit(solution)/shard_map/ppermute | solution.py:53
  11.8 21.9 %collective-permute-start.7 = (f32[768,256]{1,0:T(8,128)}, f32[768,256]{1,0:T(8,128)}, u32[]{:S(2)}, u32[]{:S(2)}) collective-permute-start(f32[768,256]{1,0:T(8,128)} %get-tuple-element.69), channel_id=1, source_target_pairs={{0,1},{1,2},{2,3},{3,0},{4,5},{5,6},{6,7},{7,4},{8,9},{9,10},{10,1... | collective-permute-start | bytes 2359304 | tf_op jit(solution)/shard_map/ppermute | solution.py:53
  11.8 21.9 %collective-permute-start.8 = (f32[768,256]{1,0:T(8,128)}, f32[768,256]{1,0:T(8,128)}, u32[]{:S(2)}, u32[]{:S(2)}) collective-permute-start(f32[768,256]{1,0:T(8,128)} %get-tuple-element.70), channel_id=1, source_target_pairs={{0,2},{1,3},{2,0},{3,1},{4,6},{5,7},{6,4},{7,5},{8,10},{9,11},{10,... | collective-permute-start | bytes 2359304 | tf_op jit(solution)/shard_map/ppermute | solution.py:53
  18.2 30.7 %collective-permute-start = (f32[768,256]{1,0:T(8,128)}, f32[768,256]{1,0:T(8,128)}, u32[]{:S(2)}, u32[]{:S(2)}) collective-permute-start(f32[768,256]{1,0:T(8,128)} %get-tuple-element.64), channel_id=1, source_target_pairs={{0,3},{1,0},{2,1},{3,2},{4,7},{5,4},{6,5},{7,6},{8,11},{9,8},{10,9... | collective-permute-start | bytes 2359304 | tf_op jit(solution)/shard_map/ppermute | solution.py:53
  19.3 35.4 %collective-permute-start.1 = (f32[768,256]{1,0:T(8,128)}, f32[768,256]{1,0:T(8,128)}, u32[]{:S(2)}, u32[]{:S(2)}) collective-permute-start(f32[768,256]{1,0:T(8,128)} %get-tuple-element.65), channel_id=1, source_target_pairs={{0,1},{1,2},{2,3},{3,0},{4,5},{5,6},{6,7},{7,4},{8,9},{9,10},{10,1... | collective-permute-start | bytes 2359304 | tf_op jit(solution)/shard_map/ppermute | solution.py:53
  30.0 24.7 %collective-permute-start.2 = (f32[768,256]{1,0:T(8,128)}, f32[768,256]{1,0:T(8,128)}, u32[]{:S(2)}, u32[]{:S(2)}) collective-permute-start(f32[768,256]{1,0:T(8,128)} %get-tuple-element.66), channel_id=1, source_target_pairs={{0,2},{1,3},{2,0},{3,1},{4,6},{5,7},{6,4},{7,5},{8,10},{9,11},{10,... | collective-permute-start | bytes 2359304 | tf_op jit(solution)/shard_map/ppermute | solution.py:53
  36.4 25.1 %collective-permute-start.10 = (f32[192,256]{1,0:T(8,128)S(1)}, f32[192,256]{1,0:T(8,128)S(1)}, u32[]{:S(2)}, u32[]{:S(2)}) collective-permute-start(f32[192,256]{1,0:T(8,128)S(1)} %get-tuple-element.142), channel_id=1, source_target_pairs={{0,4},{1,5},{2,6},{3,7},{4,8},{5,9},{6,10},{7,11},{8,12},{9,13},{1... | collective-permute-start | bytes 589832 | tf_op jit(solution)/shard_map/ppermute | solution.py:53
  38.3 25.2 %collective-permute-start.11 = (f32[192,256]{1,0:T(8,128)}, f32[192,256]{1,0:T(8,128)S(1)}, u32[]{:S(2)}, u32[]{:S(2)}) collective-permute-start(f32[192,256]{1,0:T(8,128)} %get-tuple-element.141), channel_id=1, source_target_pairs={{0,8},{1,9},{2,10},{3,11},{4,12},{5,13},{6,14},{7,15},{8,0},{9,1},... | collective-permute-start | bytes 589832 | tf_op jit(solution)/shard_map/ppermute | solution.py:53
  83.5 21.9 %collective-permute-start.16 = (f32[768,256]{1,0:T(8,128)}, f32[768,256]{1,0:T(8,128)}, u32[]{:S(2)}, u32[]{:S(2)}) collective-permute-start(f32[768,256]{1,0:T(8,128)} %shard_map.81.b0), channel_id=1, source_target_pairs={{0,1},{1,2},{2,3},{3,0},{4,5},{5,6},{6,7},{7,4},{8,9},{9,10},{10,1... | collective-permute-start | bytes 2359304 | tf_op jit(solution)/shard_map/ppermute | solution.py:53
  83.5 21.9 %collective-permute-start.17 = (f32[768,256]{1,0:T(8,128)}, f32[768,256]{1,0:T(8,128)}, u32[]{:S(2)}, u32[]{:S(2)}) collective-permute-start(f32[768,256]{1,0:T(8,128)} %shard_map.81.b0), channel_id=1, source_target_pairs={{0,3},{1,0},{2,1},{3,2},{4,7},{5,4},{6,5},{7,6},{8,11},{9,8},{10,9... | collective-permute-start | bytes 2359304 | tf_op jit(solution)/shard_map/ppermute | solution.py:53
  86.7 21.5 %collective-permute-start.15 = (f32[768,256]{1,0:T(8,128)}, f32[768,256]{1,0:T(8,128)}, u32[]{:S(2)}, u32[]{:S(2)}) collective-permute-start(f32[768,256]{1,0:T(8,128)} %shard_map.81.b0), channel_id=1, source_target_pairs={{0,2},{1,3},{2,0},{3,1},{4,6},{5,7},{6,4},{7,5},{8,10},{9,11},{10,... | collective-permute-start | bytes 2359304 | tf_op jit(solution)/shard_map/ppermute | solution.py:53
  147.9 21.6 %collective-permute-start.31 = (f32[768,256]{1,0:T(8,128)S(1)}, f32[768,256]{1,0:T(8,128)S(1)}, u32[]{:S(2)}, u32[]{:S(2)}) collective-permute-start(f32[768,256]{1,0:T(8,128)S(1)} %get-tuple-element.76), channel_id=1, source_target_pairs={{0,1},{1,2},{2,3},{3,0},{4,5},{5,6},{6,7},{7,4},{8,9},{9,10},{10,1... | collective-permute-start | bytes 2359304 | tf_op jit(solution)/shard_map/ppermute | solution.py:53
  148.0 21.5 %collective-permute-start.32 = (f32[768,256]{1,0:T(8,128)S(1)}, f32[768,256]{1,0:T(8,128)S(1)}, u32[]{:S(2)}, u32[]{:S(2)}) collective-permute-start(f32[768,256]{1,0:T(8,128)S(1)} %get-tuple-element.77), channel_id=1, source_target_pairs={{0,2},{1,3},{2,0},{3,1},{4,6},{5,7},{6,4},{7,5},{8,10},{9,11},{10,... | collective-permute-start | bytes 2359304 | tf_op jit(solution)/shard_map/ppermute | solution.py:53
  193.4 21.9 %collective-permute-start.40 = (f32[768,256]{1,0:T(8,128)}, f32[768,256]{1,0:T(8,128)}, u32[]{:S(2)}, u32[]{:S(2)}) collective-permute-start(f32[768,256]{1,0:T(8,128)} %shard_map.88.b0), channel_id=1, source_target_pairs={{0,1},{1,2},{2,3},{3,0},{4,5},{5,6},{6,7},{7,4},{8,9},{9,10},{10,1... | collective-permute-start | bytes 2359304 | tf_op jit(solution)/shard_map/ppermute | solution.py:53
  193.4 21.9 %collective-permute-start.41 = (f32[768,256]{1,0:T(8,128)}, f32[768,256]{1,0:T(8,128)}, u32[]{:S(2)}, u32[]{:S(2)}) collective-permute-start(f32[768,256]{1,0:T(8,128)} %shard_map.88.b0), channel_id=1, source_target_pairs={{0,3},{1,0},{2,1},{3,2},{4,7},{5,4},{6,5},{7,6},{8,11},{9,8},{10,9... | collective-permute-start | bytes 2359304 | tf_op jit(solution)/shard_map/ppermute | solution.py:53
  196.7 21.5 %collective-permute-start.39 = (f32[768,256]{1,0:T(8,128)}, f32[768,256]{1,0:T(8,128)}, u32[]{:S(2)}, u32[]{:S(2)}) collective-permute-start(f32[768,256]{1,0:T(8,128)} %shard_map.88.b0), channel_id=1, source_target_pairs={{0,2},{1,3},{2,0},{3,1},{4,6},{5,7},{6,4},{7,5},{8,10},{9,11},{10,... | collective-permute-start | bytes 2359304 | tf_op jit(solution)/shard_map/ppermute | solution.py:53
  257.2 21.6 %collective-permute-start.55 = (f32[768,256]{1,0:T(8,128)S(1)}, f32[768,256]{1,0:T(8,128)S(1)}, u32[]{:S(2)}, u32[]{:S(2)}) collective-permute-start(f32[768,256]{1,0:T(8,128)S(1)} %get-tuple-element.89), channel_id=1, source_target_pairs={{0,1},{1,2},{2,3},{3,0},{4,5},{5,6},{6,7},{7,4},{8,9},{9,10},{10,1... | collective-permute-start | bytes 2359304 | tf_op jit(solution)/shard_map/ppermute | solution.py:53
  257.3 21.5 %collective-permute-start.56 = (f32[768,256]{1,0:T(8,128)S(1)}, f32[768,256]{1,0:T(8,128)S(1)}, u32[]{:S(2)}, u32[]{:S(2)}) collective-permute-start(f32[768,256]{1,0:T(8,128)S(1)} %get-tuple-element.90), channel_id=1, source_target_pairs={{0,2},{1,3},{2,0},{3,1},{4,6},{5,7},{6,4},{7,5},{8,10},{9,11},{10,... | collective-permute-start | bytes 2359304 | tf_op jit(solution)/shard_map/ppermute | solution.py:53
  302.4 21.7 %collective-permute-start.64 = (f32[768,256]{1,0:T(8,128)S(1)}, f32[768,256]{1,0:T(8,128)S(1)}, u32[]{:S(2)}, u32[]{:S(2)}) collective-permute-start(f32[768,256]{1,0:T(8,128)S(1)} %shard_map.95.b0), channel_id=1, source_target_pairs={{0,1},{1,2},{2,3},{3,0},{4,5},{5,6},{6,7},{7,4},{8,9},{9,10},{10,1... | collective-permute-start | bytes 2359304 | tf_op jit(solution)/shard_map/ppermute | solution.py:53
  302.5 21.6 %collective-permute-start.65 = (f32[768,256]{1,0:T(8,128)S(1)}, f32[768,256]{1,0:T(8,128)S(1)}, u32[]{:S(2)}, u32[]{:S(2)}) collective-permute-start(f32[768,256]{1,0:T(8,128)S(1)} %shard_map.95.b0), channel_id=1, source_target_pairs={{0,3},{1,0},{2,1},{3,2},{4,7},{5,4},{6,5},{7,6},{8,11},{9,8},{10,9... | collective-permute-start | bytes 2359304 | tf_op jit(solution)/shard_map/ppermute | solution.py:53
  362.2 20.0 %collective-permute-start.78 = (f32[768,256]{1,0:T(8,128)S(1)}, f32[768,256]{1,0:T(8,128)S(1)}, u32[]{:S(2)}, u32[]{:S(2)}) collective-permute-start(f32[768,256]{1,0:T(8,128)S(1)} %get-tuple-element.101), channel_id=1, source_target_pairs={{0,3},{1,0},{2,1},{3,2},{4,7},{5,4},{6,5},{7,6},{8,11},{9,8},{10,9... | collective-permute-start | bytes 2359304 | tf_op jit(solution)/shard_map/ppermute | solution.py:53
  364.2 21.6 %collective-permute-start.79 = (f32[768,256]{1,0:T(8,128)S(1)}, f32[768,256]{1,0:T(8,128)S(1)}, u32[]{:S(2)}, u32[]{:S(2)}) collective-permute-start(f32[768,256]{1,0:T(8,128)S(1)} %get-tuple-element.102), channel_id=1, source_target_pairs={{0,1},{1,2},{2,3},{3,0},{4,5},{5,6},{6,7},{7,4},{8,9},{9,10},{10,1... | collective-permute-start | bytes 2359304 | tf_op jit(solution)/shard_map/ppermute | solution.py:53
  364.3 21.6 %collective-permute-start.80 = (f32[768,256]{1,0:T(8,128)S(1)}, f32[768,256]{1,0:T(8,128)S(1)}, u32[]{:S(2)}, u32[]{:S(2)}) collective-permute-start(f32[768,256]{1,0:T(8,128)S(1)} %get-tuple-element.103), channel_id=1, source_target_pairs={{0,2},{1,3},{2,0},{3,1},{4,6},{5,7},{6,4},{7,5},{8,10},{9,11},{10,... | collective-permute-start | bytes 2359304 | tf_op jit(solution)/shard_map/ppermute | solution.py:53
  409.6 21.7 %collective-permute-start.88 = (f32[768,256]{1,0:T(8,128)S(1)}, f32[768,256]{1,0:T(8,128)S(1)}, u32[]{:S(2)}, u32[]{:S(2)}) collective-permute-start(f32[768,256]{1,0:T(8,128)S(1)} %shard_map.103.b0), channel_id=1, source_target_pairs={{0,1},{1,2},{2,3},{3,0},{4,5},{5,6},{6,7},{7,4},{8,9},{9,10},{10,1... | collective-permute-start | bytes 2359304 | tf_op jit(solution)/shard_map/ppermute | solution.py:53
  409.6 21.6 %collective-permute-start.89 = (f32[768,256]{1,0:T(8,128)S(1)}, f32[768,256]{1,0:T(8,128)S(1)}, u32[]{:S(2)}, u32[]{:S(2)}) collective-permute-start(f32[768,256]{1,0:T(8,128)S(1)} %shard_map.103.b0), channel_id=1, source_target_pairs={{0,3},{1,0},{2,1},{3,2},{4,7},{5,4},{6,5},{7,6},{8,11},{9,8},{10,9... | collective-permute-start | bytes 2359304 | tf_op jit(solution)/shard_map/ppermute | solution.py:53
  466.1 20.0 %collective-permute-start.102 = (f32[768,256]{1,0:T(8,128)S(1)}, f32[768,256]{1,0:T(8,128)S(1)}, u32[]{:S(2)}, u32[]{:S(2)}) collective-permute-start(f32[768,256]{1,0:T(8,128)S(1)} %get-tuple-element.114), channel_id=1, source_target_pairs={{0,3},{1,0},{2,1},{3,2},{4,7},{5,4},{6,5},{7,6},{8,11},{9,8},{10,9... | collective-permute-start | bytes 2359304 | tf_op jit(solution)/shard_map/ppermute | solution.py:53
  468.1 21.6 %collective-permute-start.103 = (f32[768,256]{1,0:T(8,128)S(1)}, f32[768,256]{1,0:T(8,128)S(1)}, u32[]{:S(2)}, u32[]{:S(2)}) collective-permute-start(f32[768,256]{1,0:T(8,128)S(1)} %get-tuple-element.115), channel_id=1, source_target_pairs={{0,1},{1,2},{2,3},{3,0},{4,5},{5,6},{6,7},{7,4},{8,9},{9,10},{10,1... | collective-permute-start | bytes 2359304 | tf_op jit(solution)/shard_map/ppermute | solution.py:53
  468.2 21.5 %collective-permute-start.104 = (f32[768,256]{1,0:T(8,128)S(1)}, f32[768,256]{1,0:T(8,128)S(1)}, u32[]{:S(2)}, u32[]{:S(2)}) collective-permute-start(f32[768,256]{1,0:T(8,128)S(1)} %get-tuple-element.116), channel_id=1, source_target_pairs={{0,2},{1,3},{2,0},{3,1},{4,6},{5,7},{6,4},{7,5},{8,10},{9,11},{10,... | collective-permute-start | bytes 2359304 | tf_op jit(solution)/shard_map/ppermute | solution.py:53
  513.2 24.5 %collective-permute-start.111 = (f32[768,256]{1,0:T(8,128)S(1)}, f32[768,256]{1,0:T(8,128)S(1)}, u32[]{:S(2)}, u32[]{:S(2)}) collective-permute-start(f32[768,256]{1,0:T(8,128)S(1)} %shard_map.111.refs_0_), channel_id=1, source_target_pairs={{0,1},{1,2},{2,3},{3,0},{4,5},{5,6},{6,7},{7,4},{8,9},{9,10},{10,1... | collective-permute-start | bytes 2359304 | tf_op jit(solution)/shard_map/ppermute | solution.py:53
  513.3 24.4 %collective-permute-start.112 = (f32[768,256]{1,0:T(8,128)S(1)}, f32[768,256]{1,0:T(8,128)S(1)}, u32[]{:S(2)}, u32[]{:S(2)}) collective-permute-start(f32[768,256]{1,0:T(8,128)S(1)} %shard_map.111.refs_0_), channel_id=1, source_target_pairs={{0,3},{1,0},{2,1},{3,2},{4,7},{5,4},{6,5},{7,6},{8,11},{9,8},{10,9... | collective-permute-start | bytes 2359304 | tf_op jit(solution)/shard_map/ppermute | solution.py:53
  516.5 21.2 %collective-permute-start.113 = (f32[768,256]{1,0:T(8,128)S(1)}, f32[768,256]{1,0:T(8,128)}, u32[]{:S(2)}, u32[]{:S(2)}) collective-permute-start(f32[768,256]{1,0:T(8,128)S(1)} %shard_map.111.refs_0_), channel_id=1, source_target_pairs={{0,2},{1,3},{2,0},{3,1},{4,6},{5,7},{6,4},{7,5},{8,10},{9,11},{10,... | collective-permute-start | bytes 2359304 | tf_op jit(solution)/shard_map/ppermute | solution.py:53
  517.3 20.4 %all-to-all-start = ((f32[16,16,192]{2,1,0:T(8,128)}), f32[16,16,192]{2,1,0:T(8,128)S(1)}, u32[]{:S(2)}, u32[]{:S(2)}) async-start(f32[16,16,192]{2,1,0:T(8,128)} %bitcast.25), calls=%async_computation | async-start | bytes 524288 | tf_op jit(solution)/shard_map/all_to_all | solution.py:338
  (99 other events, 927.8 us)

commit v3 on v2

--- a/solution.py
+++ b/solution.py
@@ -1,3 +1,5 @@
+import functools
+
 import jax
 import jax.numpy as jnp
 from jax import lax
@@ -16,7 +18,7 @@
 BF16 = jnp.bfloat16
 VMEM = pl.BlockSpec(memory_space=pltpu.VMEM)
 SMEM = pl.BlockSpec(memory_space=pltpu.SMEM)
-PARAMS = pltpu.CompilerParams(vmem_limit_bytes=32 * 1024 * 1024)
+PARAMS = pltpu.CompilerParams(vmem_limit_bytes=20 * 1024 * 1024)
 
 
 def call(kernel, outs, n_in, flops, nbytes, scratch=(), smem=0):
@@ -38,9 +40,9 @@
 def moved(axis, d, x, c, z, y):
     if axis == "core":
         return x, 1 - c, z, y
-    if axis == "x":
+    if axis[c] == "x":
         return (x + d) % RING, c, z, y
-    if (axis == "first") == (c == 0):
+    if axis[c] == "y":
         return x, c, z, (y + d) % RING
     return x, c, (z + d) % RING, y
 
@@ -54,14 +56,31 @@
 
 
 def exchange(value, axis):
-    return [value] + [send(value, axis, d) for d in (1, 3, 2)]
+    return [value] + [send(value, axis, d) for d in ORDER[1:]]
+
+
+def deliver(values, axis, sign=-1):
+    return [values[0]] + [send(v, axis, sign * d) for d, v in zip(ORDER[1:], values[1:])]
+
+
+def back(place, d):
+    return lax.rem(place + RING - d, RING)
 
 
 def chunk_at(pos_ref, first, second):
     c, z, y = pos_ref[1], pos_ref[2], pos_ref[3]
     dy = jnp.where(c == 0, first, second)
     dz = jnp.where(c == 0, second, first)
-    return lax.rem(z + RING - dz, RING) * RING + lax.rem(y + RING - dy, RING)
+    return back(z, dz) * RING + back(y, dy)
+
+
+LEFT, RIGHT = "y", "z"
+PLACE = {"z": 2, "y": 3}
+CROSS = {"y": "z", "z": "y"}
+
+
+def block_place(pos_ref, place):
+    return lax.bitwise_xor(place // 2, pos_ref[1]) * 2 + lax.rem(place, 2)
 
 
 def split3(value):
@@ -71,33 +90,57 @@
     return high, mid, (rest - mid.astype(F32)).astype(BF16)
 
 
-def arrange_kernel(pos_ref, a_ref, o_ref):
-    for i, first in enumerate(ORDER):
-        for j, second in enumerate(ORDER):
-            block = a_ref[chunk_at(pos_ref, first, second)]
-            swapped = jnp.concatenate([block[:, 128:], block[:, :128]], axis=1)
-            at = (i * 4 + j) * 192
-            o_ref[at : at + 192, :] = jnp.where(pos_ref[1] == 0, block, swapped)
-
-
-def arrange(pos, factors):
-    return call(
-        arrange_kernel, jax.ShapeDtypeStruct((3072, 256), BF16), 2, 0, 3 << 20, smem=1
-    )(pos, factors.T.reshape(16, 192, 256))
-
-
-def project_kernel(a_ref, top_ref, low_ref, *o_refs):
-    parts = split3(jnp.concatenate([top_ref[...], low_ref[...]], axis=0))
-    for i, o_ref in enumerate(o_refs):
-        block = a_ref[i * 768 : (i + 1) * 768, :]
+def pieces_kernel(side, pos_ref, a_ref, *o_refs):
+    at, cross = pos_ref[PLACE[side]], pos_ref[PLACE[CROSS[side]]]
+    for o_ref, d in zip(o_refs, ORDER):
+        mine = lax.rem(at + d, RING)
+        for j, e in enumerate(ORDER):
+            theirs = back(cross, e)
+            source = theirs * RING + mine if side == "y" else mine * RING + theirs
+            o_ref[j * 192 : j * 192 + 192, :] = a_ref[source].astype(F32)
+
+
+def turned_kernel(side, pos_ref, *refs):
+    for r, d in zip(refs[:-1], ORDER):
+        refs[-1][block_place(pos_ref, back(pos_ref[PLACE[side]], d))] = r[...].astype(BF16)
+
+
+def lay_out(side, pos, factors):
+    pieces = call(functools.partial(pieces_kernel, side), [f32s(768, 256)] * 4, 2, 0, 5 << 20,
+                  smem=1)(pos, factors.T.reshape(16, 192, 256))
+    return call(functools.partial(turned_kernel, side), jax.ShapeDtypeStruct((4, 768, 256), BF16),
+                5, 0, 5 << 20, smem=1)(pos, *deliver(pieces, side * 2, 1))
+
+
+def spread_kernel(side, pos_ref, mine_ref, mate_ref, o_ref):
+    for i, d in enumerate(ORDER):
+        p = block_place(pos_ref, back(pos_ref[PLACE[side]], d))
+        for c, ref in ((pos_ref[1], mine_ref), (1 - pos_ref[1], mate_ref)):
+            at = pl.multiple_of(p * 256 + c * 128, 128)
+            o_ref[pl.ds(at, 128), :] = ref[i * 128 : i * 128 + 128, :]
+
+
+def spread(side, pos, basis):
+    half = lax.dynamic_slice_in_dim(basis, pos[1] * 128, 128, 0)
+    mine = jnp.concatenate(exchange(half, side * 2), axis=0)
+    return call(functools.partial(spread_kernel, side), f32s(1024, 256), 3, 0, 2 << 20, smem=1)(
+        pos, mine, send(mine, "core")
+    )
+
+
+def project_kernel(a_ref, *refs):
+    sources, o_refs = refs[:-4], refs[-4:]
+    parts = split3(jnp.concatenate([r[...] for r in sources], axis=0))
+    for j, o_ref in enumerate(o_refs):
+        block = jnp.concatenate([a_ref[p, j * 192 : j * 192 + 192, :] for p in range(4)], axis=1)
         o_ref[...] = sum(
             jnp.dot(block, part, preferred_element_type=F32) for part in reversed(parts)
         )
 
 
-def project(turned, top, low):
-    return call(project_kernel, [f32s(768, 256)] * 4, 3, 6 * 3072 << 16, 5 << 20)(
-        turned, top, low
+def project(turned, *sources):
+    return call(project_kernel, [f32s(192, 256)] * 4, 1 + len(sources), 6 * 3072 << 16, 4 << 20)(
+        turned, *sources
     )
 
 
@@ -168,7 +211,7 @@
 
 
 def inverse_factor(pos, mine, mate):
-    return call(inverse_kernel, f32s(K, K), 3, 1 << 33, 1 << 19,
+    return call(inverse_kernel, f32s(K, K), 3, 0, 1 << 10,
                 [pltpu.VMEM((K, K), F32)], smem=1)(pos, mine, mate)
 
 
@@ -212,46 +255,70 @@
     q_ref[...] = normalised(refs[:4], linv_ref, scale_ref[...])
 
 
-def product(a_ref, places, blocks):
-    total = 0.0
-    for i, block in zip(places, blocks):
-        a = a_ref[:, i * 768 : (i + 1) * 768]
-        total += sum(
-            jnp.dot(a, part, preferred_element_type=F32) for part in reversed(split3(block[...]))
-        )
-    return total
-
-
-def early_kernel(a_ref, b0, b1, b2, o_ref):
-    o_ref[...] = product(a_ref, (0, 1, 2), (b0, b1, b2))
-
-
-def late_kernel(a_ref, b3, part_ref, keep_ref, send_ref):
-    total = part_ref[...] + product(a_ref, (3,), (b3,))
-    keep_ref[...] = total[:128]
-    send_ref[...] = total[128:]
+def product(factors, blocks):
+    return sum(
+        jnp.dot(a[...], part, preferred_element_type=F32)
+        for a, block in zip(factors, blocks)
+        for part in reversed(split3(block[...]))
+    )
+
+
+def early_kernel(a0, a1, a2, b0, b1, b2, o_ref):
+    o_ref[...] = product((a0, a1, a2), (b0, b1, b2))
+
+
+def late_kernel(a3, b3, part_ref, keep_ref, send_ref):
+    total = part_ref[...] + product((a3,), (b3,))
+    keep_ref[...] = total[:512]
+    send_ref[...] = total[512:]
 
 
 def update(factors, blocks):
-    part = call(early_kernel, f32s(256, 256), 4, 4 * 3072 << 16, 4 << 20)(factors, *blocks[:3])
-    return call(late_kernel, [f32s(128, 256)] * 2, 3, 3 * 3072 << 16, 2 << 20)(
-        factors, blocks[3], part
-    )
-
-
-def basis_kernel(pos_ref, top_ref, low_ref, linv_ref, o_ref):
-    c = pos_ref[1]
-    linv = linv_ref[...]
-    for at, r in ((c, top_ref), (1 - c, low_ref)):
-        o_ref[pl.ds(pl.multiple_of(at * 128, 128), 128), :] = lax.dot_general(
-            r[...], linv, (((1,), (1,)), ((), ())), precision=HIGH, preferred_element_type=F32
-        )
-
-
-def basis_of(pos, top, low, linv):
-    return call(basis_kernel, f32s(256, 256), 4, 12 << 24, 1 << 20, smem=1)(
-        pos, top, low, linv
-    )
+    part = call(early_kernel, f32s(1024, 256), 6, 4 * 3072 << 16, 3 << 20)(
+        *factors[:3], *blocks[:3]
+    )
+    return call(late_kernel, [f32s(512, 256)] * 2, 3, 2 * 3072 << 16, 2 << 20)(
+        factors[3], blocks[3], part
+    )
+
+
+def first_place(side, pos_ref):
+    return jnp.where(pos_ref[1] == 0, pos_ref[0], pos_ref[PLACE[side]])
+
+
+def split_kernel(side, pos_ref, keep_ref, other_ref, *o_refs):
+    for o_ref, d in zip(o_refs, ORDER):
+        at = pl.multiple_of(back(first_place(side, pos_ref), d) * 128, 128)
+        o_ref[...] = keep_ref[pl.ds(at, 128), :] + other_ref[pl.ds(at, 128), :]
+
+
+def merge_kernel(side, pos_ref, *refs):
+    for r, d in zip(refs[:-1], ORDER):
+        at = pl.multiple_of(back(first_place(side, pos_ref), d) * 128, 128)
+        refs[-1][pl.ds(at, 128), :] = r[...]
+
+
+def add_up(side, pos, keep, other):
+    chunks = call(functools.partial(split_kernel, side), [f32s(128, 256)] * 4, 3, 0, 2 << 20,
+                  smem=1)(pos, keep, send(other, "core"))
+    chunk = sum(deliver(chunks, "x" + side))
+    chunk = sum(exchange(chunk, side + "x"))
+    return call(functools.partial(merge_kernel, side), f32s(512, 256), 5, 0, 1 << 20, smem=1)(
+        pos, *exchange(chunk, "x" + side)
+    )
+
+
+def basis_kernel(side, pos_ref, top_ref, low_ref, linv_ref, o_ref):
+    p = block_place(pos_ref, pos_ref[PLACE[side]])
+    at = pl.ds(pl.multiple_of(lax.rem(p, 2) * 256, 256), 256)
+    rows = jnp.where(p < 2, top_ref[at, :], low_ref[at, :])
+    o_ref[...] = lax.dot_general(rows, linv_ref[...], (((1,), (1,)), ((), ())), precision=HIGH,
+                                 preferred_element_type=F32)
+
+
+def basis_of(side, pos, top, low, linv):
+    return call(functools.partial(basis_kernel, side), f32s(256, 256), 4, 12 << 24, 1 << 20,
+                smem=1)(pos, top, low, linv)
 
 
 def cores_kernel(pos_ref, p_ref, *refs):
@@ -271,31 +338,18 @@
         o_ref[i * 192 : (i + 1) * 192, :] = b[...]
 
 
-def scatter_start(blocks):
-    return [blocks[0]] + [send(b, "first", -d) for d, b in zip(ORDER[1:], blocks[1:])]
-
-
-def scatter_end(arrived):
-    parts = [sum(a[i * 192 : i * 192 + 192] for a in arrived) for i in range(RING)]
-    return [parts[0]] + [send(p, "second", -d) for d, p in zip(ORDER[1:], parts[1:])]
-
-
-def gather(value):
-    joined = call(join_kernel, f32s(768, 256), 4, 0, 2 << 20)(*exchange(value, "second"))
-    return exchange(joined, "first")
-
-
-def refit(pos, factors, turned, coupling):
-    keep, other = update(factors, gather(coupling))
-    half = sum(exchange(keep + send(other, "core"), "x"))
+def gather_all(value):
+    joined = call(join_kernel, f32s(768, 256), 4, 0, 2 << 20)(*exchange(value, "zy"))
+    return exchange(joined, "yz")
+
+
+def refit(side, pos, factors, turned, coupling):
+    cross = CROSS[side] * 2
+    half = add_up(side, pos, *update(factors, exchange(coupling, cross)))
     rest = send(half, "core")
-    piece = gram(pos, half, rest)
-    piece = sum(exchange(piece, "first"))
-    arrived = scatter_start(project(turned, half, rest))
-    piece = sum(exchange(piece, "second"))
-    linv = inverse_factor(pos, piece, send(piece, "core"))
-    linv, *arrived = lax.optimization_barrier((linv, *arrived))
-    return half, rest, linv, scatter_end(arrived)
+    piece = sum(exchange(gram(pos, half, rest), cross))
+    pieces = deliver(project(turned, half, rest), cross)
+    return half, rest, inverse_factor(pos, piece, send(piece, "core")), pieces
 
 
 def column_scale(ranks):
@@ -311,18 +365,17 @@
     pos = jnp.stack([adapter // 2, c, row // 4, row % 4]).astype(jnp.int32)
     scale = column_scale(lax.dynamic_slice_in_dim(ranks, row * 12, 12, 0))
 
-    def halves(basis):
-        return (
-            lax.dynamic_slice_in_dim(basis, c * 128, 128, 0),
-            lax.dynamic_slice_in_dim(basis, (1 - c) * 128, 128, 0),
-        )
-
-    up_turned = arrange(pos, up)
-    left_pieces = scatter_start(project(up_turned, *halves(left)))
-    down_turned = arrange(pos, down)
-    right_pieces = scatter_start(project(down_turned, *halves(right)))
-    left_pieces, right_pieces = scatter_end(left_pieces), scatter_end(right_pieces)
-    up, down = up_turned.T, down_turned.T
+    left_rows, right_rows = spread(LEFT, pos, left), spread(RIGHT, pos, right)
+    up_turned, down_turned = lay_out(LEFT, pos, up), lay_out(RIGHT, pos, down)
+    left_pieces = deliver(project(up_turned, left_rows), CROSS[LEFT] * 2)
+    right_pieces = deliver(project(down_turned, right_rows), CROSS[RIGHT] * 2)
+    up, down = (
+        [
+            turned[:, j * 192 : j * 192 + 192].transpose(0, 2, 1).reshape(1024, 192)
+            for j in range(4)
+        ]
+        for turned in (up_turned, down_turned)
+    )
     side = f32s(192, 256)
     coupling, p, q = call(first_kernel, [side] * 3, 9, 1 << 28, 3 << 20)(
         *left_pieces, *right_pieces, scale
@@ -330,20 +383,20 @@
 
     step = call(next_kernel, [side] * 2, 7, 1 << 29, 3 << 20)
     for sweep in range(ITERS):
-        top, low, linv, pieces = refit(pos, up, up_turned, coupling)
+        top, low, linv, pieces = refit(LEFT, pos, up, up_turned, coupling)
         if sweep == ITERS - 1:
-            left = basis_of(pos, top, low, linv)
+            left = basis_of(LEFT, pos, top, low, linv)
         coupling, p = step(*pieces, linv, scale, q)
         if sweep == ITERS - 1:
             p_rows = lax.all_to_all(p.T.reshape(16, 16, 192), "row", 0, 0)
-        top, low, linv, pieces = refit(pos, down, down_turned, coupling)
+        top, low, linv, pieces = refit(RIGHT, pos, down, down_turned, coupling)
         if sweep == ITERS - 1:
-            right = basis_of(pos, top, low, linv)
+            right = basis_of(RIGHT, pos, top, low, linv)
             q = call(last_kernel, side, 6, 1 << 28, 2 << 20)(*pieces, linv, scale)
         else:
             coupling, q = step(*pieces, linv, scale, p)
     cores = call(cores_kernel, f32s(192, 16, 256), 6, 1 << 30, 6 << 20, smem=1)(
-        pos, p_rows, *gather(q)
+        pos, p_rows, *gather_all(q)
     )
     return left, right, cores
 

time: 552 us -> 489 us (0.89)
  waiting for transfers between devices: 298 us -> 182 us
  local copies, waits for them, and re-layouts: 11.1 us -> 37.6 us
  starting transfers between devices: 138 us -> 155 us
  Pallas kernels: 87.8 us -> 100 us
    ppermute x114 -> x110, waiting for transfers between devices: 289 us -> 171 us  [send(): return lax.ppermute(value, ('adapter', 'row'), perm)]
    transpose x2 -> x12, local copies, waits for them, and re-layouts: 2.4 us -> 21.8 us  [the longest x10 18.4 us: shards(): turned[:, j * 192:j * 192 + 192].transpose(0, 2, 1).reshape(1024, 192)]
    ppermute x114 -> x110, starting transfers between devices: 133 us -> 149 us  [send(): return lax.ppermute(value, ('adapter', 'row'), perm)]
    unnamed x32 -> x82, local copies, waits for them, and re-layouts: 3.53 us -> 12.3 us
    pallas_call x27 -> x35, Pallas kernels: 72.1 us -> 79.4 us  [the longest x4 41.4 us: inverse_factor(): call(inverse_kernel, f32s(K, K), 3, 0, 1 << 10, [pltpu.VMEM((K, K), F32)]...]
    add x22 -> x12, other arithmetic: 6.59 us -> 0.42 us  [the longest x4 0.15 us: refit(): piece = sum(exchange(gram(pos, half, rest), cross))]
  transfers between devices with their start and end apart: 115 -> 111, of which waited for: 81 -> 57; matrix products, arithmetic and copies ran while one was open for 2% -> 5% of each run, Pallas kernels for 11% -> 15%
where the time goes in v3:
time: 489 us; the launch traced here: 479 us
  waiting for transfers between devices  182 us (37%)
  starting transfers between devices  155 us (32%)
  Pallas kernels  100 us (20%)
  local copies, waits for them, and re-layouts  37.6 us (8%)
    ppermute x110, waiting for transfers between devices, send(): return lax.ppermute(value, ('adapter', 'row'), perm)  171 us
    ppermute x110, starting transfers between devices, send(): return lax.ppermute(value, ('adapter', 'row'), perm)  149 us
    pallas_call x4, Pallas kernels, inverse_factor(): call(inverse_kernel, f32s(K, K), 3, 0, 1 << 10, [pltpu.VMEM((K, K), F32)]...  41.4 us
    transpose x10, local copies, waits for them, and re-layouts, shards(): turned[:, j * 192:j * 192 + 192].transpose(0, 2, 1).reshape(1024, 192)  18.4 us
    unnamed x82, local copies, waits for them, and re-layouts  12.3 us
    all_to_all x1, waiting for transfers between devices, shards(): p_rows = lax.all_to_all(p.T.reshape(16, 16, 192), 'row', 0, 0)  11.5 us
    pallas_call x6, Pallas kernels, project(): call(project_kernel, [f32s(192, 256)] * 4, 1 + len(sources), 6 * 3072 <<...  9.84 us
  transfers between devices with their start and end apart: 111, of which 57 were waited for; matrix products, arithmetic and copies ran while one was open for 5% of the time, Pallas kernels for 15%

profile of v3, /device:TPU:0, one launch (start us, length us, event | category | flops | bytes accessed | tf_op | source)
XLA Modules:
  0.0 478.9 jit_solution(8312354135709755021)
XLA Ops:
  13.7 16.0 %collective-permute-done.13 = f32[128,256]{1,0:T(8,128)S(1)} collective-permute-done((f32[128,256]{1,0:T(8,128)S(1)}, f32[128,256]{1,0:T(8,128)S(1)}, u32[]{:S(2)}, u32[]{:S(2)}) %collective-permute-start.13) | collective-permute-done | bytes 131104 | tf_op jit(solution)/shard_map/ppermute | solution.py:55
  29.7 4.0 collective-permute-done.15
  38.6 4.1 collective-permute-done.6
  58.1 5.7 %collective-permute-done.5.refs_3_ = f32[768,256]{1,0:T(8,128)} collective-permute-done((f32[768,256]{1,0:T(8,128)}, f32[768,256]{1,0:T(8,128)}, u32[]{:S(2)}, u32[]{:S(2)}) %collective-permute-start.5) | collective-permute-done | bytes 786464 | tf_op jit(solution)/shard_map/ppermute | solution.py:55
  73.1 16.6 %collective-permute-done.1.refs_2_ = f32[768,256]{1,0:T(8,128)} collective-permute-done((f32[768,256]{1,0:T(8,128)}, f32[768,256]{1,0:T(8,128)}, u32[]{:S(2)}, u32[]{:S(2)}) %collective-permute-start.1) | collective-permute-done | bytes 786464 | tf_op jit(solution)/shard_map/ppermute | solution.py:55
  97.1 3.4 collective-permute-start.12
  102.5 3.3 collective-permute-done.12.refs_3_
  110.6 3.5 collective-permute-start.22
  138.8 5.1 %collective-permute-done.25 = f32[128,256]{1,0:T(8,128)S(1)} collective-permute-done((f32[128,256]{1,0:T(8,128)S(1)}, f32[128,256]{1,0:T(8,128)S(1)}, u32[]{:S(2)}, u32[]{:S(2)}) %collective-permute-start.25) | collective-permute-done | bytes 131104 | tf_op jit(solution)/shard_map/ppermute | solution.py:55
  144.7 4.6 collective-permute-start.28
  152.2 3.6 collective-permute-done.29
  155.9 3.2 collective-permute-start.31
  162.1 3.5 collective-permute-done.32.refs_3_
  170.1 3.2 collective-permute-start.38
  180.4 12.8 %collective-permute-start.40 = (f32[128,256]{1,0:T(8,128)S(1)}, f32[128,256]{1,0:T(8,128)S(1)}, u32[]{:S(2)}, u32[]{:S(2)}) collective-permute-start(f32[128,256]{1,0:T(8,128)S(1)} %add_add_fusion.9.mine_ref), channel_id=1, source_target_pairs={{0,16},{1,17},{2,18},{3,19},{4,20},{5,21},{6,22},{7,23},{8,24},{9,... | collective-permute-start | bytes 393224 | tf_op jit(solution)/shard_map/ppermute | solution.py:55
  194.5 10.4 %shard_map.91.refs_4_ = f32[256,256]{1,0:T(8,128)S(1)} custom-call(s32[4]{0:T(128)S(1)} %pad_add_fusion.pos_ref, f32[128,256]{1,0:T(8,128)S(1)} %add_add_fusion.9.mine_ref, f32[128,256]{1,0:T(8,128)S(1)} %collective-permute-done.40.mate_ref), custom_call_target="tpu_custom_call" | custom-call | bytes 1024 | tf_op jit(solution)/shard_map/pallas_call | solution.py:214
  233.8 3.7 collective-permute-done.46
  243.8 3.5 collective-permute-done.50
  253.7 3.5 collective-permute-done.53.refs_3_
  274.4 10.3 %shard_map.99.refs_4_ = f32[256,256]{1,0:T(8,128)S(1)} custom-call(s32[4]{0:T(128)S(1)} %pad_add_fusion.pos_ref, f32[128,256]{1,0:T(8,128)S(1)} %add_add_fusion.6.mine_ref, f32[128,256]{1,0:T(8,128)S(1)} %collective-permute-done.61.mate_ref), custom_call_target="tpu_custom_call" | custom-call | bytes 1024 | tf_op jit(solution)/shard_map/pallas_call | solution.py:214
  289.6 5.4 %collective-permute-done.63.b1 = f32[192,256]{1,0:T(8,128)S(1)} collective-permute-done((f32[192,256]{1,0:T(8,128)S(1)}, f32[192,256]{1,0:T(8,128)S(1)}, u32[]{:S(2)}, u32[]{:S(2)}) %collective-permute-start.63) | collective-permute-done | bytes 196640 | tf_op jit(solution)/shard_map/ppermute | solution.py:55
  307.5 3.7 collective-permute-done.67
  327.8 3.5 collective-permute-done.74.refs_3_
  349.5 10.3 %shard_map.106.linv_ref.refs_4_ = f32[256,256]{1,0:T(8,128)S(1)} custom-call(s32[4]{0:T(128)S(1)} %pad_add_fusion.pos_ref, f32[128,256]{1,0:T(8,128)S(1)} %add_add_fusion.3.mine_ref, f32[128,256]{1,0:T(8,128)S(1)} %collective-permute-done.79.mate_ref), custom_call_target="tpu_custom_call" | custom-call | bytes 1024 | tf_op jit(solution)/shard_map/pallas_call | solution.py:214
  364.6 9.1 %collective-permute-done.84.b1 = f32[192,256]{1,0:T(8,128)S(1)} collective-permute-done((f32[192,256]{1,0:T(8,128)S(1)}, f32[192,256]{1,0:T(8,128)S(1)}, u32[]{:S(2)}, u32[]{:S(2)}) %collective-permute-start.84) | collective-permute-done | bytes 196640 | tf_op jit(solution)/shard_map/ppermute | solution.py:55
  383.4 3.7 collective-permute-done.88
  403.4 3.5 collective-permute-done.95.refs_3_
  424.3 10.3 %shard_map.115.linv_ref.refs_4_ = f32[256,256]{1,0:T(8,128)S(1)} custom-call(s32[4]{0:T(128)S(1)} %pad_add_fusion.pos_ref, f32[128,256]{1,0:T(8,128)S(1)} %add_add_fusion.mine_ref, f32[128,256]{1,0:T(8,128)S(1)} %collective-permute-done.100.mate_ref), custom_call_target="tpu_custom_call" | custom-call | bytes 1024 | tf_op jit(solution)/shard_map/pallas_call | solution.py:214
  438.7 3.4 collective-permute-done.104.b1
  451.4 5.8 %all-to-all-start = ((f32[16,16,192]{2,1,0:T(8,128)}), f32[16,16,192]{2,1,0:T(8,128)}, u32[]{:S(2)}, u32[]{:S(2)}) async-start(f32[16,16,192]{2,1,0:T(8,128)} %bitcast.55), calls=%async_computation | async-start | bytes 524288 | tf_op jit(solution)/shard_map/all_to_all | solution.py:391
  460.6 11.5 %all-to-all-done.p_ref = f32[16,16,192]{2,1,0:T(8,128)} async-done(((f32[16,16,192]{2,1,0:T(8,128)}), f32[16,16,192]{2,1,0:T(8,128)}, u32[]{:S(2)}, u32[]{:S(2)}) %all-to-all-start) | async-done | bytes 196640 | tf_op jit(solution)/shard_map/all_to_all | solution.py:391
  472.1 6.3 %shard_map.120 = f32[192,16,256]{2,1,0:T(8,128)} custom-call(s32[4]{0:T(128)S(1)} %pad_add_fusion.pos_ref, f32[16,16,192]{2,1,0:T(8,128)} %all-to-all-done.p_ref, f32[768,256]{1,0:T(8,128)S(1)} %shard_map.119.refs_0_, f32[768,256]{1,0:T(8,128)} %collective-permute-done.107.refs_1_, f32[768,256]{1,0:T(8,128)} %collective-permute-done.108.refs_2_, ...), custom_call_target="tpu_custom_call" | custom-call | flops 1073741824 | bytes 6291456 | tf_op jit(solution)/shard_map/pallas_call | solution.py:398
  (350 shorter events, 275.8 us)
Async XLA Ops:
  5.0 49.0 %collective-permute-start.3 = (f32[768,256]{1,0:T(8,128)}, f32[768,256]{1,0:T(8,128)}, u32[]{:S(2)}, u32[]{:S(2)}) collective-permute-start(f32[768,256]{1,0:T(8,128)} %get-tuple-element.72), channel_id=1, source_target_pairs={{0,4},{1,5},{2,6},{3,7},{4,8},{5,9},{6,10},{7,11},{8,12},{9,13},{1... | collective-permute-start | bytes 2359304 | tf_op jit(solution)/shard_map/ppermute | solution.py:55
  7.0 22.7 %collective-permute-start.13 = (f32[128,256]{1,0:T(8,128)S(1)}, f32[128,256]{1,0:T(8,128)S(1)}, u32[]{:S(2)}, u32[]{:S(2)}) collective-permute-start(f32[128,256]{1,0:T(8,128)S(1)} %constant_dynamic-slice_fusion), channel_id=1, source_target_pairs={{0,4},{1,5},{2,6},{3,7},{4,8},{5,9},{6,10},{7,11},{8,12},{9,13},{1... | collective-permute-start | bytes 393224 | tf_op jit(solution)/shard_map/ppermute | solution.py:55
  9.0 20.7 %collective-permute-start.14 = (f32[128,256]{1,0:T(8,128)S(1)}, f32[128,256]{1,0:T(8,128)S(1)}, u32[]{:S(2)}, u32[]{:S(2)}) collective-permute-start(f32[128,256]{1,0:T(8,128)S(1)} %constant_dynamic-slice_fusion), channel_id=1, source_target_pairs={{0,12},{1,13},{2,14},{3,15},{4,0},{5,1},{6,2},{7,3},{8,4},{9,5},{1... | collective-permute-start | bytes 393224 | tf_op jit(solution)/shard_map/ppermute | solution.py:55
  10.3 23.3 %collective-permute-start.15 = (f32[128,256]{1,0:T(8,128)S(1)}, f32[128,256]{1,0:T(8,128)S(1)}, u32[]{:S(2)}, u32[]{:S(2)}) collective-permute-start(f32[128,256]{1,0:T(8,128)S(1)} %constant_dynamic-slice_fusion), channel_id=1, source_target_pairs={{0,8},{1,9},{2,10},{3,11},{4,12},{5,13},{6,14},{7,15},{8,0},{9,1},... | collective-permute-start | bytes 393224 | tf_op jit(solution)/shard_map/ppermute | solution.py:55
  12.7 43.6 %collective-permute-start.4 = (f32[768,256]{1,0:T(8,128)}, f32[768,256]{1,0:T(8,128)}, u32[]{:S(2)}, u32[]{:S(2)}) collective-permute-start(f32[768,256]{1,0:T(8,128)} %copy-done.31), channel_id=1, source_target_pairs={{0,12},{1,13},{2,14},{3,15},{4,0},{5,1},{6,2},{7,3},{8,4},{9,5},{1... | collective-permute-start | bytes 2359304 | tf_op jit(solution)/shard_map/ppermute | solution.py:55
  33.7 17.4 %collective-permute-start.16 = (f32[512,256]{1,0:T(8,128)S(1)}, f32[512,256]{1,0:T(8,128)S(1)}, u32[]{:S(2)}, u32[]{:S(2)}) collective-permute-start(f32[512,256]{1,0:T(8,128)S(1)} %pad_maximum_fusion.1.mine_ref), channel_id=1, source_target_pairs={{0,16},{1,17},{2,18},{3,19},{4,20},{5,21},{6,22},{7,23},{8,24},{9,... | collective-permute-start | bytes 1572872 | tf_op jit(solution)/shard_map/ppermute | solution.py:55
  42.8 21.0 %collective-permute-start.5 = (f32[768,256]{1,0:T(8,128)}, f32[768,256]{1,0:T(8,128)}, u32[]{:S(2)}, u32[]{:S(2)}) collective-permute-start(f32[768,256]{1,0:T(8,128)} %copy-done.30), channel_id=1, source_target_pairs={{0,8},{1,9},{2,10},{3,11},{4,12},{5,13},{6,14},{7,15},{8,0},{9,1},... | collective-permute-start | bytes 2359304 | tf_op jit(solution)/shard_map/ppermute | solution.py:55
  50.0 21.3 %collective-permute-start = (f32[768,256]{1,0:T(8,128)}, f32[768,256]{1,0:T(8,128)}, u32[]{:S(2)}, u32[]{:S(2)}) collective-permute-start(f32[768,256]{1,0:T(8,128)} %get-tuple-element.68), channel_id=1, source_target_pairs={{0,1},{1,2},{2,3},{3,0},{4,5},{5,6},{6,7},{7,4},{8,9},{9,10},{10,1... | collective-permute-start | bytes 2359304 | tf_op jit(solution)/shard_map/ppermute | solution.py:55
  52.0 37.8 %collective-permute-start.1 = (f32[768,256]{1,0:T(8,128)}, f32[768,256]{1,0:T(8,128)}, u32[]{:S(2)}, u32[]{:S(2)}) collective-permute-start(f32[768,256]{1,0:T(8,128)} %get-tuple-element.69), channel_id=1, source_target_pairs={{0,3},{1,0},{2,1},{3,2},{4,7},{5,4},{6,5},{7,6},{8,11},{9,8},{10,9... | collective-permute-start | bytes 2359304 | tf_op jit(solution)/shard_map/ppermute | solution.py:55
  54.0 35.7 %collective-permute-start.2 = (f32[768,256]{1,0:T(8,128)}, f32[768,256]{1,0:T(8,128)}, u32[]{:S(2)}, u32[]{:S(2)}) collective-permute-start(f32[768,256]{1,0:T(8,128)} %get-tuple-element.70), channel_id=1, source_target_pairs={{0,2},{1,3},{2,0},{3,1},{4,6},{5,7},{6,4},{7,5},{8,10},{9,11},{10,... | collective-permute-start | bytes 2359304 | tf_op jit(solution)/shard_map/ppermute | solution.py:55
  67.8 28.6 %collective-permute-start.17 = (f32[192,256]{1,0:T(8,128)S(1)}, f32[192,256]{1,0:T(8,128)S(1)}, u32[]{:S(2)}, u32[]{:S(2)}) collective-permute-start(f32[192,256]{1,0:T(8,128)S(1)} %get-tuple-element.80), channel_id=1, source_target_pairs={{0,3},{1,0},{2,1},{3,2},{4,7},{5,4},{6,5},{7,6},{8,11},{9,8},{10,9... | collective-permute-start | bytes 589832 | tf_op jit(solution)/shard_map/ppermute | solution.py:55
  70.7 29.9 %collective-permute-start.18 = (f32[192,256]{1,0:T(8,128)}, f32[192,256]{1,0:T(8,128)}, u32[]{:S(2)}, u32[]{:S(2)}) collective-permute-start(f32[192,256]{1,0:T(8,128)} %get-tuple-element.81), channel_id=1, source_target_pairs={{0,1},{1,2},{2,3},{3,0},{4,5},{5,6},{6,7},{7,4},{8,9},{9,10},{10,1... | collective-permute-start | bytes 589832 | tf_op jit(solution)/shard_map/ppermute | solution.py:55
  71.3 29.3 %collective-permute-start.19 = (f32[192,256]{1,0:T(8,128)}, f32[192,256]{1,0:T(8,128)}, u32[]{:S(2)}, u32[]{:S(2)}) collective-permute-start(f32[192,256]{1,0:T(8,128)} %get-tuple-element.82), channel_id=1, source_target_pairs={{0,2},{1,3},{2,0},{3,1},{4,6},{5,7},{6,4},{7,5},{8,10},{9,11},{10,... | collective-permute-start | bytes 589832 | tf_op jit(solution)/shard_map/ppermute | solution.py:55
  114.1 16.2 %collective-permute-start.20 = (f32[192,256]{1,0:T(8,128)}, f32[192,256]{1,0:T(8,128)S(1)}, u32[]{:S(2)}, u32[]{:S(2)}) collective-permute-start(f32[192,256]{1,0:T(8,128)} %get-tuple-element.83.b0), channel_id=1, source_target_pairs={{0,8},{1,9},{2,10},{3,11},{4,12},{5,13},{6,14},{7,15},{8,0},{9,1},... | collective-permute-start | bytes 589832 | tf_op jit(solution)/shard_map/ppermute | solution.py:55
  175.3 29.6 %collective-permute-start.34 = (f32[192,256]{1,0:T(8,128)S(1)}, f32[192,256]{1,0:T(8,128)S(1)}, u32[]{:S(2)}, u32[]{:S(2)}) collective-permute-start(f32[192,256]{1,0:T(8,128)S(1)} %get-tuple-element.91), channel_id=1, source_target_pairs={{0,12},{1,13},{2,14},{3,15},{4,0},{5,1},{6,2},{7,3},{8,4},{9,5},{1... | collective-permute-start | bytes 589832 | tf_op jit(solution)/shard_map/ppermute | solution.py:55
  176.3 28.6 %collective-permute-start.35 = (f32[192,256]{1,0:T(8,128)S(1)}, f32[192,256]{1,0:T(8,128)S(1)}, u32[]{:S(2)}, u32[]{:S(2)}) collective-permute-start(f32[192,256]{1,0:T(8,128)S(1)} %get-tuple-element.92), channel_id=1, source_target_pairs={{0,4},{1,5},{2,6},{3,7},{4,8},{5,9},{6,10},{7,11},{8,12},{9,13},{1... | collective-permute-start | bytes 589832 | tf_op jit(solution)/shard_map/ppermute | solution.py:55
  177.4 27.5 %collective-permute-start.36 = (f32[192,256]{1,0:T(8,128)S(1)}, f32[192,256]{1,0:T(8,128)S(1)}, u32[]{:S(2)}, u32[]{:S(2)}) collective-permute-start(f32[192,256]{1,0:T(8,128)S(1)} %get-tuple-element.93), channel_id=1, source_target_pairs={{0,8},{1,9},{2,10},{3,11},{4,12},{5,13},{6,14},{7,15},{8,0},{9,1},... | collective-permute-start | bytes 589832 | tf_op jit(solution)/shard_map/ppermute | solution.py:55
  180.4 14.2 %collective-permute-start.40 = (f32[128,256]{1,0:T(8,128)S(1)}, f32[128,256]{1,0:T(8,128)S(1)}, u32[]{:S(2)}, u32[]{:S(2)}) collective-permute-start(f32[128,256]{1,0:T(8,128)S(1)} %add_add_fusion.9.mine_ref), channel_id=1, source_target_pairs={{0,16},{1,17},{2,18},{3,19},{4,20},{5,21},{6,22},{7,23},{8,24},{9,... | collective-permute-start | bytes 393224 | tf_op jit(solution)/shard_map/ppermute | solution.py:55
  209.6 15.1 %collective-permute-start.41 = (f32[192,256]{1,0:T(8,128)S(1)}, f32[192,256]{1,0:T(8,128)}, u32[]{:S(2)}, u32[]{:S(2)}) collective-permute-start(f32[192,256]{1,0:T(8,128)S(1)} %get-tuple-element.95.b0), channel_id=1, source_target_pairs={{0,2},{1,3},{2,0},{3,1},{4,6},{5,7},{6,4},{7,5},{8,10},{9,11},{10,... | collective-permute-start | bytes 589832 | tf_op jit(solution)/shard_map/ppermute | solution.py:55
  268.3 16.5 %collective-permute-start.55 = (f32[192,256]{1,0:T(8,128)S(1)}, f32[192,256]{1,0:T(8,128)S(1)}, u32[]{:S(2)}, u32[]{:S(2)}) collective-permute-start(f32[192,256]{1,0:T(8,128)S(1)} %get-tuple-element.103), channel_id=1, source_target_pairs={{0,3},{1,0},{2,1},{3,2},{4,7},{5,4},{6,5},{7,6},{8,11},{9,8},{10,9... | collective-permute-start | bytes 589832 | tf_op jit(solution)/shard_map/ppermute | solution.py:55
  269.1 15.7 %collective-permute-start.56 = (f32[192,256]{1,0:T(8,128)S(1)}, f32[192,256]{1,0:T(8,128)S(1)}, u32[]{:S(2)}, u32[]{:S(2)}) collective-permute-start(f32[192,256]{1,0:T(8,128)S(1)} %get-tuple-element.104), channel_id=1, source_target_pairs={{0,1},{1,2},{2,3},{3,0},{4,5},{5,6},{6,7},{7,4},{8,9},{9,10},{10,1... | collective-permute-start | bytes 589832 | tf_op jit(solution)/shard_map/ppermute | solution.py:55
  270.4 14.4 %collective-permute-start.57 = (f32[192,256]{1,0:T(8,128)S(1)}, f32[192,256]{1,0:T(8,128)S(1)}, u32[]{:S(2)}, u32[]{:S(2)}) collective-permute-start(f32[192,256]{1,0:T(8,128)S(1)} %get-tuple-element.105), channel_id=1, source_target_pairs={{0,2},{1,3},{2,0},{3,1},{4,6},{5,7},{6,4},{7,5},{8,10},{9,11},{10,... | collective-permute-start | bytes 589832 | tf_op jit(solution)/shard_map/ppermute | solution.py:55
  342.3 17.6 %collective-permute-start.80 = (f32[192,256]{1,0:T(8,128)S(1)}, f32[192,256]{1,0:T(8,128)S(1)}, u32[]{:S(2)}, u32[]{:S(2)}) collective-permute-start(f32[192,256]{1,0:T(8,128)S(1)} %get-tuple-element.115), channel_id=1, source_target_pairs={{0,12},{1,13},{2,14},{3,15},{4,0},{5,1},{6,2},{7,3},{8,4},{9,5},{1... | collective-permute-start | bytes 589832 | tf_op jit(solution)/shard_map/ppermute | solution.py:55
  342.9 17.0 %collective-permute-start.81 = (f32[192,256]{1,0:T(8,128)S(1)}, f32[192,256]{1,0:T(8,128)S(1)}, u32[]{:S(2)}, u32[]{:S(2)}) collective-permute-start(f32[192,256]{1,0:T(8,128)S(1)} %get-tuple-element.116), channel_id=1, source_target_pairs={{0,4},{1,5},{2,6},{3,7},{4,8},{5,9},{6,10},{7,11},{8,12},{9,13},{1... | collective-permute-start | bytes 589832 | tf_op jit(solution)/shard_map/ppermute | solution.py:55
  344.4 15.5 %collective-permute-start.82 = (f32[192,256]{1,0:T(8,128)S(1)}, f32[192,256]{1,0:T(8,128)S(1)}, u32[]{:S(2)}, u32[]{:S(2)}) collective-permute-start(f32[192,256]{1,0:T(8,128)S(1)} %get-tuple-element.117), channel_id=1, source_target_pairs={{0,8},{1,9},{2,10},{3,11},{4,12},{5,13},{6,14},{7,15},{8,0},{9,1},... | collective-permute-start | bytes 589832 | tf_op jit(solution)/shard_map/ppermute | solution.py:55
  417.1 17.5 %collective-permute-start.101 = (f32[192,256]{1,0:T(8,128)S(1)}, f32[192,256]{1,0:T(8,128)S(1)}, u32[]{:S(2)}, u32[]{:S(2)}) collective-permute-start(f32[192,256]{1,0:T(8,128)S(1)} %get-tuple-element.128), channel_id=1, source_target_pairs={{0,3},{1,0},{2,1},{3,2},{4,7},{5,4},{6,5},{7,6},{8,11},{9,8},{10,9... | collective-permute-start | bytes 589832 | tf_op jit(solution)/shard_map/ppermute | solution.py:55
  417.8 16.9 %collective-permute-start.102 = (f32[192,256]{1,0:T(8,128)S(1)}, f32[192,256]{1,0:T(8,128)S(1)}, u32[]{:S(2)}, u32[]{:S(2)}) collective-permute-start(f32[192,256]{1,0:T(8,128)S(1)} %get-tuple-element.129), channel_id=1, source_target_pairs={{0,1},{1,2},{2,3},{3,0},{4,5},{5,6},{6,7},{7,4},{8,9},{9,10},{10,1... | collective-permute-start | bytes 589832 | tf_op jit(solution)/shard_map/ppermute | solution.py:55
  419.2 15.5 %collective-permute-start.103 = (f32[192,256]{1,0:T(8,128)S(1)}, f32[192,256]{1,0:T(8,128)S(1)}, u32[]{:S(2)}, u32[]{:S(2)}) collective-permute-start(f32[192,256]{1,0:T(8,128)S(1)} %get-tuple-element.130), channel_id=1, source_target_pairs={{0,2},{1,3},{2,0},{3,1},{4,6},{5,7},{6,4},{7,5},{8,10},{9,11},{10,... | collective-permute-start | bytes 589832 | tf_op jit(solution)/shard_map/ppermute | solution.py:55
  445.9 26.1 %collective-permute-start.107 = (f32[768,256]{1,0:T(8,128)S(1)}, f32[768,256]{1,0:T(8,128)}, u32[]{:S(2)}, u32[]{:S(2)}) collective-permute-start(f32[768,256]{1,0:T(8,128)S(1)} %shard_map.119.refs_0_), channel_id=1, source_target_pairs={{0,1},{1,2},{2,3},{3,0},{4,5},{5,6},{6,7},{7,4},{8,9},{9,10},{10,1... | collective-permute-start | bytes 2359304 | tf_op jit(solution)/shard_map/ppermute | solution.py:55
  447.5 24.6 %collective-permute-start.108 = (f32[768,256]{1,0:T(8,128)S(1)}, f32[768,256]{1,0:T(8,128)}, u32[]{:S(2)}, u32[]{:S(2)}) collective-permute-start(f32[768,256]{1,0:T(8,128)S(1)} %shard_map.119.refs_0_), channel_id=1, source_target_pairs={{0,3},{1,0},{2,1},{3,2},{4,7},{5,4},{6,5},{7,6},{8,11},{9,8},{10,9... | collective-permute-start | bytes 2359304 | tf_op jit(solution)/shard_map/ppermute | solution.py:55
  449.3 22.8 %collective-permute-start.109 = (f32[768,256]{1,0:T(8,128)S(1)}, f32[768,256]{1,0:T(8,128)}, u32[]{:S(2)}, u32[]{:S(2)}) collective-permute-start(f32[768,256]{1,0:T(8,128)S(1)} %shard_map.119.refs_0_), channel_id=1, source_target_pairs={{0,2},{1,3},{2,0},{3,1},{4,6},{5,7},{6,4},{7,5},{8,10},{9,11},{10,... | collective-permute-start | bytes 2359304 | tf_op jit(solution)/shard_map/ppermute | solution.py:55
  451.4 20.7 %all-to-all-start = ((f32[16,16,192]{2,1,0:T(8,128)}), f32[16,16,192]{2,1,0:T(8,128)}, u32[]{:S(2)}, u32[]{:S(2)}) async-start(f32[16,16,192]{2,1,0:T(8,128)} %bitcast.55), calls=%async_computation | async-start | bytes 524288 | tf_op jit(solution)/shard_map/all_to_all | solution.py:391
  (120 other events, 987.4 us)

commit v4 on v3

--- a/solution.py
+++ b/solution.py
@@ -18,7 +18,7 @@
 BF16 = jnp.bfloat16
 VMEM = pl.BlockSpec(memory_space=pltpu.VMEM)
 SMEM = pl.BlockSpec(memory_space=pltpu.SMEM)
-PARAMS = pltpu.CompilerParams(vmem_limit_bytes=20 * 1024 * 1024)
+PARAMS = pltpu.CompilerParams(vmem_limit_bytes=8 * 1024 * 1024)
 
 
 def call(kernel, outs, n_in, flops, nbytes, scratch=(), smem=0):
@@ -90,7 +90,7 @@
     return high, mid, (rest - mid.astype(F32)).astype(BF16)
 
 
-def pieces_kernel(side, pos_ref, a_ref, *o_refs):
+def pieces_kernel(side, pos_ref, a_ref, basis_ref, *o_refs):
     at, cross = pos_ref[PLACE[side]], pos_ref[PLACE[CROSS[side]]]
     for o_ref, d in zip(o_refs, ORDER):
         mine = lax.rem(at + d, RING)
@@ -98,64 +98,101 @@
             theirs = back(cross, e)
             source = theirs * RING + mine if side == "y" else mine * RING + theirs
             o_ref[j * 192 : j * 192 + 192, :] = a_ref[source].astype(F32)
-
-
-def turned_kernel(side, pos_ref, *refs):
-    for r, d in zip(refs[:-1], ORDER):
-        refs[-1][block_place(pos_ref, back(pos_ref[PLACE[side]], d))] = r[...].astype(BF16)
-
-
-def lay_out(side, pos, factors):
-    pieces = call(functools.partial(pieces_kernel, side), [f32s(768, 256)] * 4, 2, 0, 5 << 20,
-                  smem=1)(pos, factors.T.reshape(16, 192, 256))
-    return call(functools.partial(turned_kernel, side), jax.ShapeDtypeStruct((4, 768, 256), BF16),
-                5, 0, 5 << 20, smem=1)(pos, *deliver(pieces, side * 2, 1))
-
-
-def spread_kernel(side, pos_ref, mine_ref, mate_ref, o_ref):
-    for i, d in enumerate(ORDER):
-        p = block_place(pos_ref, back(pos_ref[PLACE[side]], d))
-        for c, ref in ((pos_ref[1], mine_ref), (1 - pos_ref[1], mate_ref)):
-            at = pl.multiple_of(p * 256 + c * 128, 128)
-            o_ref[pl.ds(at, 128), :] = ref[i * 128 : i * 128 + 128, :]
-
-
-def spread(side, pos, basis):
-    half = lax.dynamic_slice_in_dim(basis, pos[1] * 128, 128, 0)
-    mine = jnp.concatenate(exchange(half, side * 2), axis=0)
-    return call(functools.partial(spread_kernel, side), f32s(1024, 256), 3, 0, 2 << 20, smem=1)(
-        pos, mine, send(mine, "core")
-    )
-
-
-def project_kernel(a_ref, *refs):
-    sources, o_refs = refs[:-4], refs[-4:]
-    parts = split3(jnp.concatenate([r[...] for r in sources], axis=0))
+        o_ref[768:, :] = basis_ref[...]
+
+
+def pieces_of(side, pos, factors, basis):
+    return call(functools.partial(pieces_kernel, side), [f32s(1024, 256)] * 4, 3, 0, 6 << 20,
+                smem=1)(pos, factors.T.reshape(16, 192, 256), basis)
+
+
+def straight_kernel(piece_ref, o_ref):
+    o_ref[...] = piece_ref[:768, :].T.astype(BF16)
+
+
+def straighten(piece):
+    return call(straight_kernel, jax.ShapeDtypeStruct((256, 768), BF16), 1, 0, 2 << 20)(piece)
+
+
+def digest_kernel(last, piece_ref, *refs):
+    before, (turned_ref, *o_refs) = refs[: -5 if last else -2], refs[-5 if last else -2 :]
+    turned = piece_ref[:768, :].astype(BF16)
+    turned_ref[...] = turned
+    parts = split3(piece_ref[768:, :])
+    total = sum(jnp.dot(turned, part, preferred_element_type=F32) for part in reversed(parts))
+    for r in before:
+        total = r[...] + total
+    rows = 768 // len(o_refs)
     for j, o_ref in enumerate(o_refs):
-        block = jnp.concatenate([a_ref[p, j * 192 : j * 192 + 192, :] for p in range(4)], axis=1)
+        o_ref[...] = total[j * rows : j * rows + rows]
+
+
+def digest(piece, before, last=False):
+    outs = [jax.ShapeDtypeStruct((768, 256), BF16)]
+    outs += [f32s(192, 256)] * 4 if last else [f32s(768, 256)]
+    turned, *total = call(functools.partial(digest_kernel, last), outs, 1 + len(before),
+                          3 * 768 << 17, 3 << 20)(piece, *before)
+    return turned, total
+
+
+def lay_out(left, right):
+    left, right = lax.optimization_barrier((left, right))
+    right = deliver(right, RIGHT * 2, 1)
+    waiting, right[1] = lax.optimization_barrier((left[3], right[1]))
+    left = deliver([*left[:3], waiting], LEFT * 2, 1)
+    turned = {LEFT: [], RIGHT: []}
+    total = {LEFT: (), RIGHT: ()}
+    for i in range(3):
+        for side, pieces in ((LEFT, left), (RIGHT, right)):
+            block, total[side] = digest(pieces[i], total[side])
+            turned[side].append(block)
+    right[3], total[LEFT] = lax.optimization_barrier((right[3], total[LEFT]))
+    for side, pieces in ((RIGHT, right), (LEFT, left)):
+        block, total[side] = digest(pieces[3], total[side], last=True)
+        turned[side].append(block)
+    return [
+        (turned[side], [straighten(p) for p in pieces], total[side])
+        for side, pieces in ((LEFT, left), (RIGHT, right))
+    ]
+
+
+def row_places(side, pos_ref):
+    return [
+        pl.ds(pl.multiple_of(block_place(pos_ref, back(pos_ref[PLACE[side]], d)) * 256, 256), 256)
+        for d in ORDER
+    ]
+
+
+def project_kernel(side, pos_ref, a0, a1, a2, a3, top_ref, low_ref, *refs):
+    *o_refs, m_ref = refs
+    m_ref[:512, :] = top_ref[...]
+    m_ref[512:, :] = low_ref[...]
+    parts = split3(jnp.concatenate([m_ref[at, :] for at in row_places(side, pos_ref)], axis=0))
+    for j, o_ref in enumerate(o_refs):
+        block = jnp.concatenate([a[j * 192 : j * 192 + 192, :] for a in (a0, a1, a2, a3)], axis=1)
         o_ref[...] = sum(
             jnp.dot(block, part, preferred_element_type=F32) for part in reversed(parts)
         )
 
 
-def project(turned, *sources):
-    return call(project_kernel, [f32s(192, 256)] * 4, 1 + len(sources), 6 * 3072 << 16, 4 << 20)(
-        turned, *sources
-    )
-
-
-def gram_kernel(pos_ref, top_ref, low_ref, o_ref, g_ref):
-    g_ref[...] = sum(
-        lax.dot_general(r[...], r[...], (((0,), (0,)), ((), ())), precision=HIGH,
-                        preferred_element_type=F32)
-        for r in (top_ref, low_ref)
-    )
-    o_ref[...] = g_ref[pl.ds(pl.multiple_of(pos_ref[1] * 128, 128), 128), :]
-
-
-def gram(pos, top, low):
-    return call(gram_kernel, f32s(128, 256), 3, 12 << 24, 1 << 19,
-                [pltpu.VMEM((256, 256), F32)], smem=1)(pos, top, low)
+def project(side, pos, turned, top, low):
+    return call(functools.partial(project_kernel, side), [f32s(192, 256)] * 4, 7,
+                6 * 3072 << 16, 4 << 20, [pltpu.VMEM((1024, 256), F32)], smem=1)(
+        pos, *turned, top, low
+    )
+
+
+def gram_kernel(pos_ref, rows_ref, *refs):
+    mine = rows_ref[:, pl.ds(pl.multiple_of(pos_ref[1] * 128, 128), 128)]
+    total = lax.dot_general(mine, rows_ref[...], (((0,), (0,)), ((), ())), precision=HIGH,
+                            preferred_element_type=F32)
+    refs[-1][...] = refs[0][...] + total if len(refs) == 2 else total
+
+
+def gram(pos, rows, *before):
+    return call(gram_kernel, f32s(128, 256), 2 + len(before), 12 << 24, 1 << 19, smem=1)(
+        pos, rows, *before
+    )
 
 
 def eliminate(tall, at):
@@ -255,30 +292,29 @@
     q_ref[...] = normalised(refs[:4], linv_ref, scale_ref[...])
 
 
-def product(factors, blocks):
-    return sum(
-        jnp.dot(a[...], part, preferred_element_type=F32)
-        for a, block in zip(factors, blocks)
-        for part in reversed(split3(block[...]))
-    )
-
-
-def early_kernel(a0, a1, a2, b0, b1, b2, o_ref):
-    o_ref[...] = product((a0, a1, a2), (b0, b1, b2))
-
-
-def late_kernel(a3, b3, part_ref, keep_ref, send_ref):
-    total = part_ref[...] + product((a3,), (b3,))
-    keep_ref[...] = total[:512]
-    send_ref[...] = total[512:]
-
-
-def update(factors, blocks):
-    part = call(early_kernel, f32s(1024, 256), 6, 4 * 3072 << 16, 3 << 20)(
-        *factors[:3], *blocks[:3]
-    )
-    return call(late_kernel, [f32s(512, 256)] * 2, 3, 2 * 3072 << 16, 2 << 20)(
-        factors[3], blocks[3], part
+def product(factors, at, blocks):
+    a = jnp.concatenate([f[:, at : at + 384] for f in factors], axis=0)
+    b = jnp.concatenate([b[...] for b in blocks], axis=0)
+    return sum(jnp.dot(a, part, preferred_element_type=F32) for part in reversed(split3(b)))
+
+
+def early_kernel(a0, a1, a2, a3, b0, b1, o_ref):
+    o_ref[...] = product((a0, a1, a2, a3), 0, (b0, b1))
+
+
+def late_kernel(side, pos_ref, a0, a1, a2, a3, b2, b3, part_ref, keep_ref, send_ref, m_ref):
+    total = part_ref[...] + product((a0, a1, a2, a3), 384, (b2, b3))
+    for i, at in enumerate(row_places(side, pos_ref)):
+        m_ref[at, :] = total[i * 256 : i * 256 + 256]
+    keep_ref[...] = m_ref[:512, :]
+    send_ref[...] = m_ref[512:, :]
+
+
+def update(side, pos, straight, blocks):
+    part = call(early_kernel, f32s(1024, 256), 6, 3 * 3072 << 16, 3 << 20)(*straight, *blocks[:2])
+    return call(functools.partial(late_kernel, side), [f32s(512, 256)] * 2, 8, 3 * 3072 << 16,
+                3 << 20, [pltpu.VMEM((1024, 256), F32)], smem=1)(
+        pos, *straight, *blocks[2:], part
     )
 
 
@@ -328,8 +364,12 @@
         for j, second in enumerate(ORDER):
             source = chunk_at(pos_ref, first, second)
             wide = jnp.where(mask, jnp.concatenate([p_ref[source]] * 12, axis=0), 0.0)
-            q = blocks[i][j * 192 : j * 192 + 192, :]
-            core = jnp.dot(wide, q, precision=HIGH, preferred_element_type=F32)
+            p_high, p_mid, unused = split3(wide)
+            q_high, q_mid, unused = split3(blocks[i][j * 192 : j * 192 + 192, :])
+            core = sum(
+                jnp.dot(p, q, preferred_element_type=F32)
+                for p, q in ((p_mid, q_high), (p_high, q_mid), (p_high, q_high))
+            )
             o_ref[pl.ds(source * 12, 12)] = core.reshape(12, 16, 256)
 
 
@@ -343,12 +383,12 @@
     return exchange(joined, "yz")
 
 
-def refit(side, pos, factors, turned, coupling):
+def refit(side, pos, straight, turned, coupling):
     cross = CROSS[side] * 2
-    half = add_up(side, pos, *update(factors, exchange(coupling, cross)))
+    half = add_up(side, pos, *update(side, pos, straight, exchange(coupling, cross)))
     rest = send(half, "core")
-    piece = sum(exchange(gram(pos, half, rest), cross))
-    pieces = deliver(project(turned, half, rest), cross)
+    piece = sum(exchange(gram(pos, rest, gram(pos, half)), cross))
+    pieces = deliver(project(side, pos, turned, half, rest), cross)
     return half, rest, inverse_factor(pos, piece, send(piece, "core")), pieces
 
 
@@ -365,17 +405,10 @@
     pos = jnp.stack([adapter // 2, c, row // 4, row % 4]).astype(jnp.int32)
     scale = column_scale(lax.dynamic_slice_in_dim(ranks, row * 12, 12, 0))
 
-    left_rows, right_rows = spread(LEFT, pos, left), spread(RIGHT, pos, right)
-    up_turned, down_turned = lay_out(LEFT, pos, up), lay_out(RIGHT, pos, down)
-    left_pieces = deliver(project(up_turned, left_rows), CROSS[LEFT] * 2)
-    right_pieces = deliver(project(down_turned, right_rows), CROSS[RIGHT] * 2)
-    up, down = (
-        [
-            turned[:, j * 192 : j * 192 + 192].transpose(0, 2, 1).reshape(1024, 192)
-            for j in range(4)
-        ]
-        for turned in (up_turned, down_turned)
-    )
+    sides = lay_out(pieces_of(LEFT, pos, up, left), pieces_of(RIGHT, pos, down, right))
+    (up_turned, up, left_chunks), (down_turned, down, right_chunks) = sides
+    left_pieces = deliver(left_chunks, CROSS[LEFT] * 2)
+    right_pieces = deliver(right_chunks, CROSS[RIGHT] * 2)
     side = f32s(192, 256)
     coupling, p, q = call(first_kernel, [side] * 3, 9, 1 << 28, 3 << 20)(
         *left_pieces, *right_pieces, scale

time: 489 us -> 445 us (0.910)
  the two profiles are of different devices: /device:TPU:0 before, /device:TPU:1 now
where the time goes in v4:
time: 445 us; the launch traced here: 437 us
  waiting for transfers between devices  161 us (36%)
  starting transfers between devices  157 us (35%)
  Pallas kernels  100 us (22%)
  local copies, waits for them, and re-layouts  15.4 us (3%)
    ppermute x102, starting transfers between devices, send(): return lax.ppermute(value, ('adapter', 'row'), perm)  152 us
    ppermute x102, waiting for transfers between devices, send(): return lax.ppermute(value, ('adapter', 'row'), perm)  148 us
    pallas_call x4, Pallas kernels, inverse_factor(): call(inverse_kernel, f32s(K, K), 3, 0, 1 << 10, [pltpu.VMEM((K, K), F32)]...  41.4 us
    all_to_all x1, waiting for transfers between devices, shards(): p_rows = lax.all_to_all(p.T.reshape(16, 16, 192), 'row', 0, 0)  12.9 us
    unnamed x68, local copies, waits for them, and re-layouts  10.1 us
  transfers between devices with their start and end apart: 103, of which 67 were waited for; matrix products, arithmetic and copies ran while one was open for 0% of the time, Pallas kernels for 16%

profile of v4, /device:TPU:1, one launch (start us, length us, event | category | flops | bytes accessed | tf_op | source)
XLA Modules:
  0.0 436.6 jit_solution(8957083903364513844)
XLA Ops:
  12.1 3.3 collective-permute-start.5
  16.1 18.2 %collective-permute-done.2.piece_ref = f32[1024,256]{1,0:T(8,128)S(1)} collective-permute-done((f32[1024,256]{1,0:T(8,128)S(1)}, f32[1024,256]{1,0:T(8,128)S(1)}, u32[]{:S(2)}, u32[]{:S(2)}) %collective-permute-start.2) | collective-permute-done | bytes 1048608 | tf_op jit(solution)/shard_map/ppermute | solution.py:55
  34.4 2.9 collective-permute-start.3
  41.9 15.9 %collective-permute-done.5.piece_ref = f32[1024,256]{1,0:T(8,128)S(1)} collective-permute-done((f32[1024,256]{1,0:T(8,128)S(1)}, f32[1024,256]{1,0:T(8,128)S(1)}, u32[]{:S(2)}, u32[]{:S(2)}) %collective-permute-start.5) | collective-permute-done | bytes 1048608 | tf_op jit(solution)/shard_map/ppermute | solution.py:55
  71.8 3.4 collective-permute-start.6
  78.4 5.0 %collective-permute-done.7.refs_2_ = f32[192,256]{1,0:T(8,128)} collective-permute-done((f32[192,256]{1,0:T(8,128)}, f32[192,256]{1,0:T(8,128)}, u32[]{:S(2)}, u32[]{:S(2)}) %collective-permute-start.7) | collective-permute-done | bytes 196640 | tf_op jit(solution)/shard_map/ppermute | solution.py:55
  98.8 13.1 %collective-permute-start.15 = (f32[512,256]{1,0:T(8,128)S(1)}, f32[512,256]{1,0:T(8,128)S(1)}, u32[]{:S(2)}, u32[]{:S(2)}) collective-permute-start(f32[512,256]{1,0:T(8,128)S(1)} %get-tuple-element.137), channel_id=1, source_target_pairs={{0,16},{1,17},{2,18},{3,19},{4,20},{5,21},{6,22},{7,23},{8,24},{9,... | collective-permute-start | bytes 1572872 | tf_op jit(solution)/shard_map/ppermute | solution.py:55
  114.1 3.5 collective-permute-start.16
  119.6 4.8 %collective-permute-done.17 = f32[128,256]{1,0:T(8,128)S(1)} collective-permute-done((f32[128,256]{1,0:T(8,128)S(1)}, f32[128,256]{1,0:T(8,128)S(1)}, u32[]{:S(2)}, u32[]{:S(2)}) %collective-permute-start.17) | collective-permute-done | bytes 131104 | tf_op jit(solution)/shard_map/ppermute | solution.py:55
  135.5 2.8 collective-permute-done.24.refs_3_
  140.8 3.7 collective-permute-start.25
  159.5 10.3 %shard_map.102.refs_4_ = f32[256,256]{1,0:T(8,128)S(1)} custom-call(s32[4]{0:T(128)S(1)} %pad_add_fusion.pos_ref, f32[128,256]{1,0:T(8,128)S(1)} %add_add_fusion.9.mine_ref, f32[128,256]{1,0:T(8,128)S(1)} %collective-permute-done.32.mate_ref), custom_call_target="tpu_custom_call" | custom-call | bytes 1024 | tf_op jit(solution)/shard_map/pallas_call | solution.py:251
  175.4 3.5 collective-permute-done.35.b1
  193.2 4.3 collective-permute-done.38
  200.3 2.8 collective-permute-done.42
  207.1 3.1 collective-permute-done.45.refs_3_
  212.7 7.3 %collective-permute-start.46 = (f32[512,256]{1,0:T(8,128)S(1)}, f32[512,256]{1,0:T(8,128)S(1)}, u32[]{:S(2)}, u32[]{:S(2)}) collective-permute-start(f32[512,256]{1,0:T(8,128)S(1)} %shard_map.107.top_ref.rows_ref), channel_id=1, source_target_pairs={{0,16},{1,17},{2,18},{3,19},{4,20},{5,21},{6,22},{7,23},{8,24},{9,... | collective-permute-start | bytes 1572872 | tf_op jit(solution)/shard_map/ppermute | solution.py:55
  227.6 2.7 collective-permute-start.47
  234.8 10.3 %shard_map.111.refs_4_ = f32[256,256]{1,0:T(8,128)S(1)} custom-call(s32[4]{0:T(128)S(1)} %pad_add_fusion.pos_ref, f32[128,256]{1,0:T(8,128)S(1)} %add_add_fusion.6.mine_ref, f32[128,256]{1,0:T(8,128)S(1)} %collective-permute-done.53.mate_ref), custom_call_target="tpu_custom_call" | custom-call | bytes 1024 | tf_op jit(solution)/shard_map/pallas_call | solution.py:251
  249.3 8.9 %collective-permute-done.56.b1 = f32[192,256]{1,0:T(8,128)S(1)} collective-permute-done((f32[192,256]{1,0:T(8,128)S(1)}, f32[192,256]{1,0:T(8,128)S(1)}, u32[]{:S(2)}, u32[]{:S(2)}) %collective-permute-start.56) | collective-permute-done | bytes 196640 | tf_op jit(solution)/shard_map/ppermute | solution.py:55
  269.4 3.5 collective-permute-done.59
  288.8 7.4 %collective-permute-start.67 = (f32[512,256]{1,0:T(8,128)S(1)}, f32[512,256]{1,0:T(8,128)S(1)}, u32[]{:S(2)}, u32[]{:S(2)}) collective-permute-start(f32[512,256]{1,0:T(8,128)S(1)} %shard_map.116.rows_ref.top_ref), channel_id=1, source_target_pairs={{0,16},{1,17},{2,18},{3,19},{4,20},{5,21},{6,22},{7,23},{8,24},{9,... | collective-permute-start | bytes 1572872 | tf_op jit(solution)/shard_map/ppermute | solution.py:55
  310.3 10.4 %shard_map.119.linv_ref.refs_4_ = f32[256,256]{1,0:T(8,128)S(1)} custom-call(s32[4]{0:T(128)S(1)} %pad_add_fusion.pos_ref, f32[128,256]{1,0:T(8,128)S(1)} %add_add_fusion.3.mine_ref, f32[128,256]{1,0:T(8,128)S(1)} %collective-permute-done.71.mate_ref), custom_call_target="tpu_custom_call" | custom-call | bytes 1024 | tf_op jit(solution)/shard_map/pallas_call | solution.py:251
  325.3 8.9 %collective-permute-done.77.b1 = f32[192,256]{1,0:T(8,128)S(1)} collective-permute-done((f32[192,256]{1,0:T(8,128)S(1)}, f32[192,256]{1,0:T(8,128)S(1)}, u32[]{:S(2)}, u32[]{:S(2)}) %collective-permute-start.77) | collective-permute-done | bytes 196640 | tf_op jit(solution)/shard_map/ppermute | solution.py:55
  344.9 4.0 collective-permute-done.80
  358.6 2.9 collective-permute-done.87.refs_3_
  364.3 7.7 %collective-permute-start.88 = (f32[512,256]{1,0:T(8,128)S(1)}, f32[512,256]{1,0:T(8,128)S(1)}, u32[]{:S(2)}, u32[]{:S(2)}) collective-permute-start(f32[512,256]{1,0:T(8,128)S(1)} %shard_map.126.rows_ref.top_ref), channel_id=1, source_target_pairs={{0,16},{1,17},{2,18},{3,19},{4,20},{5,21},{6,22},{7,23},{8,24},{9,... | collective-permute-start | bytes 1572872 | tf_op jit(solution)/shard_map/ppermute | solution.py:55
  386.0 10.4 %shard_map.129.linv_ref.refs_4_ = f32[256,256]{1,0:T(8,128)S(1)} custom-call(s32[4]{0:T(128)S(1)} %pad_add_fusion.pos_ref, f32[128,256]{1,0:T(8,128)S(1)} %add_add_fusion.mine_ref, f32[128,256]{1,0:T(8,128)S(1)} %collective-permute-done.92.mate_ref), custom_call_target="tpu_custom_call" | custom-call | bytes 1024 | tf_op jit(solution)/shard_map/pallas_call | solution.py:251
  398.1 3.2 collective-permute-start.97
  410.5 4.5 %all-to-all-start = ((f32[16,16,192]{2,1,0:T(8,128)}), f32[16,16,192]{2,1,0:T(8,128)}, u32[]{:S(2)}, u32[]{:S(2)}) async-start(f32[16,16,192]{2,1,0:T(8,128)} %bitcast.15), calls=%async_computation | async-start | bytes 524288 | tf_op jit(solution)/shard_map/all_to_all | solution.py:424
  418.3 12.9 %all-to-all-done.p_ref = f32[16,16,192]{2,1,0:T(8,128)} async-done(((f32[16,16,192]{2,1,0:T(8,128)}), f32[16,16,192]{2,1,0:T(8,128)}, u32[]{:S(2)}, u32[]{:S(2)}) %all-to-all-start) | async-done | bytes 196640 | tf_op jit(solution)/shard_map/all_to_all | solution.py:424
  431.2 5.0 %shard_map.134 = f32[192,16,256]{2,1,0:T(8,128)} custom-call(s32[4]{0:T(128)S(1)} %pad_add_fusion.pos_ref, f32[16,16,192]{2,1,0:T(8,128)} %all-to-all-done.p_ref, f32[768,256]{1,0:T(8,128)S(1)} %shard_map.133.refs_0_, f32[768,256]{1,0:T(8,128)} %collective-permute-done.99.refs_1_, f32[768,256]{1,0:T(8,128)} %collective-permute-done.100.refs_2_, ...), custom_call_target="tpu_custom_call" | custom-call | flops 1073741824 | bytes 6291456 | tf_op jit(solution)/shard_map/pallas_call | solution.py:431
  (320 shorter events, 223.9 us)
Async XLA Ops:
  6.9 27.5 %collective-permute-start.2 = (f32[1024,256]{1,0:T(8,128)S(1)}, f32[1024,256]{1,0:T(8,128)S(1)}, u32[]{:S(2)}, u32[]{:S(2)}) collective-permute-start(f32[1024,256]{1,0:T(8,128)S(1)} %get-tuple-element.105), channel_id=1, source_target_pairs={{0,4},{1,5},{2,6},{3,7},{4,8},{5,9},{6,10},{7,11},{8,12},{9,13},{1... | collective-permute-start | bytes 3145736 | tf_op jit(solution)/shard_map/ppermute | solution.py:55
  9.4 29.7 %collective-permute-start = (f32[1024,256]{1,0:T(8,128)S(1)}, f32[1024,256]{1,0:T(8,128)S(1)}, u32[]{:S(2)}, u32[]{:S(2)}) collective-permute-start(f32[1024,256]{1,0:T(8,128)S(1)} %get-tuple-element.102), channel_id=1, source_target_pairs={{0,1},{1,2},{2,3},{3,0},{4,5},{5,6},{6,7},{7,4},{8,9},{9,10},{10,1... | collective-permute-start | bytes 3145736 | tf_op jit(solution)/shard_map/ppermute | solution.py:55
  10.7 28.9 %collective-permute-start.1 = (f32[1024,256]{1,0:T(8,128)S(1)}, f32[1024,256]{1,0:T(8,128)S(1)}, u32[]{:S(2)}, u32[]{:S(2)}) collective-permute-start(f32[1024,256]{1,0:T(8,128)S(1)} %get-tuple-element.103), channel_id=1, source_target_pairs={{0,3},{1,0},{2,1},{3,2},{4,7},{5,4},{6,5},{7,6},{8,11},{9,8},{10,9... | collective-permute-start | bytes 3145736 | tf_op jit(solution)/shard_map/ppermute | solution.py:55
  12.1 45.7 %collective-permute-start.5 = (f32[1024,256]{1,0:T(8,128)S(1)}, f32[1024,256]{1,0:T(8,128)S(1)}, u32[]{:S(2)}, u32[]{:S(2)}) collective-permute-start(f32[1024,256]{1,0:T(8,128)S(1)} %get-tuple-element.115), channel_id=1, source_target_pairs={{0,8},{1,9},{2,10},{3,11},{4,12},{5,13},{6,14},{7,15},{8,0},{9,1},... | collective-permute-start | bytes 3145736 | tf_op jit(solution)/shard_map/ppermute | solution.py:55
  15.4 44.5 %collective-permute-start.4 = (f32[1024,256]{1,0:T(8,128)S(1)}, f32[1024,256]{1,0:T(8,128)S(1)}, u32[]{:S(2)}, u32[]{:S(2)}) collective-permute-start(f32[1024,256]{1,0:T(8,128)S(1)} %get-tuple-element.112), channel_id=1, source_target_pairs={{0,12},{1,13},{2,14},{3,15},{4,0},{5,1},{6,2},{7,3},{8,4},{9,5},{1... | collective-permute-start | bytes 3145736 | tf_op jit(solution)/shard_map/ppermute | solution.py:55
  34.4 32.4 %collective-permute-start.3 = (f32[1024,256]{1,0:T(8,128)}, f32[1024,256]{1,0:T(8,128)}, u32[]{:S(2)}, u32[]{:S(2)}) collective-permute-start(f32[1024,256]{1,0:T(8,128)} %get-tuple-element.106), channel_id=1, source_target_pairs={{0,2},{1,3},{2,0},{3,1},{4,6},{5,7},{6,4},{7,5},{8,10},{9,11},{10,... | collective-permute-start | bytes 3145736 | tf_op jit(solution)/shard_map/ppermute | solution.py:55
  63.7 11.5 %collective-permute-start.9 = (f32[192,256]{1,0:T(8,128)}, f32[192,256]{1,0:T(8,128)}, u32[]{:S(2)}, u32[]{:S(2)}) collective-permute-start(f32[192,256]{1,0:T(8,128)} %get-tuple-element.132), channel_id=1, source_target_pairs={{0,3},{1,0},{2,1},{3,2},{4,7},{5,4},{6,5},{7,6},{8,11},{9,8},{10,9... | collective-permute-start | bytes 589832 | tf_op jit(solution)/shard_map/ppermute | solution.py:55
  65.1 11.4 %collective-permute-start.10 = (f32[192,256]{1,0:T(8,128)}, f32[192,256]{1,0:T(8,128)}, u32[]{:S(2)}, u32[]{:S(2)}) collective-permute-start(f32[192,256]{1,0:T(8,128)} %copy-done.28), channel_id=1, source_target_pairs={{0,1},{1,2},{2,3},{3,0},{4,5},{5,6},{6,7},{7,4},{8,9},{9,10},{10,1... | collective-permute-start | bytes 589832 | tf_op jit(solution)/shard_map/ppermute | solution.py:55
  65.2 11.4 %collective-permute-start.11 = (f32[192,256]{1,0:T(8,128)}, f32[192,256]{1,0:T(8,128)}, u32[]{:S(2)}, u32[]{:S(2)}) collective-permute-start(f32[192,256]{1,0:T(8,128)} %copy-done.27), channel_id=1, source_target_pairs={{0,2},{1,3},{2,0},{3,1},{4,6},{5,7},{6,4},{7,5},{8,10},{9,11},{10,... | collective-permute-start | bytes 589832 | tf_op jit(solution)/shard_map/ppermute | solution.py:55
  98.8 14.6 %collective-permute-start.15 = (f32[512,256]{1,0:T(8,128)S(1)}, f32[512,256]{1,0:T(8,128)S(1)}, u32[]{:S(2)}, u32[]{:S(2)}) collective-permute-start(f32[512,256]{1,0:T(8,128)S(1)} %get-tuple-element.137), channel_id=1, source_target_pairs={{0,16},{1,17},{2,18},{3,19},{4,20},{5,21},{6,22},{7,23},{8,24},{9,... | collective-permute-start | bytes 1572872 | tf_op jit(solution)/shard_map/ppermute | solution.py:55
  152.0 17.9 %collective-permute-start.26 = (f32[192,256]{1,0:T(8,128)S(1)}, f32[192,256]{1,0:T(8,128)S(1)}, u32[]{:S(2)}, u32[]{:S(2)}) collective-permute-start(f32[192,256]{1,0:T(8,128)S(1)} %get-tuple-element.143), channel_id=1, source_target_pairs={{0,12},{1,13},{2,14},{3,15},{4,0},{5,1},{6,2},{7,3},{8,4},{9,5},{1... | collective-permute-start | bytes 589832 | tf_op jit(solution)/shard_map/ppermute | solution.py:55
  154.2 15.6 %collective-permute-start.27 = (f32[192,256]{1,0:T(8,128)S(1)}, f32[192,256]{1,0:T(8,128)S(1)}, u32[]{:S(2)}, u32[]{:S(2)}) collective-permute-start(f32[192,256]{1,0:T(8,128)S(1)} %get-tuple-element.144), channel_id=1, source_target_pairs={{0,4},{1,5},{2,6},{3,7},{4,8},{5,9},{6,10},{7,11},{8,12},{9,13},{1... | collective-permute-start | bytes 589832 | tf_op jit(solution)/shard_map/ppermute | solution.py:55
  154.2 15.6 %collective-permute-start.28 = (f32[192,256]{1,0:T(8,128)S(1)}, f32[192,256]{1,0:T(8,128)S(1)}, u32[]{:S(2)}, u32[]{:S(2)}) collective-permute-start(f32[192,256]{1,0:T(8,128)S(1)} %get-tuple-element.145), channel_id=1, source_target_pairs={{0,8},{1,9},{2,10},{3,11},{4,12},{5,13},{6,14},{7,15},{8,0},{9,1},... | collective-permute-start | bytes 589832 | tf_op jit(solution)/shard_map/ppermute | solution.py:55
  227.6 17.6 %collective-permute-start.47 = (f32[192,256]{1,0:T(8,128)S(1)}, f32[192,256]{1,0:T(8,128)S(1)}, u32[]{:S(2)}, u32[]{:S(2)}) collective-permute-start(f32[192,256]{1,0:T(8,128)S(1)} %get-tuple-element.155), channel_id=1, source_target_pairs={{0,3},{1,0},{2,1},{3,2},{4,7},{5,4},{6,5},{7,6},{8,11},{9,8},{10,9... | collective-permute-start | bytes 589832 | tf_op jit(solution)/shard_map/ppermute | solution.py:55
  230.3 14.9 %collective-permute-start.48 = (f32[192,256]{1,0:T(8,128)S(1)}, f32[192,256]{1,0:T(8,128)S(1)}, u32[]{:S(2)}, u32[]{:S(2)}) collective-permute-start(f32[192,256]{1,0:T(8,128)S(1)} %get-tuple-element.156), channel_id=1, source_target_pairs={{0,1},{1,2},{2,3},{3,0},{4,5},{5,6},{6,7},{7,4},{8,9},{9,10},{10,1... | collective-permute-start | bytes 589832 | tf_op jit(solution)/shard_map/ppermute | solution.py:55
  230.3 14.9 %collective-permute-start.49 = (f32[192,256]{1,0:T(8,128)S(1)}, f32[192,256]{1,0:T(8,128)S(1)}, u32[]{:S(2)}, u32[]{:S(2)}) collective-permute-start(f32[192,256]{1,0:T(8,128)S(1)} %get-tuple-element.157), channel_id=1, source_target_pairs={{0,2},{1,3},{2,0},{3,1},{4,6},{5,7},{6,4},{7,5},{8,10},{9,11},{10,... | collective-permute-start | bytes 589832 | tf_op jit(solution)/shard_map/ppermute | solution.py:55
  246.5 11.6 %collective-permute-start.56 = (f32[192,256]{1,0:T(8,128)S(1)}, f32[192,256]{1,0:T(8,128)S(1)}, u32[]{:S(2)}, u32[]{:S(2)}) collective-permute-start(f32[192,256]{1,0:T(8,128)S(1)} %get-tuple-element.159.b0), channel_id=1, source_target_pairs={{0,4},{1,5},{2,6},{3,7},{4,8},{5,9},{6,10},{7,11},{8,12},{9,13},{1... | collective-permute-start | bytes 589832 | tf_op jit(solution)/shard_map/ppermute | solution.py:55
  246.6 12.6 %collective-permute-start.55 = (f32[192,256]{1,0:T(8,128)S(1)}, f32[192,256]{1,0:T(8,128)S(1)}, u32[]{:S(2)}, u32[]{:S(2)}) collective-permute-start(f32[192,256]{1,0:T(8,128)S(1)} %get-tuple-element.159.b0), channel_id=1, source_target_pairs={{0,8},{1,9},{2,10},{3,11},{4,12},{5,13},{6,14},{7,15},{8,0},{9,1},... | collective-permute-start | bytes 589832 | tf_op jit(solution)/shard_map/ppermute | solution.py:55
  246.9 12.3 %collective-permute-start.54 = (f32[192,256]{1,0:T(8,128)S(1)}, f32[192,256]{1,0:T(8,128)S(1)}, u32[]{:S(2)}, u32[]{:S(2)}) collective-permute-start(f32[192,256]{1,0:T(8,128)S(1)} %get-tuple-element.159.b0), channel_id=1, source_target_pairs={{0,12},{1,13},{2,14},{3,15},{4,0},{5,1},{6,2},{7,3},{8,4},{9,5},{1... | collective-permute-start | bytes 589832 | tf_op jit(solution)/shard_map/ppermute | solution.py:55
  303.1 17.5 %collective-permute-start.72 = (f32[192,256]{1,0:T(8,128)S(1)}, f32[192,256]{1,0:T(8,128)S(1)}, u32[]{:S(2)}, u32[]{:S(2)}) collective-permute-start(f32[192,256]{1,0:T(8,128)S(1)} %get-tuple-element.167), channel_id=1, source_target_pairs={{0,12},{1,13},{2,14},{3,15},{4,0},{5,1},{6,2},{7,3},{8,4},{9,5},{1... | collective-permute-start | bytes 589832 | tf_op jit(solution)/shard_map/ppermute | solution.py:55
  305.6 15.1 %collective-permute-start.73 = (f32[192,256]{1,0:T(8,128)S(1)}, f32[192,256]{1,0:T(8,128)S(1)}, u32[]{:S(2)}, u32[]{:S(2)}) collective-permute-start(f32[192,256]{1,0:T(8,128)S(1)} %get-tuple-element.168), channel_id=1, source_target_pairs={{0,4},{1,5},{2,6},{3,7},{4,8},{5,9},{6,10},{7,11},{8,12},{9,13},{1... | collective-permute-start | bytes 589832 | tf_op jit(solution)/shard_map/ppermute | solution.py:55
  305.6 15.1 %collective-permute-start.74 = (f32[192,256]{1,0:T(8,128)S(1)}, f32[192,256]{1,0:T(8,128)S(1)}, u32[]{:S(2)}, u32[]{:S(2)}) collective-permute-start(f32[192,256]{1,0:T(8,128)S(1)} %get-tuple-element.169), channel_id=1, source_target_pairs={{0,8},{1,9},{2,10},{3,11},{4,12},{5,13},{6,14},{7,15},{8,0},{9,1},... | collective-permute-start | bytes 589832 | tf_op jit(solution)/shard_map/ppermute | solution.py:55
  322.6 11.6 %collective-permute-start.77 = (f32[192,256]{1,0:T(8,128)S(1)}, f32[192,256]{1,0:T(8,128)S(1)}, u32[]{:S(2)}, u32[]{:S(2)}) collective-permute-start(f32[192,256]{1,0:T(8,128)S(1)} %get-tuple-element.171.b0), channel_id=1, source_target_pairs={{0,1},{1,2},{2,3},{3,0},{4,5},{5,6},{6,7},{7,4},{8,9},{9,10},{10,1... | collective-permute-start | bytes 589832 | tf_op jit(solution)/shard_map/ppermute | solution.py:55
  322.7 12.6 %collective-permute-start.76 = (f32[192,256]{1,0:T(8,128)S(1)}, f32[192,256]{1,0:T(8,128)S(1)}, u32[]{:S(2)}, u32[]{:S(2)}) collective-permute-start(f32[192,256]{1,0:T(8,128)S(1)} %get-tuple-element.171.b0), channel_id=1, source_target_pairs={{0,2},{1,3},{2,0},{3,1},{4,6},{5,7},{6,4},{7,5},{8,10},{9,11},{10,... | collective-permute-start | bytes 589832 | tf_op jit(solution)/shard_map/ppermute | solution.py:55
  323.1 12.1 %collective-permute-start.75 = (f32[192,256]{1,0:T(8,128)S(1)}, f32[192,256]{1,0:T(8,128)S(1)}, u32[]{:S(2)}, u32[]{:S(2)}) collective-permute-start(f32[192,256]{1,0:T(8,128)S(1)} %get-tuple-element.171.b0), channel_id=1, source_target_pairs={{0,3},{1,0},{2,1},{3,2},{4,7},{5,4},{6,5},{7,6},{8,11},{9,8},{10,9... | collective-permute-start | bytes 589832 | tf_op jit(solution)/shard_map/ppermute | solution.py:55
  378.9 17.5 %collective-permute-start.93 = (f32[192,256]{1,0:T(8,128)S(1)}, f32[192,256]{1,0:T(8,128)S(1)}, u32[]{:S(2)}, u32[]{:S(2)}) collective-permute-start(f32[192,256]{1,0:T(8,128)S(1)} %get-tuple-element.180), channel_id=1, source_target_pairs={{0,3},{1,0},{2,1},{3,2},{4,7},{5,4},{6,5},{7,6},{8,11},{9,8},{10,9... | collective-permute-start | bytes 589832 | tf_op jit(solution)/shard_map/ppermute | solution.py:55
  381.4 15.1 %collective-permute-start.94 = (f32[192,256]{1,0:T(8,128)S(1)}, f32[192,256]{1,0:T(8,128)S(1)}, u32[]{:S(2)}, u32[]{:S(2)}) collective-permute-start(f32[192,256]{1,0:T(8,128)S(1)} %get-tuple-element.181), channel_id=1, source_target_pairs={{0,1},{1,2},{2,3},{3,0},{4,5},{5,6},{6,7},{7,4},{8,9},{9,10},{10,1... | collective-permute-start | bytes 589832 | tf_op jit(solution)/shard_map/ppermute | solution.py:55
  381.4 15.1 %collective-permute-start.95 = (f32[192,256]{1,0:T(8,128)S(1)}, f32[192,256]{1,0:T(8,128)S(1)}, u32[]{:S(2)}, u32[]{:S(2)}) collective-permute-start(f32[192,256]{1,0:T(8,128)S(1)} %get-tuple-element.182), channel_id=1, source_target_pairs={{0,2},{1,3},{2,0},{3,1},{4,6},{5,7},{6,4},{7,5},{8,10},{9,11},{10,... | collective-permute-start | bytes 589832 | tf_op jit(solution)/shard_map/ppermute | solution.py:55
  407.1 24.1 %collective-permute-start.101 = (f32[768,256]{1,0:T(8,128)S(1)}, f32[768,256]{1,0:T(8,128)}, u32[]{:S(2)}, u32[]{:S(2)}) collective-permute-start(f32[768,256]{1,0:T(8,128)S(1)} %shard_map.133.refs_0_), channel_id=1, source_target_pairs={{0,2},{1,3},{2,0},{3,1},{4,6},{5,7},{6,4},{7,5},{8,10},{9,11},{10,... | collective-permute-start | bytes 2359304 | tf_op jit(solution)/shard_map/ppermute | solution.py:55
  407.2 24.0 %collective-permute-start.100 = (f32[768,256]{1,0:T(8,128)S(1)}, f32[768,256]{1,0:T(8,128)}, u32[]{:S(2)}, u32[]{:S(2)}) collective-permute-start(f32[768,256]{1,0:T(8,128)S(1)} %shard_map.133.refs_0_), channel_id=1, source_target_pairs={{0,3},{1,0},{2,1},{3,2},{4,7},{5,4},{6,5},{7,6},{8,11},{9,8},{10,9... | collective-permute-start | bytes 2359304 | tf_op jit(solution)/shard_map/ppermute | solution.py:55
  407.3 23.9 %collective-permute-start.99 = (f32[768,256]{1,0:T(8,128)S(1)}, f32[768,256]{1,0:T(8,128)}, u32[]{:S(2)}, u32[]{:S(2)}) collective-permute-start(f32[768,256]{1,0:T(8,128)S(1)} %shard_map.133.refs_0_), channel_id=1, source_target_pairs={{0,1},{1,2},{2,3},{3,0},{4,5},{5,6},{6,7},{7,4},{8,9},{9,10},{10,1... | collective-permute-start | bytes 2359304 | tf_op jit(solution)/shard_map/ppermute | solution.py:55
  410.5 20.7 %all-to-all-start = ((f32[16,16,192]{2,1,0:T(8,128)}), f32[16,16,192]{2,1,0:T(8,128)}, u32[]{:S(2)}, u32[]{:S(2)}) async-start(f32[16,16,192]{2,1,0:T(8,128)} %bitcast.15), calls=%async_computation | async-start | bytes 524288 | tf_op jit(solution)/shard_map/all_to_all | solution.py:424
  (105 other events, 815.8 us)

commit v5 on v4

--- a/solution.py
+++ b/solution.py
@@ -12,6 +12,7 @@
 RING = 4
 K = 256
 PANEL = 32
+STEP = 16
 ORDER = (0, 1, 3, 2)
 HIGH = lax.Precision.HIGHEST
 F32 = jnp.float32
@@ -90,6 +91,11 @@
     return high, mid, (rest - mid.astype(F32)).astype(BF16)
 
 
+def split2(value):
+    high = value.astype(BF16)
+    return high, (value - high.astype(F32)).astype(BF16)
+
+
 def pieces_kernel(side, pos_ref, a_ref, basis_ref, *o_refs):
     at, cross = pos_ref[PLACE[side]], pos_ref[PLACE[CROSS[side]]]
     for o_ref, d in zip(o_refs, ORDER):
@@ -118,7 +124,7 @@
     before, (turned_ref, *o_refs) = refs[: -5 if last else -2], refs[-5 if last else -2 :]
     turned = piece_ref[:768, :].astype(BF16)
     turned_ref[...] = turned
-    parts = split3(piece_ref[768:, :])
+    parts = split2(piece_ref[768:, :])
     total = sum(jnp.dot(turned, part, preferred_element_type=F32) for part in reversed(parts))
     for r in before:
         total = r[...] + total
@@ -163,11 +169,17 @@
     ]
 
 
-def project_kernel(side, pos_ref, a0, a1, a2, a3, top_ref, low_ref, *refs):
-    *o_refs, m_ref = refs
-    m_ref[:512, :] = top_ref[...]
-    m_ref[512:, :] = low_ref[...]
-    parts = split3(jnp.concatenate([m_ref[at, :] for at in row_places(side, pos_ref)], axis=0))
+def place_chunks(side, pos_ref, chunks, m_ref):
+    for i, r in enumerate(chunks):
+        c = pos_ref[1] if i < 4 else 1 - pos_ref[1]
+        at = i // 4 * 512 + back(first_place(side, pos_ref, c), ORDER[i % 4]) * 128
+        m_ref[pl.ds(pl.multiple_of(at, 128), 128), :] = r[...]
+
+
+def project_kernel(side, pos_ref, a0, a1, a2, a3, *refs):
+    chunks, o_refs, m_ref = refs[:8], refs[8:12], refs[12]
+    place_chunks(side, pos_ref, chunks, m_ref)
+    parts = split2(jnp.concatenate([m_ref[at, :] for at in row_places(side, pos_ref)], axis=0))
     for j, o_ref in enumerate(o_refs):
         block = jnp.concatenate([a[j * 192 : j * 192 + 192, :] for a in (a0, a1, a2, a3)], axis=1)
         o_ref[...] = sum(
@@ -175,23 +187,28 @@
         )
 
 
-def project(side, pos, turned, top, low):
-    return call(functools.partial(project_kernel, side), [f32s(192, 256)] * 4, 7,
-                6 * 3072 << 16, 4 << 20, [pltpu.VMEM((1024, 256), F32)], smem=1)(
-        pos, *turned, top, low
-    )
-
-
-def gram_kernel(pos_ref, rows_ref, *refs):
-    mine = rows_ref[:, pl.ds(pl.multiple_of(pos_ref[1] * 128, 128), 128)]
-    total = lax.dot_general(mine, rows_ref[...], (((0,), (0,)), ((), ())), precision=HIGH,
+def project(side, pos, turned, chunks):
+    return call(functools.partial(project_kernel, side), [f32s(192, 256)] * 4, 13,
+                4 * 3072 << 16, 4 << 20, [pltpu.VMEM((1024, 256), F32)], smem=1)(
+        pos, *turned, *chunks
+    )
+
+
+def gram_kernel(pos_ref, *refs):
+    chunks, before, o_ref = refs[:4], refs[4:-1], refs[-1]
+    rows = jnp.concatenate([r[...] for r in chunks], axis=0)
+    at = pl.ds(pl.multiple_of(pos_ref[1] * 128, 128), 128)
+    mine = jnp.concatenate([r[:, at] for r in chunks], axis=0)
+    total = lax.dot_general(mine, rows, (((0,), (0,)), ((), ())), precision=HIGH,
                             preferred_element_type=F32)
-    refs[-1][...] = refs[0][...] + total if len(refs) == 2 else total
-
-
-def gram(pos, rows, *before):
-    return call(gram_kernel, f32s(128, 256), 2 + len(before), 12 << 24, 1 << 19, smem=1)(
-        pos, rows, *before
+    for r in before:
+        total = r[...] + total
+    o_ref[...] = total
+
+
+def gram(pos, chunks, *before):
+    return call(gram_kernel, f32s(128, 256), 5 + len(before), 12 << 24, 1 << 19, smem=1)(
+        pos, *chunks, *before
     )
 
 
@@ -201,15 +218,15 @@
     lane = lax.broadcasted_iota(jnp.int32, (n, 128), 1)
     half, base = at // 128, at % 128
     columns = [
-        jnp.broadcast_to(tall[:, at + k : at + k + 1], (n, 128)) for k in range(8)
+        jnp.broadcast_to(tall[:, at + k : at + k + 1], (n, 128)) for k in range(STEP)
     ]
     sides = [tall[:, :128], tall[:, 128:]]
-    pivots = jnp.ones((8, 128), F32)
-    for j in range(8):
+    pivots = jnp.ones((STEP, 128), F32)
+    for j in range(STEP):
         pivot = columns[j][j : j + 1, :]
         times = jnp.where(sub > j, columns[j], 0.0) * (1.0 / pivot)
-        pivots = jnp.where(sub[:8] == j, pivot, pivots)
-        for k in range(j + 1, 8):
+        pivots = jnp.where(sub[:STEP] == j, pivot, pivots)
+        for k in range(j + 1, STEP):
             columns[k] = columns[k] - times * columns[k][j : j + 1, :]
         here = lane == base + j
         kept = jnp.where(here & (sub >= j), jnp.where(sub == j, 1.0, 0.0), sides[half])
@@ -219,32 +236,43 @@
     return jnp.concatenate(sides, axis=1), pivots
 
 
+def narrow_product(left, right):
+    left, right = split3(left), split3(right)
+    order = ((2, 0), (0, 2), (1, 1), (1, 0), (0, 1), (0, 0))
+    return lax.dot_general(
+        jnp.concatenate([left[i] for i, j in order], axis=0),
+        jnp.concatenate([right[j] for i, j in order], axis=0),
+        (((0,), (0,)), ((), ())),
+        preferred_element_type=F32,
+    )
+
+
 def inverse_kernel(pos_ref, mine_ref, mate_ref, o_ref, w_ref):
     for c, ref in ((pos_ref[1], mine_ref), (1 - pos_ref[1], mate_ref)):
         w_ref[pl.ds(pl.multiple_of(c * 128, 128), 128), :] = ref[...]
     lane = lax.broadcasted_iota(jnp.int32, (PANEL, K), 1)
     row = lax.broadcasted_iota(jnp.int32, (PANEL, K), 0)
-    all_lane = lax.broadcasted_iota(jnp.int32, (K, K), 1)
-    all_row = lax.broadcasted_iota(jnp.int32, (K, K), 0)
     for lo in range(0, K, PANEL):
         hi = lo + PANEL
         rest = w_ref[lo:hi, :]
         done, pivots = [], []
-        for at in range(lo, hi, 8):
+        for at in range(lo, hi, STEP):
             rest, found = eliminate(rest, at)
-            done.append(rest[:8])
+            done.append(rest[:STEP])
             pivots.append(found)
-            rest = rest[8:]
+            rest = rest[STEP:]
         r = jnp.concatenate(done, axis=0)
         pivots = jnp.concatenate(pivots, axis=0)
         pivots = jnp.concatenate([pivots, pivots], axis=1)
         clean = jnp.where((lane < hi) & (lane > row + lo), 0.0, r)
         o_ref[lo:hi, :] = jnp.where(lane <= row + lo, clean, 0.0) * lax.rsqrt(pivots)
         if hi < K:
-            times = jnp.where(lane >= hi, r, 0.0) / pivots
-            change = jnp.dot(times.T, clean, precision=HIGH, preferred_element_type=F32)
-            gone = (all_lane >= lo) & (all_lane < hi) & (all_row >= hi)
-            w_ref[...] = jnp.where(gone, 0.0, w_ref[...]) - change
+            start = hi // 128 * 128
+            change = narrow_product((r / pivots)[:, start:], clean)
+            rows = w_ref[hi:, :]
+            lanes = lax.broadcasted_iota(jnp.int32, rows.shape, 1)
+            kept = jnp.where((lanes >= lo) & (lanes < hi), 0.0, rows)
+            w_ref[hi:, :] = kept - change[hi - start :]
 
 
 def inverse_factor(pos, mine, mate):
@@ -295,66 +323,55 @@
 def product(factors, at, blocks):
     a = jnp.concatenate([f[:, at : at + 384] for f in factors], axis=0)
     b = jnp.concatenate([b[...] for b in blocks], axis=0)
-    return sum(jnp.dot(a, part, preferred_element_type=F32) for part in reversed(split3(b)))
+    return sum(jnp.dot(a, part, preferred_element_type=F32) for part in reversed(split2(b)))
 
 
 def early_kernel(a0, a1, a2, a3, b0, b1, o_ref):
     o_ref[...] = product((a0, a1, a2, a3), 0, (b0, b1))
 
 
-def late_kernel(side, pos_ref, a0, a1, a2, a3, b2, b3, part_ref, keep_ref, send_ref, m_ref):
+def late_kernel(side, pos_ref, a0, a1, a2, a3, b2, b3, part_ref, *refs):
+    o_refs, m_ref = refs[:8], refs[8]
     total = part_ref[...] + product((a0, a1, a2, a3), 384, (b2, b3))
     for i, at in enumerate(row_places(side, pos_ref)):
         m_ref[at, :] = total[i * 256 : i * 256 + 256]
-    keep_ref[...] = m_ref[:512, :]
-    send_ref[...] = m_ref[512:, :]
+    for i, o_ref in enumerate(o_refs):
+        c = pos_ref[1] if i < 4 else 1 - pos_ref[1]
+        at = i // 4 * 512 + back(first_place(side, pos_ref, c), ORDER[i % 4]) * 128
+        o_ref[...] = m_ref[pl.ds(pl.multiple_of(at, 128), 128), :]
 
 
 def update(side, pos, straight, blocks):
-    part = call(early_kernel, f32s(1024, 256), 6, 3 * 3072 << 16, 3 << 20)(*straight, *blocks[:2])
-    return call(functools.partial(late_kernel, side), [f32s(512, 256)] * 2, 8, 3 * 3072 << 16,
+    part = call(early_kernel, f32s(1024, 256), 6, 2 * 3072 << 16, 3 << 20)(*straight, *blocks[:2])
+    return call(functools.partial(late_kernel, side), [f32s(128, 256)] * 8, 8, 2 * 3072 << 16,
                 3 << 20, [pltpu.VMEM((1024, 256), F32)], smem=1)(
         pos, *straight, *blocks[2:], part
     )
 
 
-def first_place(side, pos_ref):
-    return jnp.where(pos_ref[1] == 0, pos_ref[0], pos_ref[PLACE[side]])
-
-
-def split_kernel(side, pos_ref, keep_ref, other_ref, *o_refs):
-    for o_ref, d in zip(o_refs, ORDER):
-        at = pl.multiple_of(back(first_place(side, pos_ref), d) * 128, 128)
-        o_ref[...] = keep_ref[pl.ds(at, 128), :] + other_ref[pl.ds(at, 128), :]
-
-
-def merge_kernel(side, pos_ref, *refs):
-    for r, d in zip(refs[:-1], ORDER):
-        at = pl.multiple_of(back(first_place(side, pos_ref), d) * 128, 128)
-        refs[-1][pl.ds(at, 128), :] = r[...]
-
-
-def add_up(side, pos, keep, other):
-    chunks = call(functools.partial(split_kernel, side), [f32s(128, 256)] * 4, 3, 0, 2 << 20,
-                  smem=1)(pos, keep, send(other, "core"))
+def first_place(side, pos_ref, c):
+    return jnp.where(c == 0, pos_ref[0], pos_ref[PLACE[side]])
+
+
+def add_up(side, chunks):
+    chunks = [mine + send(other, "core") for mine, other in zip(chunks[:4], chunks[4:])]
     chunk = sum(deliver(chunks, "x" + side))
     chunk = sum(exchange(chunk, side + "x"))
-    return call(functools.partial(merge_kernel, side), f32s(512, 256), 5, 0, 1 << 20, smem=1)(
-        pos, *exchange(chunk, "x" + side)
-    )
-
-
-def basis_kernel(side, pos_ref, top_ref, low_ref, linv_ref, o_ref):
-    p = block_place(pos_ref, pos_ref[PLACE[side]])
-    at = pl.ds(pl.multiple_of(lax.rem(p, 2) * 256, 256), 256)
-    rows = jnp.where(p < 2, top_ref[at, :], low_ref[at, :])
+    return exchange(chunk, "x" + side)
+
+
+def basis_kernel(side, pos_ref, *refs):
+    chunks, linv_ref, o_ref, m_ref = refs[:8], refs[8], refs[9], refs[10]
+    place_chunks(side, pos_ref, chunks, m_ref)
+    at = block_place(pos_ref, pos_ref[PLACE[side]]) * 256
+    rows = m_ref[pl.ds(pl.multiple_of(at, 256), 256), :]
     o_ref[...] = lax.dot_general(rows, linv_ref[...], (((1,), (1,)), ((), ())), precision=HIGH,
                                  preferred_element_type=F32)
 
 
-def basis_of(side, pos, top, low, linv):
-    return call(functools.partial(basis_kernel, side), f32s(256, 256), 4, 12 << 24, 1 << 20,
-                smem=1)(pos, top, low, linv)
+def basis_of(side, pos, chunks, linv):
+    return call(functools.partial(basis_kernel, side), f32s(256, 256), 10, 12 << 24, 1 << 20,
+                [pltpu.VMEM((1024, 256), F32)], smem=1)(pos, *chunks, linv)
 
 
 def cores_kernel(pos_ref, p_ref, *refs):
@@ -385,11 +402,11 @@
 
 def refit(side, pos, straight, turned, coupling):
     cross = CROSS[side] * 2
-    half = add_up(side, pos, *update(side, pos, straight, exchange(coupling, cross)))
-    rest = send(half, "core")
+    half = add_up(side, update(side, pos, straight, exchange(coupling, cross)))
+    rest = [send(chunk, "core") for chunk in half]
     piece = sum(exchange(gram(pos, rest, gram(pos, half)), cross))
-    pieces = deliver(project(side, pos, turned, half, rest), cross)
-    return half, rest, inverse_factor(pos, piece, send(piece, "core")), pieces
+    pieces = deliver(project(side, pos, turned, half + rest), cross)
+    return half + rest, inverse_factor(pos, piece, send(piece, "core")), pieces
 
 
 def column_scale(ranks):
@@ -416,15 +433,15 @@
 
     step = call(next_kernel, [side] * 2, 7, 1 << 29, 3 << 20)
     for sweep in range(ITERS):
-        top, low, linv, pieces = refit(LEFT, pos, up, up_turned, coupling)
+        chunks, linv, pieces = refit(LEFT, pos, up, up_turned, coupling)
         if sweep == ITERS - 1:
-            left = basis_of(LEFT, pos, top, low, linv)
+            left = basis_of(LEFT, pos, chunks, linv)
         coupling, p = step(*pieces, linv, scale, q)
         if sweep == ITERS - 1:
             p_rows = lax.all_to_all(p.T.reshape(16, 16, 192), "row", 0, 0)
-        top, low, linv, pieces = refit(RIGHT, pos, down, down_turned, coupling)
+        chunks, linv, pieces = refit(RIGHT, pos, down, down_turned, coupling)
         if sweep == ITERS - 1:
-            right = basis_of(RIGHT, pos, top, low, linv)
+            right = basis_of(RIGHT, pos, chunks, linv)
             q = call(last_kernel, side, 6, 1 << 28, 2 << 20)(*pieces, linv, scale)
         else:
             coupling, q = step(*pieces, linv, scale, p)

time: 445 us -> 416 us (0.935)
  the two profiles are of different devices: /device:TPU:1 before, /device:TPU:0 now
where the time goes in v5:
time: 416 us; the launch traced here: 408 us
  waiting for transfers between devices  160 us (38%)
  starting transfers between devices  143 us (34%)
  Pallas kernels  75.2 us (18%)
  local copies, waits for them, and re-layouts  26.8 us (6%)
    ppermute x126, waiting for transfers between devices, send(): return lax.ppermute(value, ('adapter', 'row'), perm)  160 us
    ppermute x126, starting transfers between devices, send(): return lax.ppermute(value, ('adapter', 'row'), perm)  138 us
    pallas_call x4, Pallas kernels, inverse_factor(): call(inverse_kernel, f32s(K, K), 3, 0, 1 << 10, [pltpu.VMEM((K, K), F32)]...  27.1 us
    unnamed x122, local copies, waits for them, and re-layouts  22.5 us
  transfers between devices with their start and end apart: 127, of which 64 were waited for; matrix products, arithmetic and copies ran while one was open for 0% of the time, Pallas kernels for 13%

profile of v5, /device:TPU:0, one launch (start us, length us, event | category | flops | bytes accessed | tf_op | source)
XLA Modules:
  0.0 408.1 jit_solution(14145139044393761329)
XLA Ops:
  12.2 3.6 collective-permute-start.5
  16.8 17.4 %collective-permute-done.2.piece_ref = f32[1024,256]{1,0:T(8,128)S(1)} collective-permute-done((f32[1024,256]{1,0:T(8,128)S(1)}, f32[1024,256]{1,0:T(8,128)S(1)}, u32[]{:S(2)}, u32[]{:S(2)}) %collective-permute-start.2) | collective-permute-done | bytes 1048608 | tf_op jit(solution)/shard_map/ppermute | solution.py:56
  34.2 3.2 collective-permute-start.3
  42.4 15.5 %collective-permute-done.5.piece_ref = f32[1024,256]{1,0:T(8,128)S(1)} collective-permute-done((f32[1024,256]{1,0:T(8,128)S(1)}, f32[1024,256]{1,0:T(8,128)S(1)}, u32[]{:S(2)}, u32[]{:S(2)}) %collective-permute-start.5) | collective-permute-done | bytes 1048608 | tf_op jit(solution)/shard_map/ppermute | solution.py:56
  74.5 6.4 %collective-permute-start.7 = (f32[192,256]{1,0:T(8,128)}, f32[192,256]{1,0:T(8,128)}, u32[]{:S(2)}, u32[]{:S(2)}) collective-permute-start(f32[192,256]{1,0:T(8,128)} %get-tuple-element.137), channel_id=1, source_target_pairs={{0,4},{1,5},{2,6},{3,7},{4,8},{5,9},{6,10},{7,11},{8,12},{9,13},{1... | collective-permute-start | bytes 589832 | tf_op jit(solution)/shard_map/ppermute | solution.py:56
  80.9 5.2 %collective-permute-start.8 = (f32[192,256]{1,0:T(8,128)}, f32[192,256]{1,0:T(8,128)}, u32[]{:S(2)}, u32[]{:S(2)}) collective-permute-start(f32[192,256]{1,0:T(8,128)} %get-tuple-element.138), channel_id=1, source_target_pairs={{0,8},{1,9},{2,10},{3,11},{4,12},{5,13},{6,14},{7,15},{8,0},{9,1},... | collective-permute-start | bytes 589832 | tf_op jit(solution)/shard_map/ppermute | solution.py:56
  88.6 7.5 %collective-permute-done.8.refs_3_ = f32[192,256]{1,0:T(8,128)} collective-permute-done((f32[192,256]{1,0:T(8,128)}, f32[192,256]{1,0:T(8,128)}, u32[]{:S(2)}, u32[]{:S(2)}) %collective-permute-start.8) | collective-permute-done | bytes 196640 | tf_op jit(solution)/shard_map/ppermute | solution.py:56
  99.5 3.6 collective-permute-start.12
  117.5 5.1 %collective-permute-done.19 = f32[128,256]{1,0:T(8,128)S(1)} collective-permute-done((f32[128,256]{1,0:T(8,128)S(1)}, f32[128,256]{1,0:T(8,128)S(1)}, u32[]{:S(2)}, u32[]{:S(2)}) %collective-permute-start.19) | collective-permute-done | bytes 131104 | tf_op jit(solution)/shard_map/ppermute | solution.py:56
  136.2 3.1 collective-permute-done.27.refs_3_
  156.3 6.8 %shard_map.100.refs_4_ = f32[256,256]{1,0:T(8,128)S(1)} custom-call(s32[4]{0:T(128)S(1)} %pad_add_fusion.pos_ref, f32[128,256]{1,0:T(8,128)S(1)} %add_add_fusion.9.mine_ref, f32[128,256]{1,0:T(8,128)S(1)} %collective-permute-done.38.mate_ref), custom_call_target="tpu_custom_call" | custom-call | bytes 1024 | tf_op jit(solution)/shard_map/pallas_call | solution.py:279
  168.9 8.0 %collective-permute-done.41.b1 = f32[192,256]{1,0:T(8,128)S(1)} collective-permute-done((f32[192,256]{1,0:T(8,128)S(1)}, f32[192,256]{1,0:T(8,128)S(1)}, u32[]{:S(2)}, u32[]{:S(2)}) %collective-permute-start.41) | collective-permute-done | bytes 196640 | tf_op jit(solution)/shard_map/ppermute | solution.py:56
  185.4 4.3 %collective-permute-done.46 = f32[128,256]{1,0:T(8,128)S(1)} collective-permute-done((f32[128,256]{1,0:T(8,128)S(1)}, f32[128,256]{1,0:T(8,128)S(1)}, u32[]{:S(2)}, u32[]{:S(2)}) %collective-permute-start.46) | collective-permute-done | bytes 131104 | tf_op jit(solution)/shard_map/ppermute | solution.py:56
  190.9 3.1 collective-permute-start.50
  197.2 3.0 collective-permute-done.49
  203.7 3.3 collective-permute-done.54.refs_3_
  216.2 3.0 collective-permute-start.59
  223.2 6.8 %shard_map.107.refs_4_ = f32[256,256]{1,0:T(8,128)S(1)} custom-call(s32[4]{0:T(128)S(1)} %pad_add_fusion.pos_ref, f32[128,256]{1,0:T(8,128)S(1)} %add_add_fusion.6.mine_ref, f32[128,256]{1,0:T(8,128)S(1)} %collective-permute-done.65.mate_ref), custom_call_target="tpu_custom_call" | custom-call | bytes 1024 | tf_op jit(solution)/shard_map/pallas_call | solution.py:279
  235.7 8.1 %collective-permute-done.68.b1 = f32[192,256]{1,0:T(8,128)S(1)} collective-permute-done((f32[192,256]{1,0:T(8,128)S(1)}, f32[192,256]{1,0:T(8,128)S(1)}, u32[]{:S(2)}, u32[]{:S(2)}) %collective-permute-start.68) | collective-permute-done | bytes 196640 | tf_op jit(solution)/shard_map/ppermute | solution.py:56
  252.4 4.3 %collective-permute-done.73 = f32[128,256]{1,0:T(8,128)S(1)} collective-permute-done((f32[128,256]{1,0:T(8,128)S(1)}, f32[128,256]{1,0:T(8,128)S(1)}, u32[]{:S(2)}, u32[]{:S(2)}) %collective-permute-start.73) | collective-permute-done | bytes 131104 | tf_op jit(solution)/shard_map/ppermute | solution.py:56
  258.0 3.1 collective-permute-start.77
  264.2 3.2 collective-permute-done.76
  292.2 6.8 %shard_map.113.refs_8_.refs_4_ = f32[256,256]{1,0:T(8,128)S(1)} custom-call(s32[4]{0:T(128)S(1)} %pad_add_fusion.pos_ref, f32[128,256]{1,0:T(8,128)S(1)} %add_add_fusion.3.mine_ref, f32[128,256]{1,0:T(8,128)S(1)} %collective-permute-done.89.mate_ref), custom_call_target="tpu_custom_call" | custom-call | bytes 1024 | tf_op jit(solution)/shard_map/pallas_call | solution.py:279
  303.9 8.8 %collective-permute-done.95.b1 = f32[192,256]{1,0:T(8,128)S(1)} collective-permute-done((f32[192,256]{1,0:T(8,128)S(1)}, f32[192,256]{1,0:T(8,128)S(1)}, u32[]{:S(2)}, u32[]{:S(2)}) %collective-permute-start.95) | collective-permute-done | bytes 196640 | tf_op jit(solution)/shard_map/ppermute | solution.py:56
  321.4 4.4 %collective-permute-done.100 = f32[128,256]{1,0:T(8,128)S(1)} collective-permute-done((f32[128,256]{1,0:T(8,128)S(1)}, f32[128,256]{1,0:T(8,128)S(1)}, u32[]{:S(2)}, u32[]{:S(2)}) %collective-permute-start.100) | collective-permute-done | bytes 131104 | tf_op jit(solution)/shard_map/ppermute | solution.py:56
  326.7 3.2 collective-permute-start.104
  353.5 3.0 collective-permute-start.117
  360.5 6.8 %shard_map.121.refs_8_.refs_4_ = f32[256,256]{1,0:T(8,128)S(1)} custom-call(s32[4]{0:T(128)S(1)} %pad_add_fusion.pos_ref, f32[128,256]{1,0:T(8,128)S(1)} %add_add_fusion.mine_ref, f32[128,256]{1,0:T(8,128)S(1)} %collective-permute-done.116.mate_ref), custom_call_target="tpu_custom_call" | custom-call | bytes 1024 | tf_op jit(solution)/shard_map/pallas_call | solution.py:279
  370.5 5.2 %collective-permute-done.122.b3 = f32[192,256]{1,0:T(8,128)S(1)} collective-permute-done((f32[192,256]{1,0:T(8,128)S(1)}, f32[192,256]{1,0:T(8,128)S(1)}, u32[]{:S(2)}, u32[]{:S(2)}) %collective-permute-start.122) | collective-permute-done | bytes 196640 | tf_op jit(solution)/shard_map/ppermute | solution.py:56
  378.4 3.1 collective-permute-start.124
  382.6 4.6 %all-to-all-start = ((f32[16,16,192]{2,1,0:T(8,128)}), f32[16,16,192]{2,1,0:T(8,128)S(1)}, u32[]{:S(2)}, u32[]{:S(2)}) async-start(f32[16,16,192]{2,1,0:T(8,128)} %bitcast.15), calls=%async_computation | async-start | bytes 524288 | tf_op jit(solution)/shard_map/all_to_all | solution.py:441
  403.3 4.4 %shard_map.126 = f32[192,16,256]{2,1,0:T(8,128)} custom-call(s32[4]{0:T(128)S(1)} %pad_add_fusion.pos_ref, f32[16,16,192]{2,1,0:T(8,128)S(1)} %all-to-all-done.p_ref, f32[768,256]{1,0:T(8,128)S(1)} %shard_map.125.refs_0_, f32[768,256]{1,0:T(8,128)} %collective-permute-done.123.refs_1_, f32[768,256]{1,0:T(8,128)S(1)} %collective-permute-done.124.refs_2_, ...), custom_call_target="tpu_custom_call" | custom-call | flops 1073741824 | bytes 6291456 | tf_op jit(solution)/shard_map/pallas_call | solution.py:448
  (426 shorter events, 227.6 us)
Async XLA Ops:
  6.9 27.3 %collective-permute-start.2 = (f32[1024,256]{1,0:T(8,128)S(1)}, f32[1024,256]{1,0:T(8,128)S(1)}, u32[]{:S(2)}, u32[]{:S(2)}) collective-permute-start(f32[1024,256]{1,0:T(8,128)S(1)} %get-tuple-element.113), channel_id=1, source_target_pairs={{0,4},{1,5},{2,6},{3,7},{4,8},{5,9},{6,10},{7,11},{8,12},{9,13},{1... | collective-permute-start | bytes 3145736 | tf_op jit(solution)/shard_map/ppermute | solution.py:56
  8.9 30.7 %collective-permute-start = (f32[1024,256]{1,0:T(8,128)S(1)}, f32[1024,256]{1,0:T(8,128)S(1)}, u32[]{:S(2)}, u32[]{:S(2)}) collective-permute-start(f32[1024,256]{1,0:T(8,128)S(1)} %get-tuple-element.110), channel_id=1, source_target_pairs={{0,1},{1,2},{2,3},{3,0},{4,5},{5,6},{6,7},{7,4},{8,9},{9,10},{10,1... | collective-permute-start | bytes 3145736 | tf_op jit(solution)/shard_map/ppermute | solution.py:56
  10.5 29.6 %collective-permute-start.1 = (f32[1024,256]{1,0:T(8,128)S(1)}, f32[1024,256]{1,0:T(8,128)S(1)}, u32[]{:S(2)}, u32[]{:S(2)}) collective-permute-start(f32[1024,256]{1,0:T(8,128)S(1)} %get-tuple-element.111), channel_id=1, source_target_pairs={{0,3},{1,0},{2,1},{3,2},{4,7},{5,4},{6,5},{7,6},{8,11},{9,8},{10,9... | collective-permute-start | bytes 3145736 | tf_op jit(solution)/shard_map/ppermute | solution.py:56
  12.2 45.7 %collective-permute-start.5 = (f32[1024,256]{1,0:T(8,128)S(1)}, f32[1024,256]{1,0:T(8,128)S(1)}, u32[]{:S(2)}, u32[]{:S(2)}) collective-permute-start(f32[1024,256]{1,0:T(8,128)S(1)} %get-tuple-element.123), channel_id=1, source_target_pairs={{0,8},{1,9},{2,10},{3,11},{4,12},{5,13},{6,14},{7,15},{8,0},{9,1},... | collective-permute-start | bytes 3145736 | tf_op jit(solution)/shard_map/ppermute | solution.py:56
  15.7 44.4 %collective-permute-start.4 = (f32[1024,256]{1,0:T(8,128)S(1)}, f32[1024,256]{1,0:T(8,128)S(1)}, u32[]{:S(2)}, u32[]{:S(2)}) collective-permute-start(f32[1024,256]{1,0:T(8,128)S(1)} %get-tuple-element.120), channel_id=1, source_target_pairs={{0,12},{1,13},{2,14},{3,15},{4,0},{5,1},{6,2},{7,3},{8,4},{9,5},{1... | collective-permute-start | bytes 3145736 | tf_op jit(solution)/shard_map/ppermute | solution.py:56
  34.2 32.8 %collective-permute-start.3 = (f32[1024,256]{1,0:T(8,128)}, f32[1024,256]{1,0:T(8,128)}, u32[]{:S(2)}, u32[]{:S(2)}) collective-permute-start(f32[1024,256]{1,0:T(8,128)} %get-tuple-element.114), channel_id=1, source_target_pairs={{0,2},{1,3},{2,0},{3,1},{4,6},{5,7},{6,4},{7,5},{8,10},{9,11},{10,... | collective-permute-start | bytes 3145736 | tf_op jit(solution)/shard_map/ppermute | solution.py:56
  63.0 17.9 %collective-permute-start.9 = (f32[192,256]{1,0:T(8,128)}, f32[192,256]{1,0:T(8,128)}, u32[]{:S(2)}, u32[]{:S(2)}) collective-permute-start(f32[192,256]{1,0:T(8,128)} %get-tuple-element.140), channel_id=1, source_target_pairs={{0,3},{1,0},{2,1},{3,2},{4,7},{5,4},{6,5},{7,6},{8,11},{9,8},{10,9... | collective-permute-start | bytes 589832 | tf_op jit(solution)/shard_map/ppermute | solution.py:56
  64.7 21.5 %collective-permute-start.10 = (f32[192,256]{1,0:T(8,128)}, f32[192,256]{1,0:T(8,128)}, u32[]{:S(2)}, u32[]{:S(2)}) collective-permute-start(f32[192,256]{1,0:T(8,128)} %copy-done.55), channel_id=1, source_target_pairs={{0,1},{1,2},{2,3},{3,0},{4,5},{5,6},{6,7},{7,4},{8,9},{9,10},{10,1... | collective-permute-start | bytes 589832 | tf_op jit(solution)/shard_map/ppermute | solution.py:56
  65.1 21.2 %collective-permute-start.11 = (f32[192,256]{1,0:T(8,128)}, f32[192,256]{1,0:T(8,128)}, u32[]{:S(2)}, u32[]{:S(2)}) collective-permute-start(f32[192,256]{1,0:T(8,128)} %copy-done.54), channel_id=1, source_target_pairs={{0,2},{1,3},{2,0},{3,1},{4,6},{5,7},{6,4},{7,5},{8,10},{9,11},{10,... | collective-permute-start | bytes 589832 | tf_op jit(solution)/shard_map/ppermute | solution.py:56
  71.8 14.5 %collective-permute-start.6 = (f32[192,256]{1,0:T(8,128)}, f32[192,256]{1,0:T(8,128)}, u32[]{:S(2)}, u32[]{:S(2)}) collective-permute-start(f32[192,256]{1,0:T(8,128)} %get-tuple-element.136), channel_id=1, source_target_pairs={{0,12},{1,13},{2,14},{3,15},{4,0},{5,1},{6,2},{7,3},{8,4},{9,5},{1... | collective-permute-start | bytes 589832 | tf_op jit(solution)/shard_map/ppermute | solution.py:56
  74.5 14.1 %collective-permute-start.7 = (f32[192,256]{1,0:T(8,128)}, f32[192,256]{1,0:T(8,128)}, u32[]{:S(2)}, u32[]{:S(2)}) collective-permute-start(f32[192,256]{1,0:T(8,128)} %get-tuple-element.137), channel_id=1, source_target_pairs={{0,4},{1,5},{2,6},{3,7},{4,8},{5,9},{6,10},{7,11},{8,12},{9,13},{1... | collective-permute-start | bytes 589832 | tf_op jit(solution)/shard_map/ppermute | solution.py:56
  80.9 15.2 %collective-permute-start.8 = (f32[192,256]{1,0:T(8,128)}, f32[192,256]{1,0:T(8,128)}, u32[]{:S(2)}, u32[]{:S(2)}) collective-permute-start(f32[192,256]{1,0:T(8,128)} %get-tuple-element.138), channel_id=1, source_target_pairs={{0,8},{1,9},{2,10},{3,11},{4,12},{5,13},{6,14},{7,15},{8,0},{9,1},... | collective-permute-start | bytes 589832 | tf_op jit(solution)/shard_map/ppermute | solution.py:56
  149.1 13.9 %collective-permute-start.32 = (f32[192,256]{1,0:T(8,128)S(1)}, f32[192,256]{1,0:T(8,128)S(1)}, u32[]{:S(2)}, u32[]{:S(2)}) collective-permute-start(f32[192,256]{1,0:T(8,128)S(1)} %get-tuple-element.153), channel_id=1, source_target_pairs={{0,12},{1,13},{2,14},{3,15},{4,0},{5,1},{6,2},{7,3},{8,4},{9,5},{1... | collective-permute-start | bytes 589832 | tf_op jit(solution)/shard_map/ppermute | solution.py:56
  164.6 12.3 %collective-permute-start.41 = (f32[192,256]{1,0:T(8,128)S(1)}, f32[192,256]{1,0:T(8,128)S(1)}, u32[]{:S(2)}, u32[]{:S(2)}) collective-permute-start(f32[192,256]{1,0:T(8,128)S(1)} %get-tuple-element.157.b0), channel_id=1, source_target_pairs={{0,1},{1,2},{2,3},{3,0},{4,5},{5,6},{6,7},{7,4},{8,9},{9,10},{10,1... | collective-permute-start | bytes 589832 | tf_op jit(solution)/shard_map/ppermute | solution.py:56
  164.7 12.9 %collective-permute-start.40 = (f32[192,256]{1,0:T(8,128)S(1)}, f32[192,256]{1,0:T(8,128)S(1)}, u32[]{:S(2)}, u32[]{:S(2)}) collective-permute-start(f32[192,256]{1,0:T(8,128)S(1)} %get-tuple-element.157.b0), channel_id=1, source_target_pairs={{0,2},{1,3},{2,0},{3,1},{4,6},{5,7},{6,4},{7,5},{8,10},{9,11},{10,... | collective-permute-start | bytes 589832 | tf_op jit(solution)/shard_map/ppermute | solution.py:56
  216.2 13.8 %collective-permute-start.59 = (f32[192,256]{1,0:T(8,128)S(1)}, f32[192,256]{1,0:T(8,128)S(1)}, u32[]{:S(2)}, u32[]{:S(2)}) collective-permute-start(f32[192,256]{1,0:T(8,128)S(1)} %get-tuple-element.167), channel_id=1, source_target_pairs={{0,3},{1,0},{2,1},{3,2},{4,7},{5,4},{6,5},{7,6},{8,11},{9,8},{10,9... | collective-permute-start | bytes 589832 | tf_op jit(solution)/shard_map/ppermute | solution.py:56
  219.3 11.3 %collective-permute-start.60 = (f32[192,256]{1,0:T(8,128)S(1)}, f32[192,256]{1,0:T(8,128)S(1)}, u32[]{:S(2)}, u32[]{:S(2)}) collective-permute-start(f32[192,256]{1,0:T(8,128)S(1)} %get-tuple-element.168), channel_id=1, source_target_pairs={{0,1},{1,2},{2,3},{3,0},{4,5},{5,6},{6,7},{7,4},{8,9},{9,10},{10,1... | collective-permute-start | bytes 589832 | tf_op jit(solution)/shard_map/ppermute | solution.py:56
  231.9 11.9 %collective-permute-start.68 = (f32[192,256]{1,0:T(8,128)S(1)}, f32[192,256]{1,0:T(8,128)S(1)}, u32[]{:S(2)}, u32[]{:S(2)}) collective-permute-start(f32[192,256]{1,0:T(8,128)S(1)} %get-tuple-element.171.b0), channel_id=1, source_target_pairs={{0,4},{1,5},{2,6},{3,7},{4,8},{5,9},{6,10},{7,11},{8,12},{9,13},{1... | collective-permute-start | bytes 589832 | tf_op jit(solution)/shard_map/ppermute | solution.py:56
  232.0 12.5 %collective-permute-start.67 = (f32[192,256]{1,0:T(8,128)S(1)}, f32[192,256]{1,0:T(8,128)S(1)}, u32[]{:S(2)}, u32[]{:S(2)}) collective-permute-start(f32[192,256]{1,0:T(8,128)S(1)} %get-tuple-element.171.b0), channel_id=1, source_target_pairs={{0,8},{1,9},{2,10},{3,11},{4,12},{5,13},{6,14},{7,15},{8,0},{9,1},... | collective-permute-start | bytes 589832 | tf_op jit(solution)/shard_map/ppermute | solution.py:56
  285.1 13.9 %collective-permute-start.90 = (f32[192,256]{1,0:T(8,128)S(1)}, f32[192,256]{1,0:T(8,128)S(1)}, u32[]{:S(2)}, u32[]{:S(2)}) collective-permute-start(f32[192,256]{1,0:T(8,128)S(1)} %get-tuple-element.181), channel_id=1, source_target_pairs={{0,12},{1,13},{2,14},{3,15},{4,0},{5,1},{6,2},{7,3},{8,4},{9,5},{1... | collective-permute-start | bytes 589832 | tf_op jit(solution)/shard_map/ppermute | solution.py:56
  287.8 11.5 %collective-permute-start.91 = (f32[192,256]{1,0:T(8,128)S(1)}, f32[192,256]{1,0:T(8,128)S(1)}, u32[]{:S(2)}, u32[]{:S(2)}) collective-permute-start(f32[192,256]{1,0:T(8,128)S(1)} %get-tuple-element.182), channel_id=1, source_target_pairs={{0,4},{1,5},{2,6},{3,7},{4,8},{5,9},{6,10},{7,11},{8,12},{9,13},{1... | collective-permute-start | bytes 589832 | tf_op jit(solution)/shard_map/ppermute | solution.py:56
  287.8 11.4 %collective-permute-start.92 = (f32[192,256]{1,0:T(8,128)S(1)}, f32[192,256]{1,0:T(8,128)S(1)}, u32[]{:S(2)}, u32[]{:S(2)}) collective-permute-start(f32[192,256]{1,0:T(8,128)S(1)} %get-tuple-element.183), channel_id=1, source_target_pairs={{0,8},{1,9},{2,10},{3,11},{4,12},{5,13},{6,14},{7,15},{8,0},{9,1},... | collective-permute-start | bytes 589832 | tf_op jit(solution)/shard_map/ppermute | solution.py:56
  300.6 12.2 %collective-permute-start.95 = (f32[192,256]{1,0:T(8,128)S(1)}, f32[192,256]{1,0:T(8,128)S(1)}, u32[]{:S(2)}, u32[]{:S(2)}) collective-permute-start(f32[192,256]{1,0:T(8,128)S(1)} %get-tuple-element.185.b0), channel_id=1, source_target_pairs={{0,1},{1,2},{2,3},{3,0},{4,5},{5,6},{6,7},{7,4},{8,9},{9,10},{10,1... | collective-permute-start | bytes 589832 | tf_op jit(solution)/shard_map/ppermute | solution.py:56
  300.7 12.8 %collective-permute-start.94 = (f32[192,256]{1,0:T(8,128)S(1)}, f32[192,256]{1,0:T(8,128)S(1)}, u32[]{:S(2)}, u32[]{:S(2)}) collective-permute-start(f32[192,256]{1,0:T(8,128)S(1)} %get-tuple-element.185.b0), channel_id=1, source_target_pairs={{0,2},{1,3},{2,0},{3,1},{4,6},{5,7},{6,4},{7,5},{8,10},{9,11},{10,... | collective-permute-start | bytes 589832 | tf_op jit(solution)/shard_map/ppermute | solution.py:56
  301.5 11.9 %collective-permute-start.93 = (f32[192,256]{1,0:T(8,128)S(1)}, f32[192,256]{1,0:T(8,128)S(1)}, u32[]{:S(2)}, u32[]{:S(2)}) collective-permute-start(f32[192,256]{1,0:T(8,128)S(1)} %get-tuple-element.185.b0), channel_id=1, source_target_pairs={{0,3},{1,0},{2,1},{3,2},{4,7},{5,4},{6,5},{7,6},{8,11},{9,8},{10,9... | collective-permute-start | bytes 589832 | tf_op jit(solution)/shard_map/ppermute | solution.py:56
  353.5 13.7 %collective-permute-start.117 = (f32[192,256]{1,0:T(8,128)S(1)}, f32[192,256]{1,0:T(8,128)S(1)}, u32[]{:S(2)}, u32[]{:S(2)}) collective-permute-start(f32[192,256]{1,0:T(8,128)S(1)} %get-tuple-element.196), channel_id=1, source_target_pairs={{0,3},{1,0},{2,1},{3,2},{4,7},{5,4},{6,5},{7,6},{8,11},{9,8},{10,9... | collective-permute-start | bytes 589832 | tf_op jit(solution)/shard_map/ppermute | solution.py:56
  356.5 11.4 %collective-permute-start.118 = (f32[192,256]{1,0:T(8,128)S(1)}, f32[192,256]{1,0:T(8,128)S(1)}, u32[]{:S(2)}, u32[]{:S(2)}) collective-permute-start(f32[192,256]{1,0:T(8,128)S(1)} %get-tuple-element.197), channel_id=1, source_target_pairs={{0,1},{1,2},{2,3},{3,0},{4,5},{5,6},{6,7},{7,4},{8,9},{9,10},{10,1... | collective-permute-start | bytes 589832 | tf_op jit(solution)/shard_map/ppermute | solution.py:56
  356.6 11.4 %collective-permute-start.119 = (f32[192,256]{1,0:T(8,128)S(1)}, f32[192,256]{1,0:T(8,128)S(1)}, u32[]{:S(2)}, u32[]{:S(2)}) collective-permute-start(f32[192,256]{1,0:T(8,128)S(1)} %get-tuple-element.198), channel_id=1, source_target_pairs={{0,2},{1,3},{2,0},{3,1},{4,6},{5,7},{6,4},{7,5},{8,10},{9,11},{10,... | collective-permute-start | bytes 589832 | tf_op jit(solution)/shard_map/ppermute | solution.py:56
  377.8 25.5 %collective-permute-start.125 = (f32[768,256]{1,0:T(8,128)S(1)}, f32[768,256]{1,0:T(8,128)S(1)}, u32[]{:S(2)}, u32[]{:S(2)}) collective-permute-start(f32[768,256]{1,0:T(8,128)S(1)} %shard_map.125.refs_0_), channel_id=1, source_target_pairs={{0,2},{1,3},{2,0},{3,1},{4,6},{5,7},{6,4},{7,5},{8,10},{9,11},{10,... | collective-permute-start | bytes 2359304 | tf_op jit(solution)/shard_map/ppermute | solution.py:56
  378.4 24.9 %collective-permute-start.124 = (f32[768,256]{1,0:T(8,128)S(1)}, f32[768,256]{1,0:T(8,128)S(1)}, u32[]{:S(2)}, u32[]{:S(2)}) collective-permute-start(f32[768,256]{1,0:T(8,128)S(1)} %shard_map.125.refs_0_), channel_id=1, source_target_pairs={{0,3},{1,0},{2,1},{3,2},{4,7},{5,4},{6,5},{7,6},{8,11},{9,8},{10,9... | collective-permute-start | bytes 2359304 | tf_op jit(solution)/shard_map/ppermute | solution.py:56
  381.5 21.8 %collective-permute-start.123 = (f32[768,256]{1,0:T(8,128)S(1)}, f32[768,256]{1,0:T(8,128)}, u32[]{:S(2)}, u32[]{:S(2)}) collective-permute-start(f32[768,256]{1,0:T(8,128)S(1)} %shard_map.125.refs_0_), channel_id=1, source_target_pairs={{0,1},{1,2},{2,3},{3,0},{4,5},{5,6},{6,7},{7,4},{8,9},{9,10},{10,1... | collective-permute-start | bytes 2359304 | tf_op jit(solution)/shard_map/ppermute | solution.py:56
  382.6 20.7 %all-to-all-start = ((f32[16,16,192]{2,1,0:T(8,128)}), f32[16,16,192]{2,1,0:T(8,128)S(1)}, u32[]{:S(2)}, u32[]{:S(2)}) async-start(f32[16,16,192]{2,1,0:T(8,128)} %bitcast.15), calls=%async_computation | async-start | bytes 524288 | tf_op jit(solution)/shard_map/all_to_all | solution.py:441
  (156 other events, 1097.3 us)

commit v6 on v5

--- a/solution.py
+++ b/solution.py
@@ -144,8 +144,10 @@
 def lay_out(left, right):
     left, right = lax.optimization_barrier((left, right))
     right = deliver(right, RIGHT * 2, 1)
-    waiting, right[1] = lax.optimization_barrier((left[3], right[1]))
-    left = deliver([*left[:3], waiting], LEFT * 2, 1)
+    *left, waiting = left
+    left = deliver(left, LEFT * 2, 1)
+    waiting, left[1] = lax.optimization_barrier((waiting, left[1]))
+    left.append(send(waiting, LEFT * 2, ORDER[3]))
     turned = {LEFT: [], RIGHT: []}
     total = {LEFT: (), RIGHT: ()}
     for i in range(3):
@@ -177,9 +179,11 @@
 
 
 def project_kernel(side, pos_ref, a0, a1, a2, a3, *refs):
-    chunks, o_refs, m_ref = refs[:8], refs[8:12], refs[12]
+    chunks, o_refs, rows_ref, m_ref = refs[:8], refs[8:12], refs[12], refs[13]
     place_chunks(side, pos_ref, chunks, m_ref)
-    parts = split2(jnp.concatenate([m_ref[at, :] for at in row_places(side, pos_ref)], axis=0))
+    places = row_places(side, pos_ref)
+    rows_ref[...] = m_ref[places[0], :]
+    parts = split2(jnp.concatenate([m_ref[at, :] for at in places], axis=0))
     for j, o_ref in enumerate(o_refs):
         block = jnp.concatenate([a[j * 192 : j * 192 + 192, :] for a in (a0, a1, a2, a3)], axis=1)
         o_ref[...] = sum(
@@ -188,8 +192,8 @@
 
 
 def project(side, pos, turned, chunks):
-    return call(functools.partial(project_kernel, side), [f32s(192, 256)] * 4, 13,
-                4 * 3072 << 16, 4 << 20, [pltpu.VMEM((1024, 256), F32)], smem=1)(
+    return call(functools.partial(project_kernel, side), [f32s(192, 256)] * 4 + [f32s(256, 256)],
+                13, 4 * 3072 << 16, 4 << 20, [pltpu.VMEM((1024, 256), F32)], smem=1)(
         pos, *turned, *chunks
     )
 
@@ -360,34 +364,53 @@
     return exchange(chunk, "x" + side)
 
 
-def basis_kernel(side, pos_ref, *refs):
-    chunks, linv_ref, o_ref, m_ref = refs[:8], refs[8], refs[9], refs[10]
-    place_chunks(side, pos_ref, chunks, m_ref)
-    at = block_place(pos_ref, pos_ref[PLACE[side]]) * 256
-    rows = m_ref[pl.ds(pl.multiple_of(at, 256), 256), :]
-    o_ref[...] = lax.dot_general(rows, linv_ref[...], (((1,), (1,)), ((), ())), precision=HIGH,
-                                 preferred_element_type=F32)
-
-
-def basis_of(side, pos, chunks, linv):
-    return call(functools.partial(basis_kernel, side), f32s(256, 256), 10, 12 << 24, 1 << 20,
-                [pltpu.VMEM((1024, 256), F32)], smem=1)(pos, *chunks, linv)
+def basis_kernel(rows_ref, linv_ref, o_ref):
+    o_ref[...] = lax.dot_general(rows_ref[...], linv_ref[...], (((1,), (1,)), ((), ())),
+                                 precision=HIGH, preferred_element_type=F32)
+
+
+def basis_of(rows, linv):
+    return call(basis_kernel, f32s(256, 256), 2, 12 << 24, 1 << 20)(rows, linv)
 
 
 def cores_kernel(pos_ref, p_ref, *refs):
-    blocks, o_ref = refs[:4], refs[4]
+    blocks, o_ref, core_ref, sems = refs[:4], refs[4], refs[5], refs[6]
     mask = block_mask(192)
+    copies = []
     for i, first in enumerate(ORDER):
         for j, second in enumerate(ORDER):
             source = chunk_at(pos_ref, first, second)
             wide = jnp.where(mask, jnp.concatenate([p_ref[source]] * 12, axis=0), 0.0)
-            p_high, p_mid, unused = split3(wide)
-            q_high, q_mid, unused = split3(blocks[i][j * 192 : j * 192 + 192, :])
+            p_high, p_low = split2(wide)
+            q_high, q_low = split2(blocks[i][j * 192 : j * 192 + 192, :])
             core = sum(
                 jnp.dot(p, q, preferred_element_type=F32)
-                for p, q in ((p_mid, q_high), (p_high, q_mid), (p_high, q_high))
+                for p, q in ((p_low, q_high), (p_high, q_low), (p_high, q_high))
             )
-            o_ref[pl.ds(source * 12, 12)] = core.reshape(12, 16, 256)
+            at = i * RING + j
+            core_ref[at] = core.reshape(12, 16, 256)
+            copies.append(
+                pltpu.make_async_copy(
+                    core_ref.at[at], o_ref.at[pl.ds(source * 12, 12)], sems.at[at]
+                )
+            )
+            copies[-1].start()
+    for copy in copies:
+        copy.wait()
+
+
+def cores_of(pos, p_rows, blocks):
+    return pl.pallas_call(
+        cores_kernel,
+        out_shape=f32s(192, 16, 256),
+        in_specs=[SMEM] + [VMEM] * 5,
+        out_specs=pl.BlockSpec(memory_space=pl.ANY),
+        scratch_shapes=[
+            pltpu.VMEM((16, 12, 16, 256), F32), pltpu.SemaphoreType.DMA((16,))
+        ],
+        compiler_params=PARAMS,
+        cost_estimate=pl.CostEstimate(flops=1 << 30, bytes_accessed=6 << 20, transcendentals=0),
+    )(pos, p_rows, *blocks)
 
 
 def join_kernel(b0, b1, b2, b3, o_ref):
@@ -400,13 +423,16 @@
     return exchange(joined, "yz")
 
 
-def refit(side, pos, straight, turned, coupling):
+def refit(side, pos, straight, turned, coupling, beside=()):
     cross = CROSS[side] * 2
-    half = add_up(side, update(side, pos, straight, exchange(coupling, cross)))
+    *blocks, last = exchange(coupling, cross)
+    last, *beside = lax.optimization_barrier((last, *beside))
+    half = add_up(side, update(side, pos, straight, [*blocks, last]))
     rest = [send(chunk, "core") for chunk in half]
     piece = sum(exchange(gram(pos, rest, gram(pos, half)), cross))
-    pieces = deliver(project(side, pos, turned, half + rest), cross)
-    return half + rest, inverse_factor(pos, piece, send(piece, "core")), pieces
+    *pieces, rows = project(side, pos, turned, half + rest)
+    linv = inverse_factor(pos, piece, send(piece, "core"))
+    return rows, linv, deliver(pieces, cross), beside
 
 
 def column_scale(ranks):
@@ -432,23 +458,18 @@
     )
 
     step = call(next_kernel, [side] * 2, 7, 1 << 29, 3 << 20)
+    beside = ()
     for sweep in range(ITERS):
-        chunks, linv, pieces = refit(LEFT, pos, up, up_turned, coupling)
-        if sweep == ITERS - 1:
-            left = basis_of(LEFT, pos, chunks, linv)
+        rows, linv, pieces, unused = refit(LEFT, pos, up, up_turned, coupling)
         coupling, p = step(*pieces, linv, scale, q)
         if sweep == ITERS - 1:
+            beside = (basis_of(rows, linv),)
             p_rows = lax.all_to_all(p.T.reshape(16, 16, 192), "row", 0, 0)
-        chunks, linv, pieces = refit(RIGHT, pos, down, down_turned, coupling)
-        if sweep == ITERS - 1:
-            right = basis_of(RIGHT, pos, chunks, linv)
-            q = call(last_kernel, side, 6, 1 << 28, 2 << 20)(*pieces, linv, scale)
-        else:
+        rows, linv, pieces, beside = refit(RIGHT, pos, down, down_turned, coupling, beside)
+        if sweep < ITERS - 1:
             coupling, q = step(*pieces, linv, scale, p)
-    cores = call(cores_kernel, f32s(192, 16, 256), 6, 1 << 30, 6 << 20, smem=1)(
-        pos, p_rows, *gather_all(q)
-    )
-    return left, right, cores
+    q = call(last_kernel, side, 6, 1 << 28, 2 << 20)(*pieces, linv, scale)
+    return beside[0], basis_of(rows, linv), cores_of(pos, p_rows, gather_all(q))
 
 
 def solution(mesh):

time: 416 us -> 408 us (0.981)
  waiting for transfers between devices: 160 us -> 179 us
  starting transfers between devices: 143 us -> 128 us
  local copies, waits for them, and re-layouts: 26.8 us -> 15.1 us
    all_to_all x1, waiting for transfers between devices: 0.01 us -> 14.8 us  [shards(): p_rows = lax.all_to_all(p.T.reshape(16, 16, 192), 'row', 0, 0)]
    ppermute x126, starting transfers between devices: 138 us -> 123 us  [send(): return lax.ppermute(value, ('adapter', 'row'), perm)]
    unnamed x122 -> x66, local copies, waits for them, and re-layouts: 22.5 us -> 10.8 us
    ppermute x126, waiting for transfers between devices: 160 us -> 165 us  [send(): return lax.ppermute(value, ('adapter', 'row'), perm)]
  transfers between devices with their start and end apart: 127 -> 127, of which waited for: 64 -> 67; matrix products, arithmetic and copies ran while one was open for 0% -> 0% of each run, Pallas kernels for 13% -> 13%
where the time goes in v6:
time: 408 us; the launch traced here: 400 us
  waiting for transfers between devices  179 us (44%)
  starting transfers between devices  128 us (31%)
  Pallas kernels  74.7 us (18%)
  local copies, waits for them, and re-layouts  15.1 us (4%)
    ppermute x126, waiting for transfers between devices, send(): return lax.ppermute(value, ('adapter', 'row'), perm)  165 us
    ppermute x126, starting transfers between devices, send(): return lax.ppermute(value, ('adapter', 'row'), perm)  123 us
    pallas_call x4, Pallas kernels, inverse_factor(): call(inverse_kernel, f32s(K, K), 3, 0, 1 << 10, [pltpu.VMEM((K, K), F32)]...  27.1 us
    all_to_all x1, waiting for transfers between devices, shards(): p_rows = lax.all_to_all(p.T.reshape(16, 16, 192), 'row', 0, 0)  14.8 us
    unnamed x66, local copies, waits for them, and re-layouts  10.8 us
  transfers between devices with their start and end apart: 127, of which 67 were waited for; matrix products, arithmetic and copies ran while one was open for 0% of the time, Pallas kernels for 13%

profile of v6, /device:TPU:0, one launch (start us, length us, event | category | flops | bytes accessed | tf_op | source)
XLA Modules:
  0.0 400.2 jit_solution(1793508028787105625)
XLA Ops:
  10.2 4.0 collective-permute-start.3
  17.3 15.8 %collective-permute-done.piece_ref = f32[1024,256]{1,0:T(8,128)S(1)} collective-permute-done((f32[1024,256]{1,0:T(8,128)S(1)}, f32[1024,256]{1,0:T(8,128)S(1)}, u32[]{:S(2)}, u32[]{:S(2)}) %collective-permute-start) | collective-permute-done | bytes 1048608 | tf_op jit(solution)/shard_map/ppermute | solution.py:56
  39.0 20.2 %collective-permute-done.4.piece_ref = f32[1024,256]{1,0:T(8,128)S(1)} collective-permute-done((f32[1024,256]{1,0:T(8,128)S(1)}, f32[1024,256]{1,0:T(8,128)S(1)}, u32[]{:S(2)}, u32[]{:S(2)}) %collective-permute-start.4) | collective-permute-done | bytes 1048608 | tf_op jit(solution)/shard_map/ppermute | solution.py:56
  78.7 5.1 %collective-permute-done.6.refs_1_ = f32[192,256]{1,0:T(8,128)} collective-permute-done((f32[192,256]{1,0:T(8,128)}, f32[192,256]{1,0:T(8,128)}, u32[]{:S(2)}, u32[]{:S(2)}) %collective-permute-start.6) | collective-permute-done | bytes 196640 | tf_op jit(solution)/shard_map/ppermute | solution.py:56
  83.9 3.4 collective-permute-done.7.refs_2_
  108.9 5.1 %collective-permute-done.19 = f32[128,256]{1,0:T(8,128)S(1)} collective-permute-done((f32[128,256]{1,0:T(8,128)S(1)}, f32[128,256]{1,0:T(8,128)S(1)}, u32[]{:S(2)}, u32[]{:S(2)}) %collective-permute-start.19) | collective-permute-done | bytes 131104 | tf_op jit(solution)/shard_map/ppermute | solution.py:56
  121.3 5.1 %collective-permute-done.22 = f32[128,256]{1,0:T(8,128)S(1)} collective-permute-done((f32[128,256]{1,0:T(8,128)S(1)}, f32[128,256]{1,0:T(8,128)S(1)}, u32[]{:S(2)}, u32[]{:S(2)}) %collective-permute-start.22) | collective-permute-done | bytes 131104 | tf_op jit(solution)/shard_map/ppermute | solution.py:56
  129.8 3.1 collective-permute-done.27.refs_3_
  149.6 6.8 %shard_map.100.refs_4_ = f32[256,256]{1,0:T(8,128)S(1)} custom-call(s32[4]{0:T(128)S(1)} %pad_add_fusion.pos_ref, f32[128,256]{1,0:T(8,128)S(1)} %add_add_fusion.9.mine_ref, f32[128,256]{1,0:T(8,128)S(1)} %collective-permute-done.38.mate_ref), custom_call_target="tpu_custom_call" | custom-call | bytes 1024 | tf_op jit(solution)/shard_map/pallas_call | solution.py:283
  163.2 5.2 %collective-permute-done.40.b3 = f32[192,256]{1,0:T(8,128)S(1)} collective-permute-done((f32[192,256]{1,0:T(8,128)S(1)}, f32[192,256]{1,0:T(8,128)S(1)}, u32[]{:S(2)}, u32[]{:S(2)}) %collective-permute-start.40) | collective-permute-done | bytes 196640 | tf_op jit(solution)/shard_map/ppermute | solution.py:56
  179.0 4.1 %collective-permute-done.46 = f32[128,256]{1,0:T(8,128)S(1)} collective-permute-done((f32[128,256]{1,0:T(8,128)S(1)}, f32[128,256]{1,0:T(8,128)S(1)}, u32[]{:S(2)}, u32[]{:S(2)}) %collective-permute-start.46) | collective-permute-done | bytes 131104 | tf_op jit(solution)/shard_map/ppermute | solution.py:56
  185.3 3.1 collective-permute-start.50
  191.0 5.1 %collective-permute-done.49 = f32[128,256]{1,0:T(8,128)S(1)} collective-permute-done((f32[128,256]{1,0:T(8,128)S(1)}, f32[128,256]{1,0:T(8,128)S(1)}, u32[]{:S(2)}, u32[]{:S(2)}) %collective-permute-start.49) | collective-permute-done | bytes 131104 | tf_op jit(solution)/shard_map/ppermute | solution.py:56
  199.6 3.4 collective-permute-done.54.refs_3_
  219.0 6.8 %shard_map.107.refs_4_ = f32[256,256]{1,0:T(8,128)S(1)} custom-call(s32[4]{0:T(128)S(1)} %pad_add_fusion.pos_ref, f32[128,256]{1,0:T(8,128)S(1)} %add_add_fusion.6.mine_ref, f32[128,256]{1,0:T(8,128)S(1)} %collective-permute-done.65.mate_ref), custom_call_target="tpu_custom_call" | custom-call | bytes 1024 | tf_op jit(solution)/shard_map/pallas_call | solution.py:283
  228.0 3.1 collective-permute-start.66
  231.1 5.8 %collective-permute-done.67.b3 = f32[192,256]{1,0:T(8,128)S(1)} collective-permute-done((f32[192,256]{1,0:T(8,128)S(1)}, f32[192,256]{1,0:T(8,128)S(1)}, u32[]{:S(2)}, u32[]{:S(2)}) %collective-permute-start.67) | collective-permute-done | bytes 196640 | tf_op jit(solution)/shard_map/ppermute | solution.py:56
  248.3 4.4 %collective-permute-done.73 = f32[128,256]{1,0:T(8,128)S(1)} collective-permute-done((f32[128,256]{1,0:T(8,128)S(1)}, f32[128,256]{1,0:T(8,128)S(1)}, u32[]{:S(2)}, u32[]{:S(2)}) %collective-permute-start.73) | collective-permute-done | bytes 131104 | tf_op jit(solution)/shard_map/ppermute | solution.py:56
  259.4 5.1 %collective-permute-done.76 = f32[128,256]{1,0:T(8,128)S(1)} collective-permute-done((f32[128,256]{1,0:T(8,128)S(1)}, f32[128,256]{1,0:T(8,128)S(1)}, u32[]{:S(2)}, u32[]{:S(2)}) %collective-permute-start.76) | collective-permute-done | bytes 131104 | tf_op jit(solution)/shard_map/ppermute | solution.py:56
  267.5 3.5 collective-permute-done.81.refs_3_
  287.3 6.8 %shard_map.114.refs_4_.linv_ref = f32[256,256]{1,0:T(8,128)S(1)} custom-call(s32[4]{0:T(128)S(1)} %pad_add_fusion.pos_ref, f32[128,256]{1,0:T(8,128)S(1)} %add_add_fusion.3.mine_ref, f32[128,256]{1,0:T(8,128)S(1)} %collective-permute-done.92.mate_ref), custom_call_target="tpu_custom_call" | custom-call | bytes 1024 | tf_op jit(solution)/shard_map/pallas_call | solution.py:283
  300.0 4.9 %collective-permute-done.93.b3 = f32[192,256]{1,0:T(8,128)S(1)} collective-permute-done((f32[192,256]{1,0:T(8,128)S(1)}, f32[192,256]{1,0:T(8,128)S(1)}, u32[]{:S(2)}, u32[]{:S(2)}) %collective-permute-start.93) | collective-permute-done | bytes 196640 | tf_op jit(solution)/shard_map/ppermute | solution.py:56
  304.8 3.2 collective-permute-done.95.b1
  316.6 4.4 %collective-permute-done.100 = f32[128,256]{1,0:T(8,128)S(1)} collective-permute-done((f32[128,256]{1,0:T(8,128)S(1)}, f32[128,256]{1,0:T(8,128)S(1)}, u32[]{:S(2)}, u32[]{:S(2)}) %collective-permute-start.100) | collective-permute-done | bytes 131104 | tf_op jit(solution)/shard_map/ppermute | solution.py:56
  324.5 3.1 collective-permute-done.105
  327.6 3.0 collective-permute-done.103
  331.6 3.1 collective-permute-start.107
  354.8 6.8 %shard_map.122.linv_ref.refs_4_ = f32[256,256]{1,0:T(8,128)S(1)} custom-call(s32[4]{0:T(128)S(1)} %pad_add_fusion.pos_ref, f32[128,256]{1,0:T(8,128)S(1)} %add_add_fusion.mine_ref, f32[128,256]{1,0:T(8,128)S(1)} %collective-permute-done.116.mate_ref), custom_call_target="tpu_custom_call" | custom-call | bytes 1024 | tf_op jit(solution)/shard_map/pallas_call | solution.py:283
  364.3 5.2 %collective-permute-done.122.b3 = f32[192,256]{1,0:T(8,128)S(1)} collective-permute-done((f32[192,256]{1,0:T(8,128)S(1)}, f32[192,256]{1,0:T(8,128)S(1)}, u32[]{:S(2)}, u32[]{:S(2)}) %collective-permute-start.122) | collective-permute-done | bytes 196640 | tf_op jit(solution)/shard_map/ppermute | solution.py:56
  375.8 4.6 %all-to-all-start = ((f32[16,16,192]{2,1,0:T(8,128)}), f32[16,16,192]{2,1,0:T(8,128)S(1)}, u32[]{:S(2)}, u32[]{:S(2)}) async-start(f32[16,16,192]{2,1,0:T(8,128)} %bitcast.15), calls=%async_computation | async-start | bytes 524288 | tf_op jit(solution)/shard_map/all_to_all | solution.py:467
  381.6 14.8 %all-to-all-done.p_ref = f32[16,16,192]{2,1,0:T(8,128)S(1)} async-done(((f32[16,16,192]{2,1,0:T(8,128)}), f32[16,16,192]{2,1,0:T(8,128)S(1)}, u32[]{:S(2)}, u32[]{:S(2)}) %all-to-all-start) | async-done | bytes 196640 | tf_op jit(solution)/shard_map/all_to_all | solution.py:467
  396.4 3.6 shard_map.126
  (370 shorter events, 216.7 us)
Async XLA Ops:
  6.9 26.3 %collective-permute-start = (f32[1024,256]{1,0:T(8,128)S(1)}, f32[1024,256]{1,0:T(8,128)S(1)}, u32[]{:S(2)}, u32[]{:S(2)}) collective-permute-start(f32[1024,256]{1,0:T(8,128)S(1)} %get-tuple-element.116), channel_id=1, source_target_pairs={{0,1},{1,2},{2,3},{3,0},{4,5},{5,6},{6,7},{7,4},{8,9},{9,10},{10,1... | collective-permute-start | bytes 3145736 | tf_op jit(solution)/shard_map/ppermute | solution.py:56
  8.6 29.2 %collective-permute-start.1 = (f32[1024,256]{1,0:T(8,128)S(1)}, f32[1024,256]{1,0:T(8,128)S(1)}, u32[]{:S(2)}, u32[]{:S(2)}) collective-permute-start(f32[1024,256]{1,0:T(8,128)S(1)} %get-tuple-element.120), channel_id=1, source_target_pairs={{0,3},{1,0},{2,1},{3,2},{4,7},{5,4},{6,5},{7,6},{8,11},{9,8},{10,9... | collective-permute-start | bytes 3145736 | tf_op jit(solution)/shard_map/ppermute | solution.py:56
  10.2 28.9 %collective-permute-start.3 = (f32[1024,256]{1,0:T(8,128)S(1)}, f32[1024,256]{1,0:T(8,128)S(1)}, u32[]{:S(2)}, u32[]{:S(2)}) collective-permute-start(f32[1024,256]{1,0:T(8,128)S(1)} %get-tuple-element.124), channel_id=1, source_target_pairs={{0,8},{1,9},{2,10},{3,11},{4,12},{5,13},{6,14},{7,15},{8,0},{9,1},... | collective-permute-start | bytes 3145736 | tf_op jit(solution)/shard_map/ppermute | solution.py:56
  14.1 45.1 %collective-permute-start.4 = (f32[1024,256]{1,0:T(8,128)S(1)}, f32[1024,256]{1,0:T(8,128)S(1)}, u32[]{:S(2)}, u32[]{:S(2)}) collective-permute-start(f32[1024,256]{1,0:T(8,128)S(1)} %get-tuple-element.130), channel_id=1, source_target_pairs={{0,4},{1,5},{2,6},{3,7},{4,8},{5,9},{6,10},{7,11},{8,12},{9,13},{1... | collective-permute-start | bytes 3145736 | tf_op jit(solution)/shard_map/ppermute | solution.py:56
  15.1 45.3 %collective-permute-start.5 = (f32[1024,256]{1,0:T(8,128)S(1)}, f32[1024,256]{1,0:T(8,128)S(1)}, u32[]{:S(2)}, u32[]{:S(2)}) collective-permute-start(f32[1024,256]{1,0:T(8,128)S(1)} %get-tuple-element.133), channel_id=1, source_target_pairs={{0,12},{1,13},{2,14},{3,15},{4,0},{5,1},{6,2},{7,3},{8,4},{9,5},{1... | collective-permute-start | bytes 3145736 | tf_op jit(solution)/shard_map/ppermute | solution.py:56
  33.2 35.5 %collective-permute-start.2 = (f32[1024,256]{1,0:T(8,128)}, f32[1024,256]{1,0:T(8,128)}, u32[]{:S(2)}, u32[]{:S(2)}) collective-permute-start(f32[1024,256]{1,0:T(8,128)} %get-tuple-element.123), channel_id=1, source_target_pairs={{0,2},{1,3},{2,0},{3,1},{4,6},{5,7},{6,4},{7,5},{8,10},{9,11},{10,... | collective-permute-start | bytes 3145736 | tf_op jit(solution)/shard_map/ppermute | solution.py:56
  64.6 11.2 %collective-permute-start.9 = (f32[192,256]{1,0:T(8,128)}, f32[192,256]{1,0:T(8,128)}, u32[]{:S(2)}, u32[]{:S(2)}) collective-permute-start(f32[192,256]{1,0:T(8,128)} %get-tuple-element.144), channel_id=1, source_target_pairs={{0,3},{1,0},{2,1},{3,2},{4,7},{5,4},{6,5},{7,6},{8,11},{9,8},{10,9... | collective-permute-start | bytes 589832 | tf_op jit(solution)/shard_map/ppermute | solution.py:56
  66.4 12.3 %collective-permute-start.10 = (f32[192,256]{1,0:T(8,128)}, f32[192,256]{1,0:T(8,128)}, u32[]{:S(2)}, u32[]{:S(2)}) collective-permute-start(f32[192,256]{1,0:T(8,128)} %copy-done.27), channel_id=1, source_target_pairs={{0,1},{1,2},{2,3},{3,0},{4,5},{5,6},{6,7},{7,4},{8,9},{9,10},{10,1... | collective-permute-start | bytes 589832 | tf_op jit(solution)/shard_map/ppermute | solution.py:56
  66.7 12.0 %collective-permute-start.11 = (f32[192,256]{1,0:T(8,128)}, f32[192,256]{1,0:T(8,128)}, u32[]{:S(2)}, u32[]{:S(2)}) collective-permute-start(f32[192,256]{1,0:T(8,128)} %copy-done.26), channel_id=1, source_target_pairs={{0,2},{1,3},{2,0},{3,1},{4,6},{5,7},{6,4},{7,5},{8,10},{9,11},{10,... | collective-permute-start | bytes 589832 | tf_op jit(solution)/shard_map/ppermute | solution.py:56
  75.8 11.4 %collective-permute-start.7 = (f32[192,256]{1,0:T(8,128)}, f32[192,256]{1,0:T(8,128)}, u32[]{:S(2)}, u32[]{:S(2)}) collective-permute-start(f32[192,256]{1,0:T(8,128)} %get-tuple-element.141), channel_id=1, source_target_pairs={{0,4},{1,5},{2,6},{3,7},{4,8},{5,9},{6,10},{7,11},{8,12},{9,13},{1... | collective-permute-start | bytes 589832 | tf_op jit(solution)/shard_map/ppermute | solution.py:56
  75.8 11.4 %collective-permute-start.8 = (f32[192,256]{1,0:T(8,128)}, f32[192,256]{1,0:T(8,128)}, u32[]{:S(2)}, u32[]{:S(2)}) collective-permute-start(f32[192,256]{1,0:T(8,128)} %get-tuple-element.142), channel_id=1, source_target_pairs={{0,8},{1,9},{2,10},{3,11},{4,12},{5,13},{6,14},{7,15},{8,0},{9,1},... | collective-permute-start | bytes 589832 | tf_op jit(solution)/shard_map/ppermute | solution.py:56
  143.6 12.8 %collective-permute-start.32 = (f32[192,256]{1,0:T(8,128)S(1)}, f32[192,256]{1,0:T(8,128)S(1)}, u32[]{:S(2)}, u32[]{:S(2)}) collective-permute-start(f32[192,256]{1,0:T(8,128)S(1)} %get-tuple-element.157), channel_id=1, source_target_pairs={{0,12},{1,13},{2,14},{3,15},{4,0},{5,1},{6,2},{7,3},{8,4},{9,5},{1... | collective-permute-start | bytes 589832 | tf_op jit(solution)/shard_map/ppermute | solution.py:56
  146.5 11.3 %collective-permute-start.33 = (f32[192,256]{1,0:T(8,128)S(1)}, f32[192,256]{1,0:T(8,128)S(1)}, u32[]{:S(2)}, u32[]{:S(2)}) collective-permute-start(f32[192,256]{1,0:T(8,128)S(1)} %get-tuple-element.158), channel_id=1, source_target_pairs={{0,4},{1,5},{2,6},{3,7},{4,8},{5,9},{6,10},{7,11},{8,12},{9,13},{1... | collective-permute-start | bytes 589832 | tf_op jit(solution)/shard_map/ppermute | solution.py:56
  146.5 11.3 %collective-permute-start.34 = (f32[192,256]{1,0:T(8,128)S(1)}, f32[192,256]{1,0:T(8,128)S(1)}, u32[]{:S(2)}, u32[]{:S(2)}) collective-permute-start(f32[192,256]{1,0:T(8,128)S(1)} %get-tuple-element.159), channel_id=1, source_target_pairs={{0,8},{1,9},{2,10},{3,11},{4,12},{5,13},{6,14},{7,15},{8,0},{9,1},... | collective-permute-start | bytes 589832 | tf_op jit(solution)/shard_map/ppermute | solution.py:56
  159.2 11.1 %collective-permute-start.41 = (f32[192,256]{1,0:T(8,128)S(1)}, f32[192,256]{1,0:T(8,128)S(1)}, u32[]{:S(2)}, u32[]{:S(2)}) collective-permute-start(f32[192,256]{1,0:T(8,128)S(1)} %get-tuple-element.161.b0), channel_id=1, source_target_pairs={{0,1},{1,2},{2,3},{3,0},{4,5},{5,6},{6,7},{7,4},{8,9},{9,10},{10,1... | collective-permute-start | bytes 589832 | tf_op jit(solution)/shard_map/ppermute | solution.py:56
  159.7 11.4 %collective-permute-start.39 = (f32[192,256]{1,0:T(8,128)S(1)}, f32[192,256]{1,0:T(8,128)S(1)}, u32[]{:S(2)}, u32[]{:S(2)}) collective-permute-start(f32[192,256]{1,0:T(8,128)S(1)} %get-tuple-element.161.b0), channel_id=1, source_target_pairs={{0,3},{1,0},{2,1},{3,2},{4,7},{5,4},{6,5},{7,6},{8,11},{9,8},{10,9... | collective-permute-start | bytes 589832 | tf_op jit(solution)/shard_map/ppermute | solution.py:56
  212.4 13.4 %collective-permute-start.59 = (f32[192,256]{1,0:T(8,128)S(1)}, f32[192,256]{1,0:T(8,128)S(1)}, u32[]{:S(2)}, u32[]{:S(2)}) collective-permute-start(f32[192,256]{1,0:T(8,128)S(1)} %get-tuple-element.171), channel_id=1, source_target_pairs={{0,3},{1,0},{2,1},{3,2},{4,7},{5,4},{6,5},{7,6},{8,11},{9,8},{10,9... | collective-permute-start | bytes 589832 | tf_op jit(solution)/shard_map/ppermute | solution.py:56
  214.8 11.4 %collective-permute-start.60 = (f32[192,256]{1,0:T(8,128)S(1)}, f32[192,256]{1,0:T(8,128)S(1)}, u32[]{:S(2)}, u32[]{:S(2)}) collective-permute-start(f32[192,256]{1,0:T(8,128)S(1)} %get-tuple-element.172), channel_id=1, source_target_pairs={{0,1},{1,2},{2,3},{3,0},{4,5},{5,6},{6,7},{7,4},{8,9},{9,10},{10,1... | collective-permute-start | bytes 589832 | tf_op jit(solution)/shard_map/ppermute | solution.py:56
  215.4 10.7 %collective-permute-start.61 = (f32[192,256]{1,0:T(8,128)S(1)}, f32[192,256]{1,0:T(8,128)S(1)}, u32[]{:S(2)}, u32[]{:S(2)}) collective-permute-start(f32[192,256]{1,0:T(8,128)S(1)} %get-tuple-element.173), channel_id=1, source_target_pairs={{0,2},{1,3},{2,0},{3,1},{4,6},{5,7},{6,4},{7,5},{8,10},{9,11},{10,... | collective-permute-start | bytes 589832 | tf_op jit(solution)/shard_map/ppermute | solution.py:56
  227.6 12.1 %collective-permute-start.68 = (f32[192,256]{1,0:T(8,128)S(1)}, f32[192,256]{1,0:T(8,128)S(1)}, u32[]{:S(2)}, u32[]{:S(2)}) collective-permute-start(f32[192,256]{1,0:T(8,128)S(1)} %get-tuple-element.175.b0), channel_id=1, source_target_pairs={{0,4},{1,5},{2,6},{3,7},{4,8},{5,9},{6,10},{7,11},{8,12},{9,13},{1... | collective-permute-start | bytes 589832 | tf_op jit(solution)/shard_map/ppermute | solution.py:56
  228.0 12.4 %collective-permute-start.66 = (f32[192,256]{1,0:T(8,128)S(1)}, f32[192,256]{1,0:T(8,128)S(1)}, u32[]{:S(2)}, u32[]{:S(2)}) collective-permute-start(f32[192,256]{1,0:T(8,128)S(1)} %get-tuple-element.175.b0), channel_id=1, source_target_pairs={{0,12},{1,13},{2,14},{3,15},{4,0},{5,1},{6,2},{7,3},{8,4},{9,5},{1... | collective-permute-start | bytes 589832 | tf_op jit(solution)/shard_map/ppermute | solution.py:56
  279.6 14.5 %collective-permute-start.86 = (f32[192,256]{1,0:T(8,128)S(1)}, f32[192,256]{1,0:T(8,128)S(1)}, u32[]{:S(2)}, u32[]{:S(2)}) collective-permute-start(f32[192,256]{1,0:T(8,128)S(1)} %get-tuple-element.185), channel_id=1, source_target_pairs={{0,12},{1,13},{2,14},{3,15},{4,0},{5,1},{6,2},{7,3},{8,4},{9,5},{1... | collective-permute-start | bytes 589832 | tf_op jit(solution)/shard_map/ppermute | solution.py:56
  282.1 12.1 %collective-permute-start.87 = (f32[192,256]{1,0:T(8,128)S(1)}, f32[192,256]{1,0:T(8,128)S(1)}, u32[]{:S(2)}, u32[]{:S(2)}) collective-permute-start(f32[192,256]{1,0:T(8,128)S(1)} %get-tuple-element.186), channel_id=1, source_target_pairs={{0,4},{1,5},{2,6},{3,7},{4,8},{5,9},{6,10},{7,11},{8,12},{9,13},{1... | collective-permute-start | bytes 589832 | tf_op jit(solution)/shard_map/ppermute | solution.py:56
  283.2 10.9 %collective-permute-start.88 = (f32[192,256]{1,0:T(8,128)S(1)}, f32[192,256]{1,0:T(8,128)S(1)}, u32[]{:S(2)}, u32[]{:S(2)}) collective-permute-start(f32[192,256]{1,0:T(8,128)S(1)} %get-tuple-element.187), channel_id=1, source_target_pairs={{0,8},{1,9},{2,10},{3,11},{4,12},{5,13},{6,14},{7,15},{8,0},{9,1},... | collective-permute-start | bytes 589832 | tf_op jit(solution)/shard_map/ppermute | solution.py:56
  295.5 12.4 %collective-permute-start.95 = (f32[192,256]{1,0:T(8,128)S(1)}, f32[192,256]{1,0:T(8,128)S(1)}, u32[]{:S(2)}, u32[]{:S(2)}) collective-permute-start(f32[192,256]{1,0:T(8,128)S(1)} %get-tuple-element.189.b0), channel_id=1, source_target_pairs={{0,1},{1,2},{2,3},{3,0},{4,5},{5,6},{6,7},{7,4},{8,9},{9,10},{10,1... | collective-permute-start | bytes 589832 | tf_op jit(solution)/shard_map/ppermute | solution.py:56
  296.0 12.7 %collective-permute-start.94 = (f32[192,256]{1,0:T(8,128)S(1)}, f32[192,256]{1,0:T(8,128)S(1)}, u32[]{:S(2)}, u32[]{:S(2)}) collective-permute-start(f32[192,256]{1,0:T(8,128)S(1)} %get-tuple-element.189.b0), channel_id=1, source_target_pairs={{0,3},{1,0},{2,1},{3,2},{4,7},{5,4},{6,5},{7,6},{8,11},{9,8},{10,9... | collective-permute-start | bytes 589832 | tf_op jit(solution)/shard_map/ppermute | solution.py:56
  347.5 14.1 %collective-permute-start.117 = (f32[192,256]{1,0:T(8,128)S(1)}, f32[192,256]{1,0:T(8,128)S(1)}, u32[]{:S(2)}, u32[]{:S(2)}) collective-permute-start(f32[192,256]{1,0:T(8,128)S(1)} %get-tuple-element.204), channel_id=1, source_target_pairs={{0,3},{1,0},{2,1},{3,2},{4,7},{5,4},{6,5},{7,6},{8,11},{9,8},{10,9... | collective-permute-start | bytes 589832 | tf_op jit(solution)/shard_map/ppermute | solution.py:56
  350.0 11.6 %collective-permute-start.118 = (f32[192,256]{1,0:T(8,128)S(1)}, f32[192,256]{1,0:T(8,128)S(1)}, u32[]{:S(2)}, u32[]{:S(2)}) collective-permute-start(f32[192,256]{1,0:T(8,128)S(1)} %get-tuple-element.205), channel_id=1, source_target_pairs={{0,1},{1,2},{2,3},{3,0},{4,5},{5,6},{6,7},{7,4},{8,9},{9,10},{10,1... | collective-permute-start | bytes 589832 | tf_op jit(solution)/shard_map/ppermute | solution.py:56
  371.6 24.9 %collective-permute-start.125 = (f32[768,256]{1,0:T(8,128)S(1)}, f32[768,256]{1,0:T(8,128)S(1)}, u32[]{:S(2)}, u32[]{:S(2)}) collective-permute-start(f32[768,256]{1,0:T(8,128)S(1)} %shard_map.125.refs_0_), channel_id=1, source_target_pairs={{0,2},{1,3},{2,0},{3,1},{4,6},{5,7},{6,4},{7,5},{8,10},{9,11},{10,... | collective-permute-start | bytes 2359304 | tf_op jit(solution)/shard_map/ppermute | solution.py:56
  372.9 23.5 %collective-permute-start.124 = (f32[768,256]{1,0:T(8,128)S(1)}, f32[768,256]{1,0:T(8,128)S(1)}, u32[]{:S(2)}, u32[]{:S(2)}) collective-permute-start(f32[768,256]{1,0:T(8,128)S(1)} %shard_map.125.refs_0_), channel_id=1, source_target_pairs={{0,3},{1,0},{2,1},{3,2},{4,7},{5,4},{6,5},{7,6},{8,11},{9,8},{10,9... | collective-permute-start | bytes 2359304 | tf_op jit(solution)/shard_map/ppermute | solution.py:56
  375.0 21.4 %collective-permute-start.123 = (f32[768,256]{1,0:T(8,128)S(1)}, f32[768,256]{1,0:T(8,128)}, u32[]{:S(2)}, u32[]{:S(2)}) collective-permute-start(f32[768,256]{1,0:T(8,128)S(1)} %shard_map.125.refs_0_), channel_id=1, source_target_pairs={{0,1},{1,2},{2,3},{3,0},{4,5},{5,6},{6,7},{7,4},{8,9},{9,10},{10,1... | collective-permute-start | bytes 2359304 | tf_op jit(solution)/shard_map/ppermute | solution.py:56
  375.8 20.6 %all-to-all-start = ((f32[16,16,192]{2,1,0:T(8,128)}), f32[16,16,192]{2,1,0:T(8,128)S(1)}, u32[]{:S(2)}, u32[]{:S(2)}) async-start(f32[16,16,192]{2,1,0:T(8,128)} %bitcast.15), calls=%async_computation | async-start | bytes 524288 | tf_op jit(solution)/shard_map/all_to_all | solution.py:467
  (128 other events, 1010.6 us)
